TPU v7x, 512 devices: a whole 4x8x8 slice. The times are simulated.
512 devices in a mesh: row: 16 (over y, core), col: 32 (over z, x).
Axes of the slice: x: 4, y: 8, z: 8, core: 2. Of those that a mesh axis runs over, the one named last changes fastest.
Arguments:
- inputs: bfloat16 [768, 8192], P('col', 'row'), may hold values from -6 to 6
- w_gate: bfloat16 [8192, 14336], P('row', 'col'), may hold values from -0.0625 to 0.0625
- w_up: bfloat16 [8192, 14336], P('row', 'col'), may hold values from -0.0625 to 0.0625
- w_down: bfloat16 [14336, 8192], P('col', 'row'), may hold values from -0.046875 to 0.046875
- cotangent: bfloat16 [768, 8192], P('col', 'row'), may hold values from -6 to 6
Outputs:
- grad_inputs: bfloat16 [768, 8192], P('col', 'row')
- grad_gate: bfloat16 [8192, 14336], P('row', 'col')
- grad_up: bfloat16 [8192, 14336], P('row', 'col')
- grad_down: bfloat16 [14336, 8192], P('col', 'row')
All inputs are finite; a program needn't handle non-finite values.
Results may differ from a plain program's by a relative error of at most 0.0049.
Values may be sent and summed in bfloat16 or wider, within the bound.
No kernel may reach another device: no remote copies, remote signals or barrier semaphores. Data moves between devices by JAX's collectives and lax.ppermute only.
A program may use at most 64 MiB of HBM per device.

v0:
```python
import jax
import jax.numpy as jnp
from jax import lax
from jax.sharding import PartitionSpec as P


def contract_rows(left, right):
    return lax.dot_general(
        left, right, (((0,), (0,)), ((), ())), preferred_element_type=jnp.float32
    )


def contract_cols(left, right):
    return lax.dot_general(
        left, right, (((1,), (1,)), ((), ())), preferred_element_type=jnp.float32
    )


def on_device(inputs, w_gate, w_up, w_down, cotangent):
    all_inputs, all_cotangent = (
        lax.all_gather(inputs, "col", axis=0, tiled=True),
        lax.all_gather(cotangent, "col", axis=0, tiled=True),
    )
    columns = w_gate.shape[1]
    rows_in = all_inputs
    rows_co = all_cotangent
    gate_part = jnp.dot(rows_in, w_gate, preferred_element_type=jnp.float32)
    up_part = jnp.dot(rows_in, w_up, preferred_element_type=jnp.float32)
    back_part = contract_cols(rows_co, w_down)
    summed = lax.psum_scatter(
        jnp.concatenate([gate_part, up_part, back_part], axis=1),
        "row",
        scatter_dimension=0,
        tiled=True,
    )
    gate_sum = summed[:, :columns]
    up_sum = summed[:, columns : 2 * columns]
    grad_hidden = summed[:, 2 * columns :]
    sigmoid_gate = jax.nn.sigmoid(gate_sum)
    activated = gate_sum * sigmoid_gate
    hidden = (activated * up_sum).astype(jnp.bfloat16)
    grad_gate_act = (
        grad_hidden * up_sum * sigmoid_gate * (1.0 + gate_sum * (1.0 - sigmoid_gate))
    ).astype(jnp.bfloat16)
    grad_up_act = (grad_hidden * activated).astype(jnp.bfloat16)
    piece_gate = lax.all_gather(grad_gate_act, "row", axis=0, tiled=True)
    piece_up = lax.all_gather(grad_up_act, "row", axis=0, tiled=True)
    piece_hidden = lax.all_gather(hidden, "row", axis=0, tiled=True)
    rows_in = all_inputs
    rows_co = all_cotangent
    acc_gate = contract_rows(rows_in, piece_gate)
    acc_up = contract_rows(rows_in, piece_up)
    acc_down = contract_rows(piece_hidden, rows_co)
    input_rows = contract_cols(piece_gate, w_gate) + contract_cols(piece_up, w_up)
    acc_inputs = input_rows
    results = (acc_gate, acc_up, acc_down, acc_inputs)
    acc_gate, acc_up, acc_down, acc_inputs = results
    grad_inputs = lax.psum_scatter(acc_inputs, "col", scatter_dimension=0, tiled=True).astype(
        jnp.bfloat16
    )
    return (
        grad_inputs,
        acc_gate.astype(jnp.bfloat16),
        acc_up.astype(jnp.bfloat16),
        acc_down.astype(jnp.bfloat16),
    )


def solution(mesh):
    placed = (P("col", "row"), P("row", "col"), P("row", "col"), P("col", "row"), P("col", "row"))
    return jax.shard_map(
        on_device,
        mesh=mesh,
        in_specs=placed,
        out_specs=(P("col", "row"), P("row", "col"), P("row", "col"), P("col", "row")),
        check_vma=False,
    )
```

profile of v0, /device:TPU:1, one launch (start us, length us, event | category | flops | bytes accessed | tf_op | source)
XLA Modules:
  0.0 447.8 jit_solution(6258600876670552219)
XLA Ops:
  7.2 0.0 reduce-scatter.7.cloned.1.call-start
  7.2 44.7 %all_gather.15 = bf16[768,512]{1,0:T(8,128)(2,1)S(1)} all-gather(bf16[24,512]{1,0:T(8,128)(2,1)} %param.5), channel_id=1, replica_groups=mesh['row'=16,'col'=32] {'col'}, dimensions={0}, use_global_device_ids=true | all-gather | bytes 811008 | tf_op jit(solution)/shard_map/all_gather | solution.py:21
  51.9 37.2 %all_gather.16 = bf16[768,512]{1,0:T(8,128)(2,1)S(1)} all-gather(bf16[24,512]{1,0:T(8,128)(2,1)} %param.9), channel_id=1, replica_groups=mesh['row'=16,'col'=32] {'col'}, dimensions={0}, use_global_device_ids=true | all-gather | bytes 811008 | tf_op jit(solution)/shard_map/all_gather | solution.py:22
  89.1 0.5 fusion.4
  89.7 0.5 fusion.3
  90.2 0.5 copy-done.3
  90.7 0.5 fusion.5
  91.2 2.2 pad_maximum_fusion
  93.4 5.7 %copy.15 = f32[768,1344]{1,0:T(8,128)} copy(f32[768,1344]{0,1:T(8,128)} %pad_maximum_fusion) | data formatting | bytes 8257536
  99.2 0.0 reduce-scatter.7.cloned.1.call-update
  99.2 0.0 reduce-scatter.5.cloned.1.call-start
  99.2 83.6 %reduce-scatter.7.cloned.1.call-done = f32[48,1344]{1,0:T(8,128)} async-done(((f32[768,1344]{1,0:T(8,128)}), f32[48,1344]{1,0:T(8,128)}) %reduce-scatter.7.cloned.1.call-update) | async-done | bytes 258064 | tf_op jit(solution)/shard_map/reduce_scatter | solution.py:30
  182.9 1.1 multiply_convert_fusion
  184.0 19.1 %all_gather.18 = bf16[768,448]{1,0:T(8,128)(2,1)S(1)} all-gather(bf16[48,448]{1,0:T(8,128)(2,1)S(1)} %get-tuple-element.5), channel_id=1, replica_groups=mesh['row'=16,'col'=32] {'row'}, dimensions={0}, use_global_device_ids=true | all-gather | bytes 731136 | tf_op jit(solution)/shard_map/all_gather | solution.py:47
  203.1 17.9 %all_gather.17 = bf16[768,448]{1,0:T(8,128)(2,1)S(1)} all-gather(bf16[48,448]{1,0:T(8,128)(2,1)S(1)} %get-tuple-element.6), channel_id=1, replica_groups=mesh['row'=16,'col'=32] {'row'}, dimensions={0}, use_global_device_ids=true | all-gather | bytes 731136 | tf_op jit(solution)/shard_map/all_gather | solution.py:46
  221.0 0.6 fusion.6
  221.6 1.7 convolution_add_fusion
  223.3 0.0 reduce-scatter.5.cloned.1.call-update
  223.3 2.5 fusion.1
  225.8 1.3 fusion
  227.1 16.6 %all_gather.19 = bf16[768,448]{1,0:T(8,128)(2,1)S(1)} all-gather(bf16[48,448]{1,0:T(8,128)(2,1)S(1)} %get-tuple-element.4), channel_id=1, replica_groups=mesh['row'=16,'col'=32] {'row'}, dimensions={0}, use_global_device_ids=true | all-gather | bytes 731136 | tf_op jit(solution)/shard_map/all_gather | solution.py:48
  243.7 1.3 convolution_convert_fusion
  245.1 194.5 %reduce-scatter.5.cloned.1.call-done = f32[24,512]{1,0:T(8,128)} async-done(((f32[768,512]{1,0:T(8,128)}), f32[24,512]{1,0:T(8,128)}) %reduce-scatter.5.cloned.1.call-update) | async-done | bytes 49168 | tf_op jit(solution)/shard_map/reduce_scatter | solution.py:58
  439.5 1.4 convert_element_type.29
  (7 shorter events, 0.0 us)
Async XLA Ops:
  7.2 82.5 %copy-start = (bf16[512,448]{0,1:T(8,128)(2,1)S(1)}, bf16[512,448]{0,1:T(8,128)(2,1)}, u32[]{:S(2)}) copy-start(bf16[512,448]{0,1:T(8,128)(2,1)} %param.6) | copy-start | bytes 1376260
  7.2 81.9 %copy-start.2 = (bf16[512,448]{0,1:T(8,128)(2,1)S(1)}, bf16[512,448]{0,1:T(8,128)(2,1)}, u32[]{:S(2)}) copy-start(bf16[512,448]{0,1:T(8,128)(2,1)} %param.7) | copy-start | bytes 1376260
  7.2 175.7 %reduce-scatter.7.cloned.1.call-start = ((), (), s32[]{:S(2)}) async-start(), calls=%async_computation.3 | async-start | bytes 4595712 | tf_op jit(solution)/shard_map/reduce_scatter | solution.py:30
  89.6 1.0 copy-start.3
  99.2 340.4 %reduce-scatter.5.cloned.1.call-start = ((), (), s32[]{:S(2)}) async-start(), calls=%async_computation.2 | async-start | bytes 1622016 | tf_op jit(solution)/shard_map/reduce_scatter | solution.py:58
  203.1 18.5 %copy-start.1 = (bf16[768,448]{1,0:T(8,128)(2,1)}, bf16[768,448]{1,0:T(8,128)(2,1)S(1)}, u32[]{:S(2)}) copy-start(bf16[768,448]{1,0:T(8,128)(2,1)S(1)} %all_gather.18) | copy-start | bytes 2064388
Sparse Core Ops, SparseCore 0:
  99.3 83.5 reduce-scatter.6
  223.4 216.0 reduce-scatter.4
where the time goes:
time: 453 us; the launch traced here: 448 us
  waiting for transfers between devices  278 us (61%)
  blocking collectives  135 us (30%)
  between operations  14.1 us (3%)
  matrix products  9.03 us (2%)
  local copies, waits for them, and re-layouts  6.19 us (1%)
  other arithmetic  4.73 us (1%)
    reduce_scatter x1, waiting for transfers between devices, on_device(): lax.psum_scatter(acc_inputs, 'col', scatter_dimension=0, tiled=True)  194 us
    reduce_scatter x1, waiting for transfers between devices, on_device(): lax.psum_scatter(jnp.concatenate([gate_part, up_part, back_part], axis=1)...  83.6 us
    all_gather x1, blocking collectives, on_device(): lax.all_gather(inputs, 'col', axis=0, tiled=True)  44.7 us
    all_gather x1, blocking collectives, on_device(): lax.all_gather(cotangent, 'col', axis=0, tiled=True)  37.2 us
    all_gather x1, blocking collectives, on_device(): piece_up = lax.all_gather(grad_up_act, 'row', axis=0, tiled=True)  19.1 us
    all_gather x1, blocking collectives, on_device(): piece_gate = lax.all_gather(grad_gate_act, 'row', axis=0, tiled=True)  17.9 us
    all_gather x1, blocking collectives, on_device(): piece_hidden = lax.all_gather(hidden, 'row', axis=0, tiled=True)  16.6 us
  transfers between devices with their start and end apart: 2, of which 2 were waited for; matrix products, arithmetic and copies ran while one was open for 1% of the time, Pallas kernels for 0%

commit v1 on v0

v1 whole, which is shorter than its diff:
```python
import jax
import jax.numpy as jnp
from jax import lax
from jax.sharding import Mesh, PartitionSpec as P

F32 = jnp.float32
BF16 = jnp.bfloat16


def dot(left, right, left_dim, right_dim):
    return lax.dot_general(
        left, right, (((left_dim,), (right_dim,)), ((), ())), preferred_element_type=F32
    )


def spread(block, axis, size):
    copies = jnp.broadcast_to(block[None], (size, *block.shape))
    return lax.all_to_all(copies, axis, 0, 0)


def build(sizes):
    ny, nc, nz, nx = sizes

    def on_device(inputs, w_gate, w_up, w_down, cotangent):
        width, columns = w_gate.shape
        rows = inputs.shape[0]
        tokens = rows * nz * nx
        half = tokens // nc
        both = jnp.concatenate([inputs, cotangent], axis=1)
        along_z = spread(both, "z", nz).reshape(nz * rows, 2 * width)
        held = spread(along_z, "x", nx).reshape(tokens, 2 * width)

        core = lax.axis_index("c")

        def partial_sums(block):
            return jnp.concatenate(
                [
                    dot(block[:, :width], w_gate, 1, 0),
                    dot(block[:, :width], w_up, 1, 0),
                    dot(block[:, width:], w_down, 1, 1),
                ],
                axis=1,
            )

        other = lax.dynamic_slice_in_dim(held, (1 - core) * half, half, 0)
        mine = lax.dynamic_slice_in_dim(held, core * half, half, 0)
        received = lax.ppermute(partial_sums(other), "c", [(0, 1), (1, 0)])
        chip_sums = (partial_sums(mine) + received).astype(BF16)
        parts = lax.all_to_all(
            chip_sums.reshape(ny, half // ny, 3 * columns), "y", 0, 0
        )
        summed = jnp.sum(parts.astype(F32), axis=0)
        gate_sum = summed[:, :columns]
        up_sum = summed[:, columns : 2 * columns]
        grad_hidden = summed[:, 2 * columns :]
        sigmoid_gate = jax.nn.sigmoid(gate_sum)
        activated = gate_sum * sigmoid_gate
        pieces = jnp.concatenate(
            [
                grad_hidden * up_sum * sigmoid_gate * (1.0 + gate_sum * (1.0 - sigmoid_gate)),
                grad_hidden * activated,
                activated * up_sum,
            ],
            axis=1,
        ).astype(BF16)
        pieces = lax.all_gather(pieces, "y", axis=0, tiled=True)
        pieces = lax.all_gather(pieces, "c", axis=0, tiled=True)
        grad_gate_act = pieces[:, :columns]
        grad_up_act = pieces[:, columns : 2 * columns]
        hidden = pieces[:, 2 * columns :]

        share = dot(grad_gate_act, w_gate, 1, 1) + dot(grad_up_act, w_up, 1, 1)
        shares = lax.all_to_all(
            share.astype(BF16).reshape(nx * nz, rows, width), ("x", "z"), 0, 0
        )
        grad_inputs = jnp.sum(shares.astype(F32), axis=0).astype(BF16)
        all_inputs, all_cotangent = held[:, :width], held[:, width:]
        return (
            grad_inputs,
            dot(all_inputs, grad_gate_act, 0, 0).astype(BF16),
            dot(all_inputs, grad_up_act, 0, 0).astype(BF16),
            dot(hidden, all_cotangent, 0, 0).astype(BF16),
        )

    return on_device


def solution(mesh):
    row, col = mesh.devices.shape
    sizes = (row // 2, 2, col // 4, 4)
    fine = Mesh(mesh.devices.reshape(sizes), ("y", "c", "z", "x"))
    token_width, width_hidden, hidden_width = (
        P(("z", "x"), ("y", "c")),
        P(("y", "c"), ("z", "x")),
        P(("z", "x"), ("y", "c")),
    )
    return jax.shard_map(
        build(sizes),
        mesh=fine,
        in_specs=(token_width, width_hidden, width_hidden, hidden_width, token_width),
        out_specs=(token_width, width_hidden, width_hidden, hidden_width),
        check_vma=False,
    )
```

time: 453 us -> 193 us (0.43)
  waiting for transfers between devices: 278 us -> 52.2 us
  blocking collectives: 135 us -> 83.3 us
  starting transfers between devices: 0.08 us -> 18.3 us
    reduce_scatter x2 -> x0, waiting for transfers between devices: 278 us -> none  [the longest x1 194 us: on_device(): lax.psum_scatter(acc_inputs, 'col', scatter_dimension=0, tiled=True)]
    all_gather x5 -> x1, blocking collectives: 135 us -> 23.6 us  [on_device(): pieces = lax.all_gather(pieces, 'y', axis=0, tiled=True)]
    all_to_all x0 -> x2, blocking collectives: none -> 59.8 us  [the longest x1 35.6 us: on_device(): lax.all_to_all(chip_sums.reshape(ny, half // ny, 3 * columns), 'y', 0, 0)]
    all_to_all x0 -> x2, waiting for transfers between devices: none -> 31.8 us  [the longest x1 18.3 us: spread(): return lax.all_to_all(copies, axis, 0, 0)]
    all_gather x0 -> x1, waiting for transfers between devices: none -> 17.7 us  [on_device(): pieces = lax.all_gather(pieces, 'c', axis=0, tiled=True)]
    all_to_all x0 -> x2, starting transfers between devices: none -> 13 us  [the longest x1 8.9 us: on_device(): lax.all_to_all(share.astype(BF16).reshape(nx * nz, rows, width), ('x', 'z...]
    unnamed x9 -> x10, local copies, waits for them, and re-layouts: 6.19 us -> 0.03 us
    ppermute x0 -> x1, starting transfers between devices: none -> 5.22 us  [on_device(): received = lax.ppermute(partial_sums(other), 'c', [(0, 1), (1, 0)])]
  transfers between devices with their start and end apart: 2 -> 4, of which waited for: 2 -> 4; matrix products, arithmetic and copies ran while one was open for 1% -> 4% of each run, Pallas kernels for 0% -> 0%
where the time goes in v1:
time: 193 us; the launch traced here: 190 us
  blocking collectives  83.3 us (43%)
  waiting for transfers between devices  52.2 us (27%)
  starting transfers between devices  18.3 us (9%)
  between operations  14.2 us (7%)
  matrix products  12.7 us (7%)
  other arithmetic  5.97 us (3%)
  local copies, waits for them, and re-layouts  3.21 us (2%)
    all_to_all x1, blocking collectives, on_device(): lax.all_to_all(chip_sums.reshape(ny, half // ny, 3 * columns), 'y', 0, 0)  35.6 us
    all_to_all x1, blocking collectives, spread(): return lax.all_to_all(copies, axis, 0, 0)  24.2 us
    all_gather x1, blocking collectives, on_device(): pieces = lax.all_gather(pieces, 'y', axis=0, tiled=True)  23.6 us
    all_to_all x1, waiting for transfers between devices, spread(): return lax.all_to_all(copies, axis, 0, 0)  18.3 us
    all_gather x1, waiting for transfers between devices, on_device(): pieces = lax.all_gather(pieces, 'c', axis=0, tiled=True)  17.7 us
    all_to_all x1, waiting for transfers between devices, on_device(): lax.all_to_all(share.astype(BF16).reshape(nx * nz, rows, width), ('x', 'z...  13.4 us
    dot_general x11, matrix products, dot(): lax.dot_general(left, right, (((left_dim,), (right_dim,)), ((), ())), pre...  12.7 us
    all_to_all x1, starting transfers between devices, on_device(): lax.all_to_all(share.astype(BF16).reshape(nx * nz, rows, width), ('x', 'z...  8.9 us
  transfers between devices with their start and end apart: 4, of which 4 were waited for; matrix products, arithmetic and copies ran while one was open for 4% of the time, Pallas kernels for 0%

profile of v1, /device:TPU:1, one launch (start us, length us, event | category | flops | bytes accessed | tf_op | source)
XLA Modules:
  0.0 189.8 jit_solution(6315377962750386318)
XLA Ops:
  7.2 0.8 pad_maximum_fusion.1
  8.0 24.2 %all_to_all.20 = bf16[8,24,1024]{2,1,0:T(8,128)(2,1)S(1)} all-to-all(bf16[8,24,1024]{2,1,0:T(8,128)(2,1)S(1)} %broadcast_in_dim.6), channel_id=1, replica_groups=mesh['y'=8,'c'=2,'z'=8,'x'=4] {'z'}, dimensions={0} | all-to-all | bytes 786432 | tf_op jit(solution)/shard_map/all_to_all | solution.py:18
  32.2 1.3 broadcast_in_dim.15
  33.6 4.1 %all-to-all-start.1 = ((bf16[4,192,1024]{2,1,0:T(8,128)(2,1)}), bf16[4,192,1024]{2,1,0:T(8,128)(2,1)S(1)}, u32[]{:S(2)}, u32[]{:S(2)}) async-start(bf16[4,192,1024]{2,1,0:T(8,128)(2,1)} %broadcast_in_dim.15), calls=%async_computation.1 | async-start | bytes 3145728 | tf_op jit(solution)/shard_map/all_to_all | solution.py:18
  37.7 18.3 %all-to-all-done.1 = bf16[4,192,1024]{2,1,0:T(8,128)(2,1)S(1)} async-done(((bf16[4,192,1024]{2,1,0:T(8,128)(2,1)}), bf16[4,192,1024]{2,1,0:T(8,128)(2,1)S(1)}, u32[]{:S(2)}, u32[]{:S(2)}) %all-to-all-start.1) | async-done | bytes 1572896 | tf_op jit(solution)/shard_map/all_to_all | solution.py:18
  56.5 0.4 fusion.16
  56.9 0.4 fusion.10
  57.4 1.4 pad_maximum_fusion
  58.8 5.2 %collective-permute-start = (f32[384,1344]{0,1:T(8,128)}, f32[384,1344]{0,1:T(8,128)}, u32[]{:S(2)}, u32[]{:S(2)}) collective-permute-start(f32[384,1344]{0,1:T(8,128)} %pad_maximum_fusion), channel_id=1, source_target_pairs={{0,32},{32,0},{1,33},{33,1},{2,34},{34,2},{3,35},{35,3},{4,36},{36... | collective-permute-start | bytes 6193160 | tf_op jit(solution)/shard_map/ppermute | solution.py:47
  64.9 0.4 fusion.20
  65.3 2.8 %collective-permute-done = f32[384,1344]{0,1:T(8,128)} collective-permute-done((f32[384,1344]{0,1:T(8,128)}, f32[384,1344]{0,1:T(8,128)}, u32[]{:S(2)}, u32[]{:S(2)}) %collective-permute-start) | collective-permute-done | bytes 2064416 | tf_op jit(solution)/shard_map/ppermute | solution.py:47
  68.1 2.8 %fusion = bf16[384,1344]{0,1:T(8,128)(2,1)} fusion(f32[384,1344]{0,1:T(8,128)} %collective-permute-done, f32[384,448]{0,1:T(8,128)S(1)} %fusion.12, f32[384,448]{0,1:T(8,128)S(1)} %fusion.18, f32[384,448]{0,1:T(8,128)S(1)} %fusion.20), kind=kLoop, calls=%fused_computation.2 | loop fusion | flops 2064384 | bytes 5160960 | tf_op jit(solution)/shard_map/convert_element_type | solution.py:48
  70.8 1.7 copy.9
  72.6 35.6 %all_to_all.21 = bf16[8,48,1344]{2,1,0:T(8,128)(2,1)S(1)} all-to-all(bf16[8,48,1344]{2,1,0:T(8,128)(2,1)S(1)} %bitcast.21), channel_id=1, replica_groups=mesh['y'=8,'c'=2,'z'=8,'x'=4] {'y'}, dimensions={0} | all-to-all | bytes 2064384 | tf_op jit(solution)/shard_map/all_to_all | solution.py:49
  108.5 23.6 %all_gather.6 = bf16[384,1344]{1,0:T(8,128)(2,1)} all-gather(bf16[48,1344]{1,0:T(8,128)(2,1)S(1)} %concatenate.16), channel_id=1, replica_groups=mesh['y'=8,'c'=2,'z'=8,'x'=4] {'y'}, dimensions={0}, use_global_device_ids=true | all-gather | bytes 1161216 | tf_op jit(solution)/shard_map/all_gather | solution.py:66
  132.1 17.7 %all-gather.2.cloned.1.call-done = bf16[768,1344]{1,0:T(8,128)(2,1)} async-done(((bf16[384,1344]{1,0:T(8,128)(2,1)}), bf16[768,1344]{1,0:T(8,128)(2,1)}) %all-gather.2.cloned.1.call-update) | async-done | bytes 2064400 | tf_op jit(solution)/shard_map/all_gather | solution.py:67
  149.8 1.7 fusion.8
  151.5 2.7 %add_convert_fusion = bf16[768,512]{1,0:T(8,128)(2,1)} fusion(f32[768,512]{1,0:T(8,128)S(1)} %fusion.8, bf16[512,448]{0,1:T(8,128)(2,1)S(1)} %copy-done.2, bf16[768,1344]{1,0:T(8,128)(2,1)} %all-gather.2.cloned.1.call-done), kind=kOutput, calls=%fused_computation.4 | convolution fusion | flops 353107968 | bytes 3604480 | tf_op jit(solution)/shard_map/dot_general | solution.py:11
  154.2 8.9 %all-to-all-start.3 = ((bf16[32,24,512]{2,1,0:T(8,128)(2,1)}), bf16[32,24,512]{2,1,0:T(8,128)(2,1)S(1)}, u32[]{:S(2)}, u32[]{:S(2)}) async-start(bf16[32,24,512]{2,1,0:T(8,128)(2,1)} %bitcast.3), calls=%async_computation.3 | async-start | bytes 1572864 | tf_op jit(solution)/shard_map/all_to_all | solution.py:73
  163.1 2.6 %convolution_convert_fusion = bf16[448,512]{1,0:T(8,128)(2,1)} fusion(bf16[768,1024]{1,0:T(8,128)(2,1)S(1)} %bitcast.18, bf16[768,1344]{1,0:T(8,128)(2,1)} %all-gather.2.cloned.1.call-done), kind=kOutput, calls=%fused_computation.5 | convolution fusion | flops 352550912 | bytes 2031616 | tf_op jit(solution)/shard_map/dot_general | solution.py:11
  165.7 1.7 convolution_convert_fusion.1
  167.5 1.3 convolution_convert_fusion.2
  168.8 13.4 %all-to-all-done.3 = bf16[32,24,512]{2,1,0:T(8,128)(2,1)S(1)} async-done(((bf16[32,24,512]{2,1,0:T(8,128)(2,1)}), bf16[32,24,512]{2,1,0:T(8,128)(2,1)S(1)}, u32[]{:S(2)}, u32[]{:S(2)}) %all-to-all-start.3) | async-done | bytes 786464 | tf_op jit(solution)/shard_map/all_to_all | solution.py:73
  182.2 0.7 reduce_sum.22
  (19 shorter events, 1.7 us)
Async XLA Ops:
  7.2 49.3 %copy-start = (bf16[512,448]{0,1:T(8,128)(2,1)S(1)}, bf16[512,448]{0,1:T(8,128)(2,1)}, u32[]{:S(2)}) copy-start(bf16[512,448]{0,1:T(8,128)(2,1)} %param.6) | copy-start | bytes 1376260
  33.6 22.5 %copy-start.1 = (bf16[512,448]{0,1:T(8,128)(2,1)S(1)}, bf16[512,448]{0,1:T(8,128)(2,1)}, u32[]{:S(2)}) copy-start(bf16[512,448]{0,1:T(8,128)(2,1)} %param.7) | copy-start | bytes 1376260
  33.6 22.5 %all-to-all-start.1 = ((bf16[4,192,1024]{2,1,0:T(8,128)(2,1)}), bf16[4,192,1024]{2,1,0:T(8,128)(2,1)S(1)}, u32[]{:S(2)}, u32[]{:S(2)}) async-start(bf16[4,192,1024]{2,1,0:T(8,128)(2,1)} %broadcast_in_dim.15), calls=%async_computation.1 | async-start | bytes 3145728 | tf_op jit(solution)/shard_map/all_to_all | solution.py:18
  37.7 19.2 %copy-start.3 = (bf16[448,512]{1,0:T(8,128)(2,1)S(1)}, bf16[448,512]{1,0:T(8,128)(2,1)}, u32[]{:S(2)}) copy-start(bf16[448,512]{1,0:T(8,128)(2,1)} %param.8) | copy-start | bytes 1376260
  37.7 112.1 %all-gather.2.cloned.1.call-start = ((), (), s32[]{:S(2)}) async-start(), calls=%async_computation.4 | async-start | bytes 3244032 | tf_op jit(solution)/shard_map/all_gather | solution.py:67
  58.8 9.3 %collective-permute-start = (f32[384,1344]{0,1:T(8,128)}, f32[384,1344]{0,1:T(8,128)}, u32[]{:S(2)}, u32[]{:S(2)}) collective-permute-start(f32[384,1344]{0,1:T(8,128)} %pad_maximum_fusion), channel_id=1, source_target_pairs={{0,32},{32,0},{1,33},{33,1},{2,34},{34,2},{3,35},{35,3},{4,36},{36... | collective-permute-start | bytes 6193160 | tf_op jit(solution)/shard_map/ppermute | solution.py:47
  132.1 19.4 %copy-start.2 = (bf16[512,448]{0,1:T(8,128)(2,1)S(1)}, bf16[512,448]{0,1:T(8,128)(2,1)}, u32[]{:S(2)}) copy-start(bf16[512,448]{0,1:T(8,128)(2,1)} %param.7) | copy-start | bytes 1376260
  154.2 28.0 %all-to-all-start.3 = ((bf16[32,24,512]{2,1,0:T(8,128)(2,1)}), bf16[32,24,512]{2,1,0:T(8,128)(2,1)S(1)}, u32[]{:S(2)}, u32[]{:S(2)}) async-start(bf16[32,24,512]{2,1,0:T(8,128)(2,1)} %bitcast.3), calls=%async_computation.3 | async-start | bytes 1572864 | tf_op jit(solution)/shard_map/all_to_all | solution.py:73
  163.1 2.6 %copy-start.4 = (bf16[768,1344]{1,0:T(8,128)(2,1)S(1)}, bf16[768,1344]{1,0:T(8,128)(2,1)}, u32[]{:S(2)}) copy-start(bf16[768,1344]{1,0:T(8,128)(2,1)} %all-gather.2.cloned.1.call-done) | copy-start | bytes 6193156
Sparse Core Ops, SparseCore 0:
  132.2 17.5 all-gather.1

commit v2 on v1

v2 whole, which is shorter than its diff:
```python
import functools

import jax
import jax.numpy as jnp
from jax import lax
from jax.experimental import pallas as pl
from jax.experimental.pallas import tpu as pltpu
from jax.sharding import Mesh, PartitionSpec as P

F32 = jnp.float32
BF16 = jnp.bfloat16
SWAP = [(0, 1), (1, 0)]


def dot(left, right, left_dim, right_dim):
    return lax.dot_general(
        left, right, (((left_dim,), (right_dim,)), ((), ())), preferred_element_type=F32
    )


def sibling(value):
    return lax.ppermute(value, "c", SWAP)


def spread(block, axis, size):
    copies = jnp.broadcast_to(block[None], (size, *block.shape))
    return lax.all_to_all(copies, axis, 0, 0)


def after(value, *earlier):
    return lax.optimization_barrier((value, *earlier))[0]


def local(kernel, out_shape, flops, moved, core, *operands):
    return pl.pallas_call(
        kernel,
        out_shape=out_shape,
        in_specs=[pl.BlockSpec(memory_space=pltpu.SMEM)]
        + [pl.BlockSpec(memory_space=pltpu.VMEM)] * len(operands),
        out_specs=jax.tree.map(lambda _: pl.BlockSpec(memory_space=pltpu.VMEM), out_shape),
        compiler_params=pltpu.CompilerParams(vmem_limit_bytes=24 * 1024 * 1024),
        cost_estimate=pl.CostEstimate(flops=flops, bytes_accessed=moved, transcendentals=0),
    )(core.reshape(1).astype(jnp.int32), *operands)


def sums_kernel(count, flip, core_ref, block_ref, *refs):
    weights, rest = refs[:count], refs[count:]
    out_ref = rest[-1]
    half = block_ref.shape[0] // 2
    side = 1 - core_ref[0] if flip else core_ref[0]
    block = block_ref[pl.ds(pl.multiple_of(side * half, half), half), :]
    ny, rows = out_ref.shape[0], out_ref.shape[1] // count
    for k in range(count):
        at = pl.ds(k * rows, rows)
        product = dot(block, weights[k][...], 1, 1).reshape(ny, rows, out_ref.shape[2])
        if not flip:
            product = product + rest[0][:, at, :]
        out_ref[:, at, :] = product.astype(out_ref.dtype)


def activations_kernel(core_ref, gate_up_ref, back_ref, out_ref):
    rows = out_ref.shape[1]
    gate_sum = gate_up_ref[:rows, :]
    up_sum = gate_up_ref[rows:, :]
    grad_hidden = jnp.sum(back_ref[...].astype(F32), axis=0)
    sigmoid_gate = jax.nn.sigmoid(gate_sum)
    activated = gate_sum * sigmoid_gate
    out_ref[0] = (
        grad_hidden * up_sum * sigmoid_gate * (1.0 + gate_sum * (1.0 - sigmoid_gate))
    ).astype(BF16)
    out_ref[1] = (grad_hidden * activated).astype(BF16)
    out_ref[2] = (activated * up_sum).astype(BF16)


def inputs_kernel(core_ref, own_ref, other_ref, gate_ref, up_ref, out_ref):
    half = out_ref.shape[0] // 2
    for pieces, side in ((own_ref, core_ref[0]), (other_ref, 1 - core_ref[0])):
        columns = pieces.shape[-1]
        grad_gate_act = pieces[:, 0].reshape(half, columns)
        grad_up_act = pieces[:, 1].reshape(half, columns)
        share = dot(grad_gate_act, gate_ref[...], 1, 0) + dot(grad_up_act, up_ref[...], 1, 0)
        at = pl.ds(pl.multiple_of(side * half, half), half)
        out_ref[at, :] = share.astype(BF16)


def build(sizes):
    ny, nc, nz, nx = sizes

    def on_device(inputs, w_gate, w_up, w_down, cotangent):
        width, columns = w_gate.shape
        rows = inputs.shape[0]
        tokens = rows * nz * nx
        half = tokens // nc
        share_rows = half // ny
        core = lax.axis_index("c")
        gate_t, up_t = w_gate.T, w_up.T

        both = jnp.concatenate([inputs, cotangent], axis=1)
        along_z = spread(both, "z", nz).reshape(nz * rows, 2 * width)

        def add_over_cores(block, weights, out_type):
            count = len(weights)
            shape = (ny, count * share_rows, columns)
            flops = 2 * half * width * columns * count
            moved = 2 * (half * width + count * width * columns) + 4 * count * half * columns
            received = sibling(
                local(
                    functools.partial(sums_kernel, count, True),
                    jax.ShapeDtypeStruct(shape, F32),
                    flops,
                    moved,
                    core,
                    block,
                    *weights,
                )
            )
            return local(
                functools.partial(sums_kernel, count, False),
                jax.ShapeDtypeStruct(shape, out_type),
                flops,
                moved + 4 * count * half * columns,
                core,
                block,
                *weights,
                received,
            )

        all_inputs = spread(along_z[:, :width], "x", nx).reshape(tokens, width)
        chip_gate_up = add_over_cores(all_inputs, (gate_t, up_t), F32)
        gate_up = lax.psum_scatter(
            chip_gate_up.reshape(2 * half, columns), "y", scatter_dimension=0, tiled=True
        )
        all_cotangent = spread(after(along_z[:, width:], chip_gate_up), "x", nx).reshape(
            tokens, width
        )
        back = lax.all_to_all(add_over_cores(all_cotangent, (w_down,), BF16), "y", 0, 0)

        pieces = local(
            activations_kernel,
            jax.ShapeDtypeStruct((3, share_rows, columns), BF16),
            20 * share_rows * columns,
            2 * half * columns,
            core,
            gate_up,
            back,
        )
        own = lax.all_gather(pieces, "y")
        other = sibling(own[:, :2])
        share = local(
            inputs_kernel,
            jax.ShapeDtypeStruct((tokens, width), BF16),
            4 * tokens * width * columns,
            4 * tokens * columns + 2 * tokens * width,
            core,
            own,
            other,
            gate_t,
            up_t,
        )
        shares = lax.all_to_all(share.reshape(nx * nz, rows, width), ("x", "z"), 0, 0)
        grad_inputs = jnp.sum(shares.astype(F32), axis=0).astype(BF16)

        other_hidden = sibling(after(own[:, 2], share))

        def whole(mine, theirs):
            mine, theirs = mine.reshape(half, columns), theirs.reshape(half, columns)
            first = jnp.where(core == 0, mine, theirs)
            second = jnp.where(core == 0, theirs, mine)
            return jnp.concatenate([first, second], axis=0)

        grad_gate_act = whole(own[:, 0], after(other[:, 0], share))
        grad_up_act = whole(own[:, 1], after(other[:, 1], share))
        hidden = whole(own[:, 2], other_hidden)
        return (
            grad_inputs,
            dot(all_inputs, grad_gate_act, 0, 0).astype(BF16),
            dot(all_inputs, grad_up_act, 0, 0).astype(BF16),
            dot(hidden, all_cotangent, 0, 0).astype(BF16),
        )

    return on_device


def solution(mesh):
    row, col = mesh.devices.shape
    sizes = (row // 2, 2, col // 4, 4)
    fine = Mesh(mesh.devices.reshape(sizes), ("y", "c", "z", "x"))
    token_width = P(("z", "x"), ("y", "c"))
    width_hidden = P(("y", "c"), ("z", "x"))
    return jax.shard_map(
        build(sizes),
        mesh=fine,
        in_specs=(token_width, width_hidden, width_hidden, token_width, token_width),
        out_specs=(token_width, width_hidden, width_hidden, token_width),
        check_vma=False,
    )
```

time: 193 us -> 179 us (0.927)
  the two profiles are of different devices: /device:TPU:1 before, /device:TPU:64 now
where the time goes in v2:
time: 179 us; the launch traced here: 178 us
  blocking collectives  90.3 us (50%)
  waiting for transfers between devices  33.9 us (19%)
  starting transfers between devices  22.3 us (12%)
  between operations  14.2 us (8%)
  local copies, waits for them, and re-layouts  6.36 us (4%)
  Pallas kernels  5.35 us (3%)
  matrix products  4.02 us (2%)
  other arithmetic  1.8 us (1%)
    all_to_all x2, blocking collectives, spread(): return lax.all_to_all(copies, axis, 0, 0)  38.4 us
    all_gather x1, blocking collectives, on_device(): own = lax.all_gather(pieces, 'y')  26.9 us
    all_to_all x1, blocking collectives, on_device(): lax.all_to_all(add_over_cores(all_cotangent, (w_down,), BF16), 'y', 0, 0)  25 us
    all_to_all x1, waiting for transfers between devices, on_device(): lax.all_to_all(share.reshape(nx * nz, rows, width), ('x', 'z'), 0, 0)  15.5 us
    all_to_all x1, starting transfers between devices, on_device(): lax.all_to_all(share.reshape(nx * nz, rows, width), ('x', 'z'), 0, 0)  10.3 us
    all_to_all x1, waiting for transfers between devices, spread(): return lax.all_to_all(copies, axis, 0, 0)  10.1 us
    ppermute x4, starting transfers between devices, sibling(): return lax.ppermute(value, 'c', SWAP)  7.67 us
    ppermute x4, waiting for transfers between devices, sibling(): return lax.ppermute(value, 'c', SWAP)  7.19 us
  transfers between devices with their start and end apart: 7, of which 7 were waited for; matrix products, arithmetic and copies ran while one was open for 4% of the time, Pallas kernels for 0%

profile of v2, /device:TPU:64, one launch (start us, length us, event | category | flops | bytes accessed | tf_op | source)
XLA Modules:
  0.0 178.2 jit_solution(10443424887807005682)
XLA Ops:
  8.0 23.0 %all_to_all.25 = bf16[8,24,1024]{2,1,0:T(8,128)(2,1)S(1)} all-to-all(bf16[8,24,1024]{2,1,0:T(8,128)(2,1)S(1)} %broadcast_in_dim.6), channel_id=1, replica_groups=mesh['y'=8,'c'=2,'z'=8,'x'=4] {'z'}, dimensions={0} | all-to-all | bytes 786432 | tf_op jit(solution)/shard_map/all_to_all | solution.py:27
  31.9 4.3 %all-to-all-start.1 = ((bf16[4,192,512]{2,1,0:T(8,128)(2,1)}), bf16[4,192,512]{2,1,0:T(8,128)(2,1)S(1)}, u32[]{:S(2)}, u32[]{:S(2)}) async-start(bf16[4,192,512]{2,1,0:T(8,128)(2,1)} %broadcast_in_dim.7), calls=%async_computation.1 | async-start | bytes 1572864 | tf_op jit(solution)/shard_map/all_to_all | solution.py:27
  36.2 10.1 %all-to-all-done.1 = bf16[4,192,512]{2,1,0:T(8,128)(2,1)S(1)} async-done(((bf16[4,192,512]{2,1,0:T(8,128)(2,1)}), bf16[4,192,512]{2,1,0:T(8,128)(2,1)S(1)}, u32[]{:S(2)}, u32[]{:S(2)}) %all-to-all-start.1) | async-done | bytes 786464 | tf_op jit(solution)/shard_map/all_to_all | solution.py:27
  47.0 1.9 %collective-permute-start = (f32[8,96,448]{2,1,0:T(8,128)S(1)}, f32[8,96,448]{2,1,0:T(8,128)S(1)}, u32[]{:S(2)}, u32[]{:S(2)}) collective-permute-start(f32[8,96,448]{2,1,0:T(8,128)S(1)} %shard_map.84), channel_id=1, source_target_pairs={{0,32},{32,0},{1,33},{33,1},{2,34},{34,2},{3,35},{35,3},{4,36},{36... | collective-permute-start | bytes 4128776 | tf_op jit(solution)/shard_map/ppermute | solution.py:22
  48.9 3.4 %collective-permute-done.refs_2_ = f32[8,96,448]{2,1,0:T(8,128)S(1)} collective-permute-done((f32[8,96,448]{2,1,0:T(8,128)S(1)}, f32[8,96,448]{2,1,0:T(8,128)S(1)}, u32[]{:S(2)}, u32[]{:S(2)}) %collective-permute-start) | collective-permute-done | bytes 1376288 | tf_op jit(solution)/shard_map/ppermute | solution.py:22
  52.3 1.8 shard_map.85
  54.1 15.4 %all_to_all.26 = bf16[4,192,512]{2,1,0:T(8,128)(2,1)S(1)} all-to-all(bf16[4,192,512]{2,1,0:T(8,128)(2,1)S(1)} %broadcast_in_dim.8), channel_id=1, replica_groups=mesh['y'=8,'c'=2,'z'=8,'x'=4] {'x'}, dimensions={0} | all-to-all | bytes 1572864 | tf_op jit(solution)/shard_map/all_to_all | solution.py:27
  69.9 1.9 %collective-permute-start.1 = (f32[8,48,448]{2,1,0:T(8,128)S(1)}, f32[8,48,448]{2,1,0:T(8,128)S(1)}, u32[]{:S(2)}, u32[]{:S(2)}) collective-permute-start(f32[8,48,448]{2,1,0:T(8,128)S(1)} %shard_map.86), channel_id=1, source_target_pairs={{0,32},{32,0},{1,33},{33,1},{2,34},{34,2},{3,35},{35,3},{4,36},{36... | collective-permute-start | bytes 2064392 | tf_op jit(solution)/shard_map/ppermute | solution.py:22
  71.9 2.3 %collective-permute-done.1.refs_1_ = f32[8,48,448]{2,1,0:T(8,128)S(1)} collective-permute-done((f32[8,48,448]{2,1,0:T(8,128)S(1)}, f32[8,48,448]{2,1,0:T(8,128)S(1)}, u32[]{:S(2)}, u32[]{:S(2)}) %collective-permute-start.1) | collective-permute-done | bytes 688160 | tf_op jit(solution)/shard_map/ppermute | solution.py:22
  74.5 25.0 %all_to_all.27.back_ref = bf16[8,48,448]{2,1,0:T(8,128)(2,1)S(1)} all-to-all(bf16[8,48,448]{2,1,0:T(8,128)(2,1)S(1)} %shard_map.87), channel_id=1, replica_groups=mesh['y'=8,'c'=2,'z'=8,'x'=4] {'y'}, dimensions={0} | all-to-all | bytes 688128 | tf_op jit(solution)/shard_map/all_to_all | solution.py:136
  99.5 1.1 reduce-scatter.2.cloned.1.call-done.gate_up_ref
  101.6 26.9 %all-gather = bf16[24,48,448]{2,1,0:T(8,128)(2,1)S(1)} all-gather(bf16[3,48,448]{2,1,0:T(8,128)(2,1)S(1)} %shard_map.88), channel_id=2, replica_groups=mesh['y'=8,'c'=2,'z'=8,'x'=4] {'y'}, dimensions={0}, use_global_device_ids=true | all-gather | bytes 1161216 | tf_op jit(solution)/shard_map/all_gather | solution.py:147
  128.5 1.0 slice.35
  129.4 1.9 %collective-permute-start.2 = (bf16[8,2,48,448]{3,2,1,0:T(8,128)(2,1)}, bf16[8,2,48,448]{3,2,1,0:T(8,128)(2,1)}, u32[]{:S(2)}, u32[]{:S(2)}) collective-permute-start(bf16[8,2,48,448]{3,2,1,0:T(8,128)(2,1)} %slice.35), channel_id=1, source_target_pairs={{0,32},{32,0},{1,33},{33,1},{2,34},{34,2},{3,35},{35,3},{4,36},{36... | collective-permute-start | bytes 2064392 | tf_op jit(solution)/shard_map/ppermute | solution.py:22
  131.4 1.2 fusion.12
  132.6 1.4 collective-permute-done.2.other_ref
  134.0 2.1 %shard_map.89 = bf16[768,512]{1,0:T(8,128)(2,1)S(1)} custom-call(s32[1]{0:T(128)} %bitcast.core_ref, bf16[8,3,48,448]{3,2,1,0:T(8,128)(2,1)S(1)} %bitcast.38, bf16[8,2,48,448]{3,2,1,0:T(8,128)(2,1)} %collective-permute-done.2.other_ref, bf16[448,512]{1,0:T(8,128)(2,1)S(1)} %bitcast.48, bf16[448,512]{1,0:T(8,128)(2,1)S(1)} %bitcast.51), custom_call_target="tpu_custom_call" | custom-call | flops 704643072 | bytes 2162688 | tf_op jit(solution)/shard_map/pallas_call | solution.py:35
  137.0 10.3 %all-to-all-start.4 = ((bf16[32,24,512]{2,1,0:T(8,128)(2,1)}), bf16[32,24,512]{2,1,0:T(8,128)(2,1)S(1)}, u32[]{:S(2)}, u32[]{:S(2)}) async-start(bf16[32,24,512]{2,1,0:T(8,128)(2,1)} %bitcast.52), calls=%async_computation.5 | async-start | bytes 1572864 | tf_op jit(solution)/shard_map/all_to_all | solution.py:160
  147.3 1.2 slice_bitcast_fusion
  148.6 1.9 %collective-permute-start.3 = (bf16[8,48,448]{2,1,0:T(8,128)(2,1)S(1)}, bf16[8,48,448]{2,1,0:T(8,128)(2,1)S(1)}, u32[]{:S(2)}, u32[]{:S(2)}) collective-permute-start(bf16[8,48,448]{2,1,0:T(8,128)(2,1)S(1)} %copy-done.9), channel_id=1, source_target_pairs={{0,32},{32,0},{1,33},{33,1},{2,34},{34,2},{3,35},{35,3},{4,36},{36... | collective-permute-start | bytes 1032200 | tf_op jit(solution)/shard_map/ppermute | solution.py:22
  150.7 1.3 convolution_convert_fusion.2
  152.4 1.3 convolution_convert_fusion.1
  153.8 1.3 convolution_convert_fusion
  155.1 15.5 %all-to-all-done.4 = bf16[32,24,512]{2,1,0:T(8,128)(2,1)S(1)} async-done(((bf16[32,24,512]{2,1,0:T(8,128)(2,1)}), bf16[32,24,512]{2,1,0:T(8,128)(2,1)S(1)}, u32[]{:S(2)}, u32[]{:S(2)}) %all-to-all-start.4) | async-done | bytes 786464 | tf_op jit(solution)/shard_map/all_to_all | solution.py:160
  (35 shorter events, 6.4 us)
Async XLA Ops:
  31.0 15.4 %copy-start = (bf16[512,448]{0,1:T(8,128)(2,1)S(1)}, bf16[512,448]{0,1:T(8,128)(2,1)}, u32[]{:S(2)}) copy-start(bf16[512,448]{0,1:T(8,128)(2,1)} %param.6) | copy-start | bytes 1376260
  31.0 15.4 %copy-start.1 = (bf16[512,448]{0,1:T(8,128)(2,1)S(1)}, bf16[512,448]{0,1:T(8,128)(2,1)}, u32[]{:S(2)}) copy-start(bf16[512,448]{0,1:T(8,128)(2,1)} %param.7) | copy-start | bytes 1376260
  31.9 14.4 %all-to-all-start.1 = ((bf16[4,192,512]{2,1,0:T(8,128)(2,1)}), bf16[4,192,512]{2,1,0:T(8,128)(2,1)S(1)}, u32[]{:S(2)}, u32[]{:S(2)}) async-start(bf16[4,192,512]{2,1,0:T(8,128)(2,1)} %broadcast_in_dim.7), calls=%async_computation.1 | async-start | bytes 1572864 | tf_op jit(solution)/shard_map/all_to_all | solution.py:27
  36.2 64.3 %reduce-scatter.2.cloned.1.call-start = ((), (), s32[]{:S(2)}) async-start(), calls=%async_computation.6 | async-start | bytes 1769472 | tf_op jit(solution)/shard_map/reduce_scatter | solution.py:130
  47.0 5.3 %collective-permute-start = (f32[8,96,448]{2,1,0:T(8,128)S(1)}, f32[8,96,448]{2,1,0:T(8,128)S(1)}, u32[]{:S(2)}, u32[]{:S(2)}) collective-permute-start(f32[8,96,448]{2,1,0:T(8,128)S(1)} %shard_map.84), channel_id=1, source_target_pairs={{0,32},{32,0},{1,33},{33,1},{2,34},{34,2},{3,35},{35,3},{4,36},{36... | collective-permute-start | bytes 4128776 | tf_op jit(solution)/shard_map/ppermute | solution.py:22
  54.1 15.5 %copy-start.4 = (bf16[448,512]{1,0:T(8,128)(2,1)S(1)}, bf16[448,512]{1,0:T(8,128)(2,1)}, u32[]{:S(2)}) copy-start(bf16[448,512]{1,0:T(8,128)(2,1)} %refs_0_.3) | copy-start | bytes 1376260
  69.9 4.2 %collective-permute-start.1 = (f32[8,48,448]{2,1,0:T(8,128)S(1)}, f32[8,48,448]{2,1,0:T(8,128)S(1)}, u32[]{:S(2)}, u32[]{:S(2)}) collective-permute-start(f32[8,48,448]{2,1,0:T(8,128)S(1)} %shard_map.86), channel_id=1, source_target_pairs={{0,32},{32,0},{1,33},{33,1},{2,34},{34,2},{3,35},{35,3},{4,36},{36... | collective-permute-start | bytes 2064392 | tf_op jit(solution)/shard_map/ppermute | solution.py:22
  100.5 0.9 copy-start.5
  129.4 4.5 %collective-permute-start.2 = (bf16[8,2,48,448]{3,2,1,0:T(8,128)(2,1)}, bf16[8,2,48,448]{3,2,1,0:T(8,128)(2,1)}, u32[]{:S(2)}, u32[]{:S(2)}) collective-permute-start(bf16[8,2,48,448]{3,2,1,0:T(8,128)(2,1)} %slice.35), channel_id=1, source_target_pairs={{0,32},{32,0},{1,33},{33,1},{2,34},{34,2},{3,35},{35,3},{4,36},{36... | collective-permute-start | bytes 2064392 | tf_op jit(solution)/shard_map/ppermute | solution.py:22
  131.4 2.6 %copy-start.2 = (bf16[512,448]{0,1:T(8,128)(2,1)S(1)}, bf16[512,448]{0,1:T(8,128)(2,1)}, u32[]{:S(2)}) copy-start(bf16[512,448]{0,1:T(8,128)(2,1)} %param.7) | copy-start | bytes 1376260
  136.1 0.9 copy-start.3
  137.0 13.5 %copy-start.6 = (bf16[8,1,48,448]{3,2,1,0:T(8,128)(2,1)S(1)}, bf16[8,1,48,448]{3,2,1,0:T(8,128)(2,1)}, u32[]{:S(2)}) copy-start(bf16[8,1,48,448]{3,2,1,0:T(8,128)(2,1)} %get-tuple-element.15) | copy-start | bytes 1032196
  137.0 33.6 %all-to-all-start.4 = ((bf16[32,24,512]{2,1,0:T(8,128)(2,1)}), bf16[32,24,512]{2,1,0:T(8,128)(2,1)S(1)}, u32[]{:S(2)}, u32[]{:S(2)}) async-start(bf16[32,24,512]{2,1,0:T(8,128)(2,1)} %bitcast.52), calls=%async_computation.5 | async-start | bytes 1572864 | tf_op jit(solution)/shard_map/all_to_all | solution.py:160
  147.3 1.2 copy-start.9
  148.6 3.6 %collective-permute-start.3 = (bf16[8,48,448]{2,1,0:T(8,128)(2,1)S(1)}, bf16[8,48,448]{2,1,0:T(8,128)(2,1)S(1)}, u32[]{:S(2)}, u32[]{:S(2)}) collective-permute-start(bf16[8,48,448]{2,1,0:T(8,128)(2,1)S(1)} %copy-done.9), channel_id=1, source_target_pairs={{0,32},{32,0},{1,33},{33,1},{2,34},{34,2},{3,35},{35,3},{4,36},{36... | collective-permute-start | bytes 1032200 | tf_op jit(solution)/shard_map/ppermute | solution.py:22
  150.6 1.6 copy-start.7
  150.6 1.6 copy-start.8
Sparse Core Ops, SparseCore 0:
  54.2 46.2 reduce-scatter.1

commit v3 on v1

v3 whole, which is shorter than its diff:
```python
import jax
import jax.numpy as jnp
from jax import lax
from jax.experimental import pallas as pl
from jax.experimental.pallas import tpu as pltpu
from jax.sharding import Mesh, PartitionSpec as P

F32 = jnp.float32
BF16 = jnp.bfloat16
SWAP = [(0, 1), (1, 0)]


def dot(left, right, left_dim, right_dim):
    return lax.dot_general(
        left, right, (((left_dim,), (right_dim,)), ((), ())), preferred_element_type=F32
    )


def sibling(value):
    return lax.ppermute(value, "c", SWAP)


def spread(block, axis, size):
    copies = jnp.broadcast_to(block[None], (size, *block.shape))
    return lax.all_to_all(copies, axis, 0, 0)


def after(value, *earlier):
    return lax.optimization_barrier((value, *earlier))[0]


def local(kernel, out_shape, flops, moved, core, *operands):
    return pl.pallas_call(
        kernel,
        out_shape=out_shape,
        in_specs=[pl.BlockSpec(memory_space=pltpu.SMEM)]
        + [pl.BlockSpec(memory_space=pltpu.VMEM)] * len(operands),
        out_specs=jax.tree.map(lambda _: pl.BlockSpec(memory_space=pltpu.VMEM), out_shape),
        compiler_params=pltpu.CompilerParams(vmem_limit_bytes=24 * 1024 * 1024),
        cost_estimate=pl.CostEstimate(flops=flops, bytes_accessed=moved, transcendentals=0),
    )(core.reshape(1).astype(jnp.int32), *operands)


def sums_kernel(core_ref, block_ref, own_ref, sib_ref, own_down_ref, sib_down_ref, out_ref):
    core = core_ref[0]
    packed, width = own_ref.shape
    half = block_ref.shape[0] * block_ref.shape[2]
    own = block_ref[:, core].reshape(half, 2 * width)
    sib = block_ref[:, 1 - core].reshape(half, 2 * width)
    sums = dot(own[:, :width], own_ref[...], 1, 1) + dot(sib[:, :width], sib_ref[...], 1, 1)
    back = dot(own[:, width:], own_down_ref[...], 1, 1) + dot(
        sib[:, width:], sib_down_ref[...], 1, 1
    )
    ny, rows, _ = out_ref.shape
    out_ref[:, :, :packed] = sums.astype(BF16).reshape(ny, rows, packed)
    out_ref[:, :, packed:] = back.astype(BF16).reshape(ny, rows, packed // 2)


def activations_kernel(core_ref, parts_ref, out_ref):
    columns = parts_ref.shape[2] // 3
    sums = jnp.sum(parts_ref[...].astype(F32), axis=0)
    gate_sum = sums[:, :columns]
    up_sum = sums[:, columns : 2 * columns]
    grad_hidden = sums[:, 2 * columns :]
    sigmoid_gate = jax.nn.sigmoid(gate_sum)
    activated = gate_sum * sigmoid_gate
    out_ref[:, :columns] = (
        grad_hidden * up_sum * sigmoid_gate * (1.0 + gate_sum * (1.0 - sigmoid_gate))
    ).astype(BF16)
    out_ref[:, columns : 2 * columns] = (grad_hidden * activated).astype(BF16)
    out_ref[:, 2 * columns :] = (activated * up_sum).astype(BF16)


def share_kernel(core_ref, pieces_ref, weight_ref, out_ref):
    packed = weight_ref.shape[0]
    pieces = pieces_ref[:, :, :packed].reshape(out_ref.shape[0], packed)
    out_ref[...] = dot(pieces, weight_ref[...], 1, 0).astype(BF16)


def join_kernel(core_ref, mine_ref, theirs_ref, out_ref):
    half = mine_ref.shape[0]
    out_ref[pl.ds(pl.multiple_of(core_ref[0] * half, half), half), :] = mine_ref[...]
    out_ref[pl.ds(pl.multiple_of((1 - core_ref[0]) * half, half), half), :] = theirs_ref[...]


def weights_kernel(
    core_ref,
    own_ref,
    other_ref,
    own_block_ref,
    other_block_ref,
    gate_ref,
    up_ref,
    down_ref,
):
    columns, width = gate_ref.shape
    half = own_ref.shape[0] * own_ref.shape[1]
    core = core_ref[0]
    own = own_ref[...].reshape(half, 3 * columns)
    other = other_ref[...].reshape(half, 3 * columns)
    own_block = own_block_ref[:, core].reshape(half, 2 * width)
    other_block = other_block_ref[...].reshape(half, 2 * width)
    packed = dot(own[:, : 2 * columns], own_block[:, :width], 0, 0) + dot(
        other[:, : 2 * columns], other_block[:, :width], 0, 0
    )
    gate_ref[...] = packed[:columns].astype(BF16)
    up_ref[...] = packed[columns:].astype(BF16)
    down_ref[...] = (
        dot(own[:, 2 * columns :], own_block[:, width:], 0, 0)
        + dot(other[:, 2 * columns :], other_block[:, width:], 0, 0)
    ).astype(BF16)


def build(sizes):
    ny, nc, nh, nl, nx = sizes
    nz = nh * nl

    def on_device(inputs, w_gate, w_up, w_down, cotangent):
        width, columns = w_gate.shape
        rows = inputs.shape[0]
        part = nl * rows
        half = part * nx
        share_rows = half // ny
        core = lax.axis_index("c")
        both = jnp.concatenate([inputs, cotangent], axis=1)
        along_z = lax.all_gather(both, ("h", "l", "c"), axis=0, tiled=True)
        along_z = along_z.reshape(nh, nl, nc, rows, 2 * width)
        kept = lax.dynamic_index_in_dim(along_z, core, 0, False)
        kept = kept.swapaxes(0, 1).reshape(nc, part, 2 * width)

        w_gate, w_up, w_down = (after(w, along_z) for w in (w_gate, w_up, w_down))
        own_gate_up = jnp.concatenate([w_gate.T, w_up.T], axis=0)
        sib_gate_up, sib_down = sibling(own_gate_up), sibling(w_down)
        block = spread(kept, "x", nx)
        sums = local(
            sums_kernel,
            jax.ShapeDtypeStruct((ny, share_rows, 3 * columns), BF16),
            12 * half * width * columns,
            8 * half * width + 12 * columns * width + 6 * half * columns,
            core,
            block,
            own_gate_up,
            sib_gate_up,
            w_down,
            sib_down,
        )
        pieces = local(
            activations_kernel,
            jax.ShapeDtypeStruct((share_rows, 3 * columns), BF16),
            20 * share_rows * columns,
            6 * half * columns,
            core,
            lax.all_to_all(sums, "y", 0, 0),
        )
        pieces = lax.all_gather(pieces, "y")

        def share(weight):
            return local(
                share_kernel,
                jax.ShapeDtypeStruct((half, width), BF16),
                4 * half * width * columns,
                6 * half * columns + 2 * half * width + 4 * columns * width,
                core,
                pieces,
                weight,
            )

        theirs = sibling(share(sib_gate_up))
        mine = share(own_gate_up)
        shares = local(
            join_kernel,
            jax.ShapeDtypeStruct((2 * half, width), BF16),
            0,
            8 * half * width,
            core,
            mine,
            theirs,
        )
        parts = lax.all_to_all(
            shares.reshape(nz * nx, rows, width), ("h", "x", "l"), 0, 0
        )
        grad_inputs = jnp.sum(parts.astype(F32), axis=0).astype(BF16)

        gradient = jax.ShapeDtypeStruct((columns, width), BF16)
        grad_gate, grad_up, grad_down = local(
            weights_kernel,
            (gradient, gradient, gradient),
            12 * half * width * columns,
            12 * half * columns + 8 * half * width + 6 * columns * width,
            core,
            pieces,
            sibling(after(pieces, shares)),
            block,
            sibling(lax.dynamic_index_in_dim(after(block, shares), 1 - core, 1, False)),
        )
        return grad_inputs, grad_gate.T, grad_up.T, grad_down

    return on_device


def solution(mesh):
    row, col = mesh.devices.shape
    sizes = (row // 2, 2, 2, col // 8, 4)
    fine = Mesh(mesh.devices.reshape(sizes), ("y", "c", "h", "l", "x"))
    token_width = P(("h", "l", "x"), ("y", "c"))
    width_hidden = P(("y", "c"), ("h", "l", "x"))
    return jax.shard_map(
        build(sizes),
        mesh=fine,
        in_specs=(token_width, width_hidden, width_hidden, token_width, token_width),
        out_specs=(token_width, width_hidden, width_hidden, token_width),
        check_vma=False,
    )
```

time: 193 us -> 155 us (0.80); the launches traced: 190 us -> 154 us
  waiting for transfers between devices: 52.2 us -> 30.6 us
  between operations: 14.2 us -> 0.8 us
  matrix products: 12.7 us -> 0 us
  starting transfers between devices: 18.3 us -> 27.2 us
  Pallas kernels: 0 us -> 7.41 us
  other arithmetic: 5.97 us -> 1.55 us
    all_to_all x2 -> x1, blocking collectives: 59.8 us -> 33.6 us  [on_device(): lax.all_to_all(sums, 'y', 0, 0)]
    all_gather x1 -> x2, blocking collectives: 23.6 us -> 48.7 us  [the longest x1 26.6 us: on_device(): along_z = lax.all_gather(both, ('h', 'l', 'c'), axis=0, tiled=True)]
    all_gather x1 -> x0, waiting for transfers between devices: 17.7 us -> none  [on_device(): pieces = lax.all_gather(pieces, 'c', axis=0, tiled=True)]
    ppermute x1 -> x5, starting transfers between devices: 5.22 us -> 19.1 us  [sibling(): return lax.ppermute(value, 'c', SWAP)]
    dot_general x11 -> x0, matrix products: 12.7 us -> none  [dot(): lax.dot_general(left, right, (((left_dim,), (right_dim,)), ((), ())), pre...]
    pallas_call x0 -> x6, Pallas kernels: none -> 7.41 us  [local(): pl.pallas_call(kernel, out_shape=out_shape, in_specs=[pl.BlockSpec(memory...]
    all_to_all x1, waiting for transfers between devices: 18.3 us -> 13.3 us  [spread(): return lax.all_to_all(copies, axis, 0, 0)]
    all_to_all x1, starting transfers between devices: 8.9 us -> 3.91 us  [on_device(): lax.all_to_all(shares.reshape(nz * nx, rows, width), ('h', 'x', 'l'), 0, 0)]
  transfers between devices with their start and end apart: 4 -> 7, of which waited for: 4 -> 5; matrix products, arithmetic and copies ran while one was open for 4% -> 0% of each run, Pallas kernels for 0% -> 3%
where the time goes in v3:
time: 155 us; the launch traced here: 154 us
  blocking collectives  82.3 us (53%)
  waiting for transfers between devices  30.6 us (20%)
  starting transfers between devices  27.2 us (18%)
  Pallas kernels  7.41 us (5%)
  local copies, waits for them, and re-layouts  4.31 us (3%)
  other arithmetic  1.55 us (1%)
    all_to_all x1, blocking collectives, on_device(): lax.all_to_all(sums, 'y', 0, 0)  33.6 us
    all_gather x1, blocking collectives, on_device(): along_z = lax.all_gather(both, ('h', 'l', 'c'), axis=0, tiled=True)  26.6 us
    all_gather x1, blocking collectives, on_device(): pieces = lax.all_gather(pieces, 'y')  22.1 us
    ppermute x5, starting transfers between devices, sibling(): return lax.ppermute(value, 'c', SWAP)  19.1 us
    all_to_all x1, waiting for transfers between devices, spread(): return lax.all_to_all(copies, axis, 0, 0)  13.3 us
    all_to_all x1, waiting for transfers between devices, on_device(): lax.all_to_all(shares.reshape(nz * nx, rows, width), ('h', 'x', 'l'), 0, 0)  12.7 us
    pallas_call x6, Pallas kernels, local(): pl.pallas_call(kernel, out_shape=out_shape, in_specs=[pl.BlockSpec(memory...  7.41 us
    ppermute x5, waiting for transfers between devices, sibling(): return lax.ppermute(value, 'c', SWAP)  4.6 us
  transfers between devices with their start and end apart: 7, of which 5 were waited for; matrix products, arithmetic and copies ran while one was open for 0% of the time, Pallas kernels for 3%

profile of v3, /device:TPU:1, one launch (start us, length us, event | category | flops | bytes accessed | tf_op | source)
XLA Modules:
  0.0 154.2 jit_solution(1175117012830882120)
XLA Ops:
  0.6 0.8 pad_maximum_fusion.1
  1.4 26.6 %all_gather.9 = bf16[384,1024]{1,0:T(8,128)(2,1)S(1)} all-gather(bf16[24,1024]{1,0:T(8,128)(2,1)S(1)} %pad_maximum_fusion.1), channel_id=1, replica_groups=mesh['y'=8,'c'=2,'h'=2,'l'=4,'x'=4] {'h','l','c'}, dimensions={0}, use_global_device_ids=true | all-gather | bytes 835584 | tf_op jit(solution)/shard_map/all_gather | solution.py:126
  28.1 1.4 broadcast_in_dim.8
  29.5 4.1 %all-to-all-start = ((bf16[4,2,96,1024]{3,2,1,0:T(8,128)(2,1)}), bf16[4,2,96,1024]{3,2,1,0:T(8,128)(2,1)S(1)}, u32[]{:S(2)}, u32[]{:S(2)}) async-start(bf16[4,2,96,1024]{3,2,1,0:T(8,128)(2,1)} %broadcast_in_dim.8), calls=%async_computation | async-start | bytes 3145728 | tf_op jit(solution)/shard_map/all_to_all | solution.py:25
  33.7 2.5 %collective-permute-start = (bf16[896,512]{1,0:T(8,128)(2,1)S(1)}, bf16[896,512]{1,0:T(8,128)(2,1)S(1)}, u32[]{:S(2)}, u32[]{:S(2)}) collective-permute-start(bf16[896,512]{1,0:T(8,128)(2,1)S(1)} %pad_maximum_fusion.own_ref.weight_ref), channel_id=1, source_target_pairs={{0,32},{32,0},{1,33},{33,1},{2,34},{34,2},{3,35},{35,3},{4,36},{36... | collective-permute-start | bytes 2752520 | tf_op jit(solution)/shard_map/ppermute | solution.py:20
  36.2 2.0 %collective-permute-start.1 = (bf16[448,512]{1,0:T(8,128)(2,1)S(1)}, bf16[448,512]{1,0:T(8,128)(2,1)S(1)}, u32[]{:S(2)}, u32[]{:S(2)}) collective-permute-start(bf16[448,512]{1,0:T(8,128)(2,1)S(1)} %copy-done.4), channel_id=1, source_target_pairs={{0,32},{32,0},{1,33},{33,1},{2,34},{34,2},{3,35},{35,3},{4,36},{36... | collective-permute-start | bytes 1376264 | tf_op jit(solution)/shard_map/ppermute | solution.py:20
  38.2 1.7 %collective-permute-done.1.sib_down_ref = bf16[448,512]{1,0:T(8,128)(2,1)S(1)} collective-permute-done((bf16[448,512]{1,0:T(8,128)(2,1)S(1)}, bf16[448,512]{1,0:T(8,128)(2,1)S(1)}, u32[]{:S(2)}, u32[]{:S(2)}) %collective-permute-start.1) | collective-permute-done | bytes 458784 | tf_op jit(solution)/shard_map/ppermute | solution.py:20
  39.9 0.8 copy-done.6
  40.7 13.3 %all-to-all-done.block_ref.own_block_ref = bf16[4,2,96,1024]{3,2,1,0:T(8,128)(2,1)S(1)} async-done(((bf16[4,2,96,1024]{3,2,1,0:T(8,128)(2,1)}), bf16[4,2,96,1024]{3,2,1,0:T(8,128)(2,1)S(1)}, u32[]{:S(2)}, u32[]{:S(2)}) %all-to-all-start) | async-done | bytes 1572896 | tf_op jit(solution)/shard_map/all_to_all | solution.py:25
  54.0 1.0 copy-done.5
  55.0 1.0 copy-done.7
  56.0 1.4 shard_map.84
  57.5 33.6 %all_to_all.15.parts_ref = bf16[8,48,1344]{2,1,0:T(8,128)(2,1)S(1)} all-to-all(bf16[8,48,1344]{2,1,0:T(8,128)(2,1)S(1)} %shard_map.84), channel_id=1, replica_groups=mesh['y'=8,'c'=2,'h'=2,'l'=4,'x'=4] {'y'}, dimensions={0} | all-to-all | bytes 2064384 | tf_op jit(solution)/shard_map/all_to_all | solution.py:153
  91.4 22.1 %all-gather = bf16[384,1344]{1,0:T(8,128)(2,1)S(1)} all-gather(bf16[48,1344]{1,0:T(8,128)(2,1)S(1)} %shard_map.85), channel_id=2, replica_groups=mesh['y'=8,'c'=2,'h'=2,'l'=4,'x'=4] {'y'}, dimensions={0}, use_global_device_ids=true | all-gather | bytes 1161216 | tf_op jit(solution)/shard_map/all_gather | solution.py:155
  114.0 10.3 %collective-permute-start.2 = (bf16[384,512]{1,0:T(8,128)(2,1)S(1)}, bf16[384,512]{1,0:T(8,128)(2,1)S(1)}, u32[]{:S(2)}, u32[]{:S(2)}) collective-permute-start(bf16[384,512]{1,0:T(8,128)(2,1)S(1)} %shard_map.87), channel_id=1, source_target_pairs={{0,32},{32,0},{1,33},{33,1},{2,34},{34,2},{3,35},{35,3},{4,36},{36... | collective-permute-start | bytes 1179656 | tf_op jit(solution)/shard_map/ppermute | solution.py:20
  125.0 0.7 collective-permute-done.2.theirs_ref
  125.7 1.0 shard_map.88
  126.7 3.9 %all-to-all-start.2 = ((bf16[32,24,512]{2,1,0:T(8,128)(2,1)}), bf16[32,24,512]{2,1,0:T(8,128)(2,1)S(1)}, u32[]{:S(2)}, u32[]{:S(2)}) async-start(bf16[32,24,512]{2,1,0:T(8,128)(2,1)} %bitcast.8), calls=%async_computation.2 | async-start | bytes 1572864 | tf_op jit(solution)/shard_map/all_to_all | solution.py:179
  130.6 2.3 %collective-permute-start.3 = (bf16[8,48,1344]{2,1,0:T(8,128)(2,1)S(1)}, bf16[8,48,1344]{2,1,0:T(8,128)(2,1)}, u32[]{:S(2)}, u32[]{:S(2)}) collective-permute-start(bf16[8,48,1344]{2,1,0:T(8,128)(2,1)S(1)} %bitcast.17), channel_id=1, source_target_pairs={{0,32},{32,0},{1,33},{33,1},{2,34},{34,2},{3,35},{35,3},{4,36},{36... | collective-permute-start | bytes 3096584 | tf_op jit(solution)/shard_map/ppermute | solution.py:20
  132.9 2.0 %collective-permute-start.4 = (bf16[4,96,1024]{2,1,0:T(8,128)(2,1)S(1)}, bf16[4,96,1024]{2,1,0:T(8,128)(2,1)S(1)}, u32[]{:S(2)}, u32[]{:S(2)}) collective-permute-start(bf16[4,96,1024]{2,1,0:T(8,128)(2,1)S(1)} %dynamic-slice_bitcast_fusion), channel_id=1, source_target_pairs={{0,32},{32,0},{1,33},{33,1},{2,34},{34,2},{3,35},{35,3},{4,36},{36... | collective-permute-start | bytes 2359304 | tf_op jit(solution)/shard_map/ppermute | solution.py:20
  135.0 2.1 %collective-permute-done.4.other_block_ref = bf16[4,96,1024]{2,1,0:T(8,128)(2,1)S(1)} collective-permute-done((bf16[4,96,1024]{2,1,0:T(8,128)(2,1)S(1)}, bf16[4,96,1024]{2,1,0:T(8,128)(2,1)S(1)}, u32[]{:S(2)}, u32[]{:S(2)}) %collective-permute-start.4) | collective-permute-done | bytes 786464 | tf_op jit(solution)/shard_map/ppermute | solution.py:20
  137.1 3.6 %shard_map.89 = (bf16[448,512]{1,0:T(8,128)(2,1)}, bf16[448,512]{1,0:T(8,128)(2,1)}, bf16[448,512]{1,0:T(8,128)(2,1)}) custom-call(s32[1]{0:T(128)} %bitcast.core_ref, bf16[8,48,1344]{2,1,0:T(8,128)(2,1)S(1)} %bitcast.18, bf16[8,48,1344]{2,1,0:T(8,128)(2,1)} %collective-permute-done.3.other_ref, ...), custom_call_target="tpu_custom_call" | custom-call | flops 1056964608 | bytes 5013504 | tf_op jit(solution)/shard_map/pallas_call | solution.py:33
  140.8 12.7 %all-to-all-done.2 = bf16[32,24,512]{2,1,0:T(8,128)(2,1)S(1)} async-done(((bf16[32,24,512]{2,1,0:T(8,128)(2,1)}), bf16[32,24,512]{2,1,0:T(8,128)(2,1)S(1)}, u32[]{:S(2)}, u32[]{:S(2)}) %all-to-all-start.2) | async-done | bytes 786464 | tf_op jit(solution)/shard_map/all_to_all | solution.py:179
  153.4 0.7 reduce_sum.12
  (26 shorter events, 1.6 us)
Async XLA Ops:
  29.5 4.2 %copy-start.8 = (bf16[512,448]{0,1:T(8,128)(2,1)S(1)}, bf16[512,448]{0,1:T(8,128)(2,1)}, u32[]{:S(2)}) copy-start(bf16[512,448]{0,1:T(8,128)(2,1)} %param.7) | copy-start | bytes 1376260
  29.5 4.2 %copy-start.9 = (bf16[512,448]{0,1:T(8,128)(2,1)S(1)}, bf16[512,448]{0,1:T(8,128)(2,1)}, u32[]{:S(2)}) copy-start(bf16[512,448]{0,1:T(8,128)(2,1)} %param.6) | copy-start | bytes 1376260
  29.5 24.5 %all-to-all-start = ((bf16[4,2,96,1024]{3,2,1,0:T(8,128)(2,1)}), bf16[4,2,96,1024]{3,2,1,0:T(8,128)(2,1)S(1)}, u32[]{:S(2)}, u32[]{:S(2)}) async-start(bf16[4,2,96,1024]{3,2,1,0:T(8,128)(2,1)} %broadcast_in_dim.8), calls=%async_computation | async-start | bytes 3145728 | tf_op jit(solution)/shard_map/all_to_all | solution.py:25
  33.6 2.6 %copy-start.4 = (bf16[448,512]{1,0:T(8,128)(2,1)S(1)}, bf16[448,512]{1,0:T(8,128)(2,1)}, u32[]{:S(2)}) copy-start(bf16[448,512]{1,0:T(8,128)(2,1)} %own_down_ref) | copy-start | bytes 1376260
  33.7 23.8 %copy-start = (bf16[896,512]{1,0:T(8,128)(2,1)}, bf16[896,512]{1,0:T(8,128)(2,1)S(1)}, u32[]{:S(2)}) copy-start(bf16[896,512]{1,0:T(8,128)(2,1)S(1)} %pad_maximum_fusion.own_ref.weight_ref) | copy-start | bytes 2752516
  33.7 7.0 %collective-permute-start = (bf16[896,512]{1,0:T(8,128)(2,1)S(1)}, bf16[896,512]{1,0:T(8,128)(2,1)S(1)}, u32[]{:S(2)}, u32[]{:S(2)}) collective-permute-start(bf16[896,512]{1,0:T(8,128)(2,1)S(1)} %pad_maximum_fusion.own_ref.weight_ref), channel_id=1, source_target_pairs={{0,32},{32,0},{1,33},{33,1},{2,34},{34,2},{3,35},{35,3},{4,36},{36... | collective-permute-start | bytes 2752520 | tf_op jit(solution)/shard_map/ppermute | solution.py:20
  36.2 3.7 %collective-permute-start.1 = (bf16[448,512]{1,0:T(8,128)(2,1)S(1)}, bf16[448,512]{1,0:T(8,128)(2,1)S(1)}, u32[]{:S(2)}, u32[]{:S(2)}) collective-permute-start(bf16[448,512]{1,0:T(8,128)(2,1)S(1)} %copy-done.4), channel_id=1, source_target_pairs={{0,32},{32,0},{1,33},{33,1},{2,34},{34,2},{3,35},{35,3},{4,36},{36... | collective-permute-start | bytes 1376264 | tf_op jit(solution)/shard_map/ppermute | solution.py:20
  39.9 0.8 copy-start.6
  40.7 16.8 %copy-start.2 = (bf16[896,512]{1,0:T(8,128)(2,1)}, bf16[896,512]{1,0:T(8,128)(2,1)S(1)}, u32[]{:S(2)}) copy-start(bf16[896,512]{1,0:T(8,128)(2,1)S(1)} %collective-permute-done.sib_ref.weight_ref) | copy-start | bytes 2752516
  54.0 1.0 copy-start.5
  55.0 1.0 copy-start.7
  91.1 22.3 %copy-start.3 = (bf16[896,512]{1,0:T(8,128)(2,1)S(1)}, bf16[896,512]{1,0:T(8,128)(2,1)}, u32[]{:S(2)}) copy-start(bf16[896,512]{1,0:T(8,128)(2,1)} %copy-done.2) | copy-start | bytes 2752516
  91.4 33.0 %copy-start.1 = (bf16[896,512]{1,0:T(8,128)(2,1)S(1)}, bf16[896,512]{1,0:T(8,128)(2,1)}, u32[]{:S(2)}) copy-start(bf16[896,512]{1,0:T(8,128)(2,1)} %copy-done) | copy-start | bytes 2752516
  114.0 11.7 %collective-permute-start.2 = (bf16[384,512]{1,0:T(8,128)(2,1)S(1)}, bf16[384,512]{1,0:T(8,128)(2,1)S(1)}, u32[]{:S(2)}, u32[]{:S(2)}) collective-permute-start(bf16[384,512]{1,0:T(8,128)(2,1)S(1)} %shard_map.87), channel_id=1, source_target_pairs={{0,32},{32,0},{1,33},{33,1},{2,34},{34,2},{3,35},{35,3},{4,36},{36... | collective-permute-start | bytes 1179656 | tf_op jit(solution)/shard_map/ppermute | solution.py:20
  126.7 26.8 %all-to-all-start.2 = ((bf16[32,24,512]{2,1,0:T(8,128)(2,1)}), bf16[32,24,512]{2,1,0:T(8,128)(2,1)S(1)}, u32[]{:S(2)}, u32[]{:S(2)}) async-start(bf16[32,24,512]{2,1,0:T(8,128)(2,1)} %bitcast.8), calls=%async_computation.2 | async-start | bytes 1572864 | tf_op jit(solution)/shard_map/all_to_all | solution.py:179
  130.6 6.5 %collective-permute-start.3 = (bf16[8,48,1344]{2,1,0:T(8,128)(2,1)S(1)}, bf16[8,48,1344]{2,1,0:T(8,128)(2,1)}, u32[]{:S(2)}, u32[]{:S(2)}) collective-permute-start(bf16[8,48,1344]{2,1,0:T(8,128)(2,1)S(1)} %bitcast.17), channel_id=1, source_target_pairs={{0,32},{32,0},{1,33},{33,1},{2,34},{34,2},{3,35},{35,3},{4,36},{36... | collective-permute-start | bytes 3096584 | tf_op jit(solution)/shard_map/ppermute | solution.py:20
  132.9 4.2 %collective-permute-start.4 = (bf16[4,96,1024]{2,1,0:T(8,128)(2,1)S(1)}, bf16[4,96,1024]{2,1,0:T(8,128)(2,1)S(1)}, u32[]{:S(2)}, u32[]{:S(2)}) collective-permute-start(bf16[4,96,1024]{2,1,0:T(8,128)(2,1)S(1)} %dynamic-slice_bitcast_fusion), channel_id=1, source_target_pairs={{0,32},{32,0},{1,33},{33,1},{2,34},{34,2},{3,35},{35,3},{4,36},{36... | collective-permute-start | bytes 2359304 | tf_op jit(solution)/shard_map/ppermute | solution.py:20

commit v4 on v3

v4 whole, which is shorter than its diff:
```python
import jax
import jax.numpy as jnp
from jax import lax
from jax.experimental import pallas as pl
from jax.experimental.pallas import tpu as pltpu
from jax.sharding import Mesh, PartitionSpec as P

F32 = jnp.float32
BF16 = jnp.bfloat16
SWAP = [(0, 1), (1, 0)]


def dot(left, right, left_dim, right_dim):
    return lax.dot_general(
        left, right, (((left_dim,), (right_dim,)), ((), ())), preferred_element_type=F32
    )


def sibling(value):
    return lax.ppermute(value, "c", SWAP)


def after(value, *earlier):
    return lax.optimization_barrier((value, *earlier))[0]


def local(kernel, out_shape, flops, moved, core, *operands):
    return pl.pallas_call(
        kernel,
        out_shape=out_shape,
        in_specs=[pl.BlockSpec(memory_space=pltpu.SMEM)]
        + [pl.BlockSpec(memory_space=pltpu.VMEM)] * len(operands),
        out_specs=jax.tree.map(lambda _: pl.BlockSpec(memory_space=pltpu.VMEM), out_shape),
        compiler_params=pltpu.CompilerParams(vmem_limit_bytes=16 * 1024 * 1024),
        cost_estimate=pl.CostEstimate(flops=flops, bytes_accessed=moved, transcendentals=0),
    )(core.reshape(1).astype(jnp.int32), *operands)


def sums_kernel(core_ref, block_ref, own_ref, sib_ref, out_ref):
    core = core_ref[0]
    half = block_ref.shape[0] * block_ref.shape[2]
    own = block_ref[:, core].reshape(half, block_ref.shape[3])
    sib = block_ref[:, 1 - core].reshape(half, block_ref.shape[3])
    sums = dot(own, own_ref[...], 1, 1) + dot(sib, sib_ref[...], 1, 1)
    out_ref[...] = sums.astype(BF16).reshape(out_ref.shape)


def activations_kernel(core_ref, gate_up_ref, back_ref, out_ref, hidden_ref):
    columns = back_ref.shape[2]
    gate_up = jnp.sum(gate_up_ref[...].astype(F32), axis=0)
    gate_sum = gate_up[:, :columns]
    up_sum = gate_up[:, columns:]
    grad_hidden = jnp.sum(back_ref[...].astype(F32), axis=0)
    sigmoid_gate = jax.nn.sigmoid(gate_sum)
    activated = gate_sum * sigmoid_gate
    grad_gate_act = grad_hidden * up_sum * sigmoid_gate * (1.0 + gate_sum * (1.0 - sigmoid_gate))
    out_ref[0, :, :columns] = grad_gate_act.astype(BF16)
    out_ref[0, :, columns:] = (grad_hidden * activated).astype(BF16)
    for k in range(1, out_ref.shape[0]):
        out_ref[k] = out_ref[0]
    hidden_ref[...] = (activated * up_sum).astype(BF16)


def share_kernel(core_ref, pieces_ref, weight_ref, out_ref):
    pieces = pieces_ref[...].reshape(out_ref.shape[0], weight_ref.shape[0])
    out_ref[...] = dot(pieces, weight_ref[...], 1, 0).astype(BF16)


def shares_kernel(core_ref, mine_ref, pieces_ref, weight_ref, out_ref):
    half = mine_ref.shape[0]
    pieces = pieces_ref[...].reshape(half, weight_ref.shape[0])
    theirs = dot(pieces, weight_ref[...], 1, 0).astype(BF16)
    out_ref[pl.ds(pl.multiple_of(core_ref[0] * half, half), half), :] = mine_ref[...]
    out_ref[pl.ds(pl.multiple_of((1 - core_ref[0]) * half, half), half), :] = theirs


def weights_kernel(
    core_ref,
    own_ref,
    other_ref,
    hidden_ref,
    own_inputs_ref,
    other_inputs_ref,
    own_cotangent_ref,
    other_cotangent_ref,
    gate_ref,
    up_ref,
    down_ref,
):
    columns, width = gate_ref.shape
    half = own_ref.shape[0] * own_ref.shape[1]
    core = core_ref[0]
    own = own_ref[...].reshape(half, 2 * columns)
    other = other_ref[...].reshape(half, 2 * columns)
    own_hidden = hidden_ref[:, core].reshape(half, columns)
    other_hidden = hidden_ref[:, 1 - core].reshape(half, columns)
    own_inputs = own_inputs_ref[:, core].reshape(half, width)
    other_inputs = other_inputs_ref[...].reshape(half, width)
    own_cotangent = own_cotangent_ref[:, core].reshape(half, width)
    other_cotangent = other_cotangent_ref[...].reshape(half, width)
    packed = dot(own, own_inputs, 0, 0) + dot(other, other_inputs, 0, 0)
    gate_ref[...] = packed[:columns].astype(BF16)
    up_ref[...] = packed[columns:].astype(BF16)
    down_ref[...] = (
        dot(own_hidden, own_cotangent, 0, 0)
        + dot(other_hidden, other_cotangent, 0, 0)
    ).astype(BF16)


def total_kernel(core_ref, parts_ref, out_ref):
    out_ref[...] = jnp.sum(parts_ref[...].astype(F32), axis=0).astype(BF16)


def build(sizes):
    ny, nc, nh, nl, nx = sizes
    nz = nh * nl

    def on_device(inputs, w_gate, w_up, w_down, cotangent):
        width, columns = w_gate.shape
        rows = inputs.shape[0]
        part = nl * rows
        half = part * nx
        share_rows = half // ny
        core = lax.axis_index("c")
        both = jnp.concatenate([inputs, cotangent], axis=1)
        along_z = lax.all_gather(both, ("h", "l", "c"), axis=0, tiled=True)
        along_z = along_z.reshape(nh, nl, nc, rows, 2 * width)
        kept = lax.dynamic_index_in_dim(along_z, core, 0, False)
        kept = kept.swapaxes(0, 1).reshape(nc, part, 2 * width)

        w_gate, w_up, w_down = (after(w, along_z) for w in (w_gate, w_up, w_down))
        own_gate_up = jnp.concatenate([w_gate.T, w_up.T], axis=0)
        sib_gate_up, sib_down = sibling(own_gate_up), sibling(w_down)
        def sums(block, own, sib):
            return local(
                sums_kernel,
                jax.ShapeDtypeStruct((ny, share_rows, own.shape[0]), BF16),
                4 * half * width * own.shape[0],
                4 * (half + own.shape[0]) * width + 2 * half * own.shape[0],
                core,
                block,
                own,
                sib,
            )

        def of_other_tokens(block, earlier):
            return sibling(lax.dynamic_index_in_dim(after(block, earlier), 1 - core, 1, False))

        all_inputs = lax.all_gather(kept[:, :, :width], "x")
        gate_up = sums(all_inputs, own_gate_up, sib_gate_up)
        all_cotangent = lax.all_gather(after(kept[:, :, width:], gate_up), "x")
        other_inputs = of_other_tokens(all_inputs, gate_up)
        gate_up = lax.all_to_all(gate_up, "y", 0, 0)
        back = sums(after(all_cotangent, gate_up, other_inputs), w_down, sib_down)
        back = lax.all_to_all(back, "y", 0, 0)
        pieces, hidden = local(
            activations_kernel,
            (
                jax.ShapeDtypeStruct((ny, share_rows, 2 * columns), BF16),
                jax.ShapeDtypeStruct((share_rows, columns), BF16),
            ),
            20 * share_rows * columns,
            10 * half * columns,
            core,
            gate_up,
            back,
        )
        pieces = lax.all_to_all(pieces, "y", 0, 0)

        other_pieces = sibling(pieces)
        flops = 4 * half * width * columns
        moved = 4 * half * columns + 2 * half * width + 4 * columns * width
        mine = local(
            share_kernel,
            jax.ShapeDtypeStruct((half, width), BF16),
            flops,
            moved,
            core,
            pieces,
            own_gate_up,
        )
        shares = local(
            shares_kernel,
            pltpu.HBM((2 * half, width), BF16),
            flops,
            moved + 4 * half * width,
            core,
            mine,
            other_pieces,
            own_gate_up,
        )
        parts = lax.all_to_all(
            shares.reshape(nz * nx, rows, width), ("h", "x", "l"), 0, 0
        )
        grad_inputs = local(
            total_kernel,
            jax.ShapeDtypeStruct((rows, width), BF16),
            2 * half * width,
            4 * half * width,
            core,
            parts,
        )

        gradient = jax.ShapeDtypeStruct((columns, width), BF16)
        grad_gate, grad_up, grad_down = local(
            weights_kernel,
            (gradient, gradient, gradient),
            12 * half * width * columns,
            12 * half * columns + 8 * half * width + 6 * columns * width,
            core,
            pieces,
            other_pieces,
            lax.all_gather(after(hidden, shares), ("y", "c"), axis=0, tiled=True).reshape(
                ny, nc, share_rows, columns
            ),
            all_inputs,
            other_inputs,
            all_cotangent,
            of_other_tokens(all_cotangent, shares),
        )
        return grad_inputs, grad_gate.T, grad_up.T, grad_down

    return on_device


def solution(mesh):
    row, col = mesh.devices.shape
    sizes = (row // 2, 2, 2, col // 8, 4)
    fine = Mesh(mesh.devices.reshape(sizes), ("y", "c", "h", "l", "x"))
    token_width = P(("h", "l", "x"), ("y", "c"))
    width_hidden = P(("y", "c"), ("h", "l", "x"))
    return jax.shard_map(
        build(sizes),
        mesh=fine,
        in_specs=(token_width, width_hidden, width_hidden, token_width, token_width),
        out_specs=(token_width, width_hidden, width_hidden, token_width),
        check_vma=False,
    )
```

time: 155 us -> 150 us (0.968)
  waiting for transfers between devices: 30.6 us -> 2.08 us
  blocking collectives: 82.3 us -> 106 us
  local copies, waits for them, and re-layouts: 4.31 us -> 0.93 us
  starting transfers between devices: 27.2 us -> 29.3 us
  Pallas kernels: 7.41 us -> 9.01 us
    all_gather x1 -> x3, blocking collectives: 22.1 us -> 41.3 us  [the longest x1 16.7 us: on_device(): lax.all_gather(after(hidden, shares), ('y', 'c'), axis=0, tiled=True)]
    all_to_all x1, waiting for transfers between devices: 13.3 us -> 0.01 us  [on_device(): gate_up = lax.all_to_all(gate_up, 'y', 0, 0)]
    all_to_all x1, waiting for transfers between devices: 12.7 us -> 0.89 us  [on_device(): lax.all_to_all(shares.reshape(nz * nx, rows, width), ('h', 'x', 'l'), 0, 0)]
    all_to_all x1 -> x2, blocking collectives: 33.6 us -> 38.4 us  [the longest x1 20 us: on_device(): pieces = lax.all_to_all(pieces, 'y', 0, 0)]
    ppermute x5, waiting for transfers between devices: 4.6 us -> 1.18 us  [sibling(): return lax.ppermute(value, 'c', SWAP)]
    all_to_all x1, starting transfers between devices: 4.14 us -> 6.82 us  [on_device(): gate_up = lax.all_to_all(gate_up, 'y', 0, 0)]
    unnamed x20 -> x12, local copies, waits for them, and re-layouts: 2.83 us -> 0.77 us
    pallas_call x6 -> x7, Pallas kernels: 7.41 us -> 9.01 us  [local(): pl.pallas_call(kernel, out_shape=out_shape, in_specs=[pl.BlockSpec(memory...]
  transfers between devices with their start and end apart: 7 -> 7, of which waited for: 5 -> 2; matrix products, arithmetic and copies ran while one was open for 0% -> 0% of each run, Pallas kernels for 3% -> 2%
where the time goes in v4:
time: 150 us; the launch traced here: 149 us
  blocking collectives  106 us (71%)
  starting transfers between devices  29.3 us (20%)
  Pallas kernels  9.01 us (6%)
  waiting for transfers between devices  2.08 us (1%)
    all_gather x1, blocking collectives, on_device(): along_z = lax.all_gather(both, ('h', 'l', 'c'), axis=0, tiled=True)  26.6 us
    all_to_all x1, blocking collectives, on_device(): pieces = lax.all_to_all(pieces, 'y', 0, 0)  20 us
    all_to_all x1, blocking collectives, on_device(): back = lax.all_to_all(back, 'y', 0, 0)  18.4 us
    ppermute x5, starting transfers between devices, sibling(): return lax.ppermute(value, 'c', SWAP)  17.9 us
    all_gather x1, blocking collectives, on_device(): lax.all_gather(after(hidden, shares), ('y', 'c'), axis=0, tiled=True)  16.7 us
    all_gather x1, blocking collectives, on_device(): all_cotangent = lax.all_gather(after(kept[:, :, width:], gate_up), 'x')  12.6 us
    all_gather x1, blocking collectives, on_device(): all_inputs = lax.all_gather(kept[:, :, :width], 'x')  12 us
    pallas_call x7, Pallas kernels, local(): pl.pallas_call(kernel, out_shape=out_shape, in_specs=[pl.BlockSpec(memory...  9.01 us
  transfers between devices with their start and end apart: 7, of which 2 were waited for; matrix products, arithmetic and copies ran while one was open for 0% of the time, Pallas kernels for 2%

profile of v4, /device:TPU:1, one launch (start us, length us, event | category | flops | bytes accessed | tf_op | source)
XLA Modules:
  0.0 149.3 jit_solution(15915044081090540600)
XLA Ops:
  0.7 0.8 pad_maximum_fusion.1
  1.5 26.6 %all_gather.18 = bf16[384,1024]{1,0:T(8,128)(2,1)S(1)} all-gather(bf16[24,1024]{1,0:T(8,128)(2,1)S(1)} %pad_maximum_fusion.1), channel_id=1, replica_groups=mesh['y'=8,'c'=2,'h'=2,'l'=4,'x'=4] {'h','l','c'}, dimensions={0}, use_global_device_ids=true | all-gather | bytes 835584 | tf_op jit(solution)/shard_map/all_gather | solution.py:126
  28.2 2.1 %collective-permute-start = (bf16[896,512]{1,0:T(8,128)(2,1)S(1)}, bf16[896,512]{1,0:T(8,128)(2,1)S(1)}, u32[]{:S(2)}, u32[]{:S(2)}) collective-permute-start(bf16[896,512]{1,0:T(8,128)(2,1)S(1)} %pad_maximum_fusion.own_ref.weight_ref), channel_id=1, source_target_pairs={{0,32},{32,0},{1,33},{33,1},{2,34},{34,2},{3,35},{35,3},{4,36},{36... | collective-permute-start | bytes 2752520 | tf_op jit(solution)/shard_map/ppermute | solution.py:20
  30.4 12.0 %all-gather = bf16[8,96,512]{2,1,0:T(8,128)(2,1)S(1)} all-gather(bf16[2,96,512]{2,1,0:T(8,128)(2,1)S(1)} %get-tuple-element.31), channel_id=2, replica_groups=mesh['y'=8,'c'=2,'h'=2,'l'=4,'x'=4] {'x'}, dimensions={0}, use_global_device_ids=true | all-gather | bytes 983040 | tf_op jit(solution)/shard_map/all_gather | solution.py:149
  42.4 1.9 %shard_map.84 = bf16[8,48,896]{2,1,0:T(8,128)(2,1)} custom-call(s32[1]{0:T(128)} %bitcast.core_ref, bf16[4,2,96,512]{3,2,1,0:T(8,128)(2,1)S(1)} %bitcast.19, bf16[896,512]{1,0:T(8,128)(2,1)S(1)} %pad_maximum_fusion.own_ref.weight_ref, bf16[896,512]{1,0:T(8,128)(2,1)S(1)} %collective-permute-done.sib_ref), custom_call_target="tpu_custom_call" | custom-call | flops 704643072 | bytes 3309568 | tf_op jit(solution)/shard_map/pallas_call | solution.py:28
  44.3 6.8 %all-to-all-start = ((bf16[8,48,896]{2,1,0:T(8,128)(2,1)}), bf16[8,48,896]{2,1,0:T(8,128)(2,1)S(1)}, u32[]{:S(2)}, u32[]{:S(2)}) async-start(bf16[8,48,896]{2,1,0:T(8,128)(2,1)} %shard_map.84), calls=%async_computation | async-start | bytes 1376256 | tf_op jit(solution)/shard_map/all_to_all | solution.py:153
  51.1 4.4 %collective-permute-start.2 = (bf16[448,512]{1,0:T(8,128)(2,1)}, bf16[448,512]{1,0:T(8,128)(2,1)}, u32[]{:S(2)}, u32[]{:S(2)}) collective-permute-start(bf16[448,512]{1,0:T(8,128)(2,1)} %own_ref), channel_id=1, source_target_pairs={{0,32},{32,0},{1,33},{33,1},{2,34},{34,2},{3,35},{35,3},{4,36},{36... | collective-permute-start | bytes 1376264 | tf_op jit(solution)/shard_map/ppermute | solution.py:20
  55.6 1.9 %collective-permute-start.1 = (bf16[4,96,512]{2,1,0:T(8,128)(2,1)S(1)}, bf16[4,96,512]{2,1,0:T(8,128)(2,1)S(1)}, u32[]{:S(2)}, u32[]{:S(2)}) collective-permute-start(bf16[4,96,512]{2,1,0:T(8,128)(2,1)S(1)} %dynamic-slice_bitcast_fusion.1), channel_id=1, source_target_pairs={{0,32},{32,0},{1,33},{33,1},{2,34},{34,2},{3,35},{35,3},{4,36},{36... | collective-permute-start | bytes 1179656 | tf_op jit(solution)/shard_map/ppermute | solution.py:20
  57.5 12.6 %all-gather.1 = bf16[8,96,512]{2,1,0:T(8,128)(2,1)S(1)} all-gather(bf16[2,96,512]{2,1,0:T(8,128)(2,1)S(1)} %get-tuple-element.19), channel_id=3, replica_groups=mesh['y'=8,'c'=2,'h'=2,'l'=4,'x'=4] {'x'}, dimensions={0}, use_global_device_ids=true | all-gather | bytes 983040 | tf_op jit(solution)/shard_map/all_gather | solution.py:151
  70.1 0.7 copy-done.2
  70.8 1.7 %shard_map.85 = bf16[8,48,448]{2,1,0:T(8,128)(2,1)S(1)} custom-call(s32[1]{0:T(128)} %bitcast.core_ref, bf16[4,2,96,512]{3,2,1,0:T(8,128)(2,1)S(1)} %bitcast.22, bf16[448,512]{1,0:T(8,128)(2,1)} %own_ref, bf16[448,512]{1,0:T(8,128)(2,1)} %collective-permute-done.2.sib_ref), custom_call_target="tpu_custom_call" | custom-call | flops 352321536 | bytes 2048000 | tf_op jit(solution)/shard_map/pallas_call | solution.py:28
  72.6 18.4 %all_to_all.20.back_ref = bf16[8,48,448]{2,1,0:T(8,128)(2,1)S(1)} all-to-all(bf16[8,48,448]{2,1,0:T(8,128)(2,1)S(1)} %shard_map.85), channel_id=1, replica_groups=mesh['y'=8,'c'=2,'h'=2,'l'=4,'x'=4] {'y'}, dimensions={0} | all-to-all | bytes 688128 | tf_op jit(solution)/shard_map/all_to_all | solution.py:155
  90.9 0.2 shard_map.86
  91.2 20.0 %all_to_all.21.pieces_ref.own_ref = bf16[8,48,896]{2,1,0:T(8,128)(2,1)S(1)} all-to-all(bf16[8,48,896]{2,1,0:T(8,128)(2,1)S(1)} %get-tuple-element.23), channel_id=1, replica_groups=mesh['y'=8,'c'=2,'h'=2,'l'=4,'x'=4] {'y'}, dimensions={0} | all-to-all | bytes 1376256 | tf_op jit(solution)/shard_map/all_to_all | solution.py:168
  111.2 6.8 %collective-permute-start.3 = (bf16[8,48,896]{2,1,0:T(8,128)(2,1)S(1)}, bf16[8,48,896]{2,1,0:T(8,128)(2,1)S(1)}, u32[]{:S(2)}, u32[]{:S(2)}) collective-permute-start(bf16[8,48,896]{2,1,0:T(8,128)(2,1)S(1)} %all_to_all.21.pieces_ref.own_ref), channel_id=1, source_target_pairs={{0,32},{32,0},{1,33},{33,1},{2,34},{34,2},{3,35},{35,3},{4,36},{36... | collective-permute-start | bytes 2064392 | tf_op jit(solution)/shard_map/ppermute | solution.py:20
  118.0 0.6 shard_map.87.mine_ref
  118.6 1.2 collective-permute-done.3.pieces_ref.other_ref
  119.7 1.5 shard_map.88
  121.2 4.5 %all-to-all-start.3 = ((bf16[32,24,512]{2,1,0:T(8,128)(2,1)}), bf16[32,24,512]{2,1,0:T(8,128)(2,1)S(1)}, u32[]{:S(2)}, u32[]{:S(2)}) async-start(bf16[32,24,512]{2,1,0:T(8,128)(2,1)} %bitcast.26), calls=%async_computation.3 | async-start | bytes 1572864 | tf_op jit(solution)/shard_map/all_to_all | solution.py:192
  125.8 2.7 %collective-permute-start.4 = (bf16[4,96,512]{2,1,0:T(8,128)(2,1)S(1)}, bf16[4,96,512]{2,1,0:T(8,128)(2,1)S(1)}, u32[]{:S(2)}, u32[]{:S(2)}) collective-permute-start(bf16[4,96,512]{2,1,0:T(8,128)(2,1)S(1)} %dynamic-slice_bitcast_fusion), channel_id=1, source_target_pairs={{0,32},{32,0},{1,33},{33,1},{2,34},{34,2},{3,35},{35,3},{4,36},{36... | collective-permute-start | bytes 1179656 | tf_op jit(solution)/shard_map/ppermute | solution.py:20
  128.5 16.7 %all_gather.23 = bf16[768,448]{1,0:T(8,128)(2,1)S(1)} all-gather(bf16[48,448]{1,0:T(8,128)(2,1)S(1)} %get-tuple-element.25), channel_id=1, replica_groups=mesh['y'=8,'c'=2,'h'=2,'l'=4,'x'=4] {'y','c'}, dimensions={0}, use_global_device_ids=true | all-gather | bytes 731136 | tf_op jit(solution)/shard_map/all_gather | solution.py:213
  145.3 2.4 %shard_map.90 = (bf16[448,512]{1,0:T(8,128)(2,1)}, bf16[448,512]{1,0:T(8,128)(2,1)}, bf16[448,512]{1,0:T(8,128)(2,1)}) custom-call(s32[1]{0:T(128)} %bitcast.core_ref, bf16[8,48,896]{2,1,0:T(8,128)(2,1)S(1)} %all_to_all.21.pieces_ref.own_ref, bf16[8,48,896]{2,1,0:T(8,128)(2,1)S(1)} %copy-done.1, bf16[8,2,48,448]{3,2,1,0:T(8,128)(2,1)S(1)} %bitcast.25, ...), custom_call_target="tpu_custom_call" | custom-call | flops 1056964608 | bytes 5013504 | tf_op jit(solution)/shard_map/pallas_call | solution.py:28
  147.7 0.9 all-to-all-done.3.parts_ref
  148.6 0.7 shard_map.89
  (22 shorter events, 0.3 us)
Async XLA Ops:
  0.6 27.5 %copy-start.4 = (bf16[512,448]{0,1:T(8,128)(2,1)S(1)}, bf16[512,448]{0,1:T(8,128)(2,1)}, u32[]{:S(2)}) copy-start(bf16[512,448]{0,1:T(8,128)(2,1)} %param.7) | copy-start | bytes 1376260
  0.6 27.5 %copy-start.5 = (bf16[512,448]{0,1:T(8,128)(2,1)S(1)}, bf16[512,448]{0,1:T(8,128)(2,1)}, u32[]{:S(2)}) copy-start(bf16[512,448]{0,1:T(8,128)(2,1)} %param.6) | copy-start | bytes 1376260
  28.2 14.2 %collective-permute-start = (bf16[896,512]{1,0:T(8,128)(2,1)S(1)}, bf16[896,512]{1,0:T(8,128)(2,1)S(1)}, u32[]{:S(2)}, u32[]{:S(2)}) collective-permute-start(bf16[896,512]{1,0:T(8,128)(2,1)S(1)} %pad_maximum_fusion.own_ref.weight_ref), channel_id=1, source_target_pairs={{0,32},{32,0},{1,33},{33,1},{2,34},{34,2},{3,35},{35,3},{4,36},{36... | collective-permute-start | bytes 2752520 | tf_op jit(solution)/shard_map/ppermute | solution.py:20
  44.3 26.6 %all-to-all-start = ((bf16[8,48,896]{2,1,0:T(8,128)(2,1)}), bf16[8,48,896]{2,1,0:T(8,128)(2,1)S(1)}, u32[]{:S(2)}, u32[]{:S(2)}) async-start(bf16[8,48,896]{2,1,0:T(8,128)(2,1)} %shard_map.84), calls=%async_computation | async-start | bytes 1376256 | tf_op jit(solution)/shard_map/all_to_all | solution.py:153
  51.1 19.7 %collective-permute-start.2 = (bf16[448,512]{1,0:T(8,128)(2,1)}, bf16[448,512]{1,0:T(8,128)(2,1)}, u32[]{:S(2)}, u32[]{:S(2)}) collective-permute-start(bf16[448,512]{1,0:T(8,128)(2,1)} %own_ref), channel_id=1, source_target_pairs={{0,32},{32,0},{1,33},{33,1},{2,34},{34,2},{3,35},{35,3},{4,36},{36... | collective-permute-start | bytes 1376264 | tf_op jit(solution)/shard_map/ppermute | solution.py:20
  55.6 14.5 %collective-permute-start.1 = (bf16[4,96,512]{2,1,0:T(8,128)(2,1)S(1)}, bf16[4,96,512]{2,1,0:T(8,128)(2,1)S(1)}, u32[]{:S(2)}, u32[]{:S(2)}) collective-permute-start(bf16[4,96,512]{2,1,0:T(8,128)(2,1)S(1)} %dynamic-slice_bitcast_fusion.1), channel_id=1, source_target_pairs={{0,32},{32,0},{1,33},{33,1},{2,34},{34,2},{3,35},{35,3},{4,36},{36... | collective-permute-start | bytes 1179656 | tf_op jit(solution)/shard_map/ppermute | solution.py:20
  70.1 0.7 copy-start.2
  111.2 8.5 %collective-permute-start.3 = (bf16[8,48,896]{2,1,0:T(8,128)(2,1)S(1)}, bf16[8,48,896]{2,1,0:T(8,128)(2,1)S(1)}, u32[]{:S(2)}, u32[]{:S(2)}) collective-permute-start(bf16[8,48,896]{2,1,0:T(8,128)(2,1)S(1)} %all_to_all.21.pieces_ref.own_ref), channel_id=1, source_target_pairs={{0,32},{32,0},{1,33},{33,1},{2,34},{34,2},{3,35},{35,3},{4,36},{36... | collective-permute-start | bytes 2064392 | tf_op jit(solution)/shard_map/ppermute | solution.py:20
  119.7 1.5 copy-start
  121.2 27.4 %all-to-all-start.3 = ((bf16[32,24,512]{2,1,0:T(8,128)(2,1)}), bf16[32,24,512]{2,1,0:T(8,128)(2,1)S(1)}, u32[]{:S(2)}, u32[]{:S(2)}) async-start(bf16[32,24,512]{2,1,0:T(8,128)(2,1)} %bitcast.26), calls=%async_computation.3 | async-start | bytes 1572864 | tf_op jit(solution)/shard_map/all_to_all | solution.py:192
  125.8 19.5 %copy-start.1 = (bf16[8,48,896]{2,1,0:T(8,128)(2,1)S(1)}, bf16[8,48,896]{2,1,0:T(8,128)(2,1)}, u32[]{:S(2)}) copy-start(bf16[8,48,896]{2,1,0:T(8,128)(2,1)} %copy-done) | copy-start | bytes 2064388
  125.8 19.5 %copy-start.3 = (bf16[4,96,512]{2,1,0:T(8,128)(2,1)S(1)}, bf16[4,96,512]{2,1,0:T(8,128)(2,1)}, u32[]{:S(2)}) copy-start(bf16[4,96,512]{2,1,0:T(8,128)(2,1)} %copy-done.2) | copy-start | bytes 1179652
  125.8 19.5 %collective-permute-start.4 = (bf16[4,96,512]{2,1,0:T(8,128)(2,1)S(1)}, bf16[4,96,512]{2,1,0:T(8,128)(2,1)S(1)}, u32[]{:S(2)}, u32[]{:S(2)}) collective-permute-start(bf16[4,96,512]{2,1,0:T(8,128)(2,1)S(1)} %dynamic-slice_bitcast_fusion), channel_id=1, source_target_pairs={{0,32},{32,0},{1,33},{33,1},{2,34},{34,2},{3,35},{35,3},{4,36},{36... | collective-permute-start | bytes 1179656 | tf_op jit(solution)/shard_map/ppermute | solution.py:20

commit v5 on v4

--- a/solution.py
+++ b/solution.py
@@ -24,33 +24,64 @@
     return lax.optimization_barrier((value, *earlier))[0]
 
 
-def local(kernel, out_shape, flops, moved, core, *operands):
+def local(kernel, out_shape, flops, moved, core, *operands, fetched=()):
+    scratch = [pltpu.VMEM(value.shape, value.dtype) for value in fetched]
+    if fetched:
+        scratch.append(pltpu.SemaphoreType.DMA((len(fetched),)))
+    spaces = [pltpu.SMEM] + [pltpu.VMEM] * len(operands) + [pltpu.HBM] * len(fetched)
     return pl.pallas_call(
         kernel,
         out_shape=out_shape,
-        in_specs=[pl.BlockSpec(memory_space=pltpu.SMEM)]
-        + [pl.BlockSpec(memory_space=pltpu.VMEM)] * len(operands),
+        in_specs=[pl.BlockSpec(memory_space=space) for space in spaces],
         out_specs=jax.tree.map(lambda _: pl.BlockSpec(memory_space=pltpu.VMEM), out_shape),
+        scratch_shapes=scratch,
         compiler_params=pltpu.CompilerParams(vmem_limit_bytes=16 * 1024 * 1024),
         cost_estimate=pl.CostEstimate(flops=flops, bytes_accessed=moved, transcendentals=0),
-    )(core.reshape(1).astype(jnp.int32), *operands)
-
-
-def sums_kernel(core_ref, block_ref, own_ref, sib_ref, out_ref):
+    )(
+        core.reshape(1).astype(jnp.int32),
+        *operands,
+        *(pltpu.with_memory_space_constraint(value, pltpu.HBM) for value in fetched),
+    )
+
+
+def sums_kernel(
+    core_ref,
+    block_ref,
+    own_ref,
+    sib_ref,
+    own_down_hbm,
+    sib_down_hbm,
+    out_ref,
+    own_down_ref,
+    sib_down_ref,
+    semaphores,
+):
+    own_copy = pltpu.make_async_copy(own_down_hbm, own_down_ref, semaphores.at[0])
+    sib_copy = pltpu.make_async_copy(sib_down_hbm, sib_down_ref, semaphores.at[1])
+    own_copy.start()
+    sib_copy.start()
     core = core_ref[0]
+    packed, width = own_ref.shape
     half = block_ref.shape[0] * block_ref.shape[2]
-    own = block_ref[:, core].reshape(half, block_ref.shape[3])
-    sib = block_ref[:, 1 - core].reshape(half, block_ref.shape[3])
-    sums = dot(own, own_ref[...], 1, 1) + dot(sib, sib_ref[...], 1, 1)
-    out_ref[...] = sums.astype(BF16).reshape(out_ref.shape)
-
-
-def activations_kernel(core_ref, gate_up_ref, back_ref, out_ref, hidden_ref):
-    columns = back_ref.shape[2]
-    gate_up = jnp.sum(gate_up_ref[...].astype(F32), axis=0)
-    gate_sum = gate_up[:, :columns]
-    up_sum = gate_up[:, columns:]
-    grad_hidden = jnp.sum(back_ref[...].astype(F32), axis=0)
+    own = block_ref[:, core].reshape(half, 2 * width)
+    sib = block_ref[:, 1 - core].reshape(half, 2 * width)
+    ny, rows, _ = out_ref.shape
+    sums = dot(own[:, :width], own_ref[...], 1, 1) + dot(sib[:, :width], sib_ref[...], 1, 1)
+    out_ref[:, :, :packed] = sums.astype(BF16).reshape(ny, rows, packed)
+    own_copy.wait()
+    sib_copy.wait()
+    back = dot(own[:, width:], own_down_ref[...], 1, 1) + dot(
+        sib[:, width:], sib_down_ref[...], 1, 1
+    )
+    out_ref[:, :, packed:] = back.astype(BF16).reshape(ny, rows, packed // 2)
+
+
+def activations_kernel(core_ref, parts_ref, out_ref, hidden_ref):
+    columns = hidden_ref.shape[1]
+    sums = jnp.sum(parts_ref[...].astype(F32), axis=0)
+    gate_sum = sums[:, :columns]
+    up_sum = sums[:, columns : 2 * columns]
+    grad_hidden = sums[:, 2 * columns :]
     sigmoid_gate = jax.nn.sigmoid(gate_sum)
     activated = gate_sum * sigmoid_gate
     grad_gate_act = grad_hidden * up_sum * sigmoid_gate * (1.0 + gate_sum * (1.0 - sigmoid_gate))
@@ -62,13 +93,15 @@
 
 
 def share_kernel(core_ref, pieces_ref, weight_ref, out_ref):
-    pieces = pieces_ref[...].reshape(out_ref.shape[0], weight_ref.shape[0])
+    packed = pieces_ref.shape[2]
+    pieces = pieces_ref[...].reshape(out_ref.shape[0], packed)
     out_ref[...] = dot(pieces, weight_ref[...], 1, 0).astype(BF16)
 
 
 def shares_kernel(core_ref, mine_ref, pieces_ref, weight_ref, out_ref):
     half = mine_ref.shape[0]
-    pieces = pieces_ref[...].reshape(half, weight_ref.shape[0])
+    packed = pieces_ref.shape[2]
+    pieces = pieces_ref[...].reshape(half, packed)
     theirs = dot(pieces, weight_ref[...], 1, 0).astype(BF16)
     out_ref[pl.ds(pl.multiple_of(core_ref[0] * half, half), half), :] = mine_ref[...]
     out_ref[pl.ds(pl.multiple_of((1 - core_ref[0]) * half, half), half), :] = theirs
@@ -79,10 +112,8 @@
     own_ref,
     other_ref,
     hidden_ref,
-    own_inputs_ref,
-    other_inputs_ref,
-    own_cotangent_ref,
-    other_cotangent_ref,
+    own_block_ref,
+    other_block_ref,
     gate_ref,
     up_ref,
     down_ref,
@@ -94,10 +125,10 @@
     other = other_ref[...].reshape(half, 2 * columns)
     own_hidden = hidden_ref[:, core].reshape(half, columns)
     other_hidden = hidden_ref[:, 1 - core].reshape(half, columns)
-    own_inputs = own_inputs_ref[:, core].reshape(half, width)
-    other_inputs = other_inputs_ref[...].reshape(half, width)
-    own_cotangent = own_cotangent_ref[:, core].reshape(half, width)
-    other_cotangent = other_cotangent_ref[...].reshape(half, width)
+    own_block = own_block_ref[:, core].reshape(half, 2 * width)
+    own_inputs, own_cotangent = own_block[:, :width], own_block[:, width:]
+    other_block = other_block_ref[...].reshape(half, 2 * width)
+    other_inputs, other_cotangent = other_block[:, :width], other_block[:, width:]
     packed = dot(own, own_inputs, 0, 0) + dot(other, other_inputs, 0, 0)
     gate_ref[...] = packed[:columns].astype(BF16)
     up_ref[...] = packed[columns:].astype(BF16)
@@ -131,28 +162,19 @@
         w_gate, w_up, w_down = (after(w, along_z) for w in (w_gate, w_up, w_down))
         own_gate_up = jnp.concatenate([w_gate.T, w_up.T], axis=0)
         sib_gate_up, sib_down = sibling(own_gate_up), sibling(w_down)
-        def sums(block, own, sib):
-            return local(
-                sums_kernel,
-                jax.ShapeDtypeStruct((ny, share_rows, own.shape[0]), BF16),
-                4 * half * width * own.shape[0],
-                4 * (half + own.shape[0]) * width + 2 * half * own.shape[0],
-                core,
-                block,
-                own,
-                sib,
-            )
-
-        def of_other_tokens(block, earlier):
-            return sibling(lax.dynamic_index_in_dim(after(block, earlier), 1 - core, 1, False))
-
-        all_inputs = lax.all_gather(kept[:, :, :width], "x")
-        gate_up = sums(all_inputs, own_gate_up, sib_gate_up)
-        all_cotangent = lax.all_gather(after(kept[:, :, width:], gate_up), "x")
-        other_inputs = of_other_tokens(all_inputs, gate_up)
-        gate_up = lax.all_to_all(gate_up, "y", 0, 0)
-        back = sums(after(all_cotangent, gate_up, other_inputs), w_down, sib_down)
-        back = lax.all_to_all(back, "y", 0, 0)
+        block = lax.all_to_all(jnp.broadcast_to(kept[None], (nx, *kept.shape)), "x", 0, 0)
+        sums = local(
+            sums_kernel,
+            jax.ShapeDtypeStruct((ny, share_rows, 3 * columns), BF16),
+            12 * half * width * columns,
+            8 * half * width + 12 * columns * width + 6 * half * columns,
+            core,
+            block,
+            own_gate_up,
+            sib_gate_up,
+            fetched=(w_down, sib_down),
+        )
+        sums = lax.all_to_all(sums, "y", 0, 0)
         pieces, hidden = local(
             activations_kernel,
             (
@@ -162,8 +184,7 @@
             20 * share_rows * columns,
             10 * half * columns,
             core,
-            gate_up,
-            back,
+            sums,
         )
         pieces = lax.all_to_all(pieces, "y", 0, 0)
 
@@ -213,10 +234,8 @@
             lax.all_gather(after(hidden, shares), ("y", "c"), axis=0, tiled=True).reshape(
                 ny, nc, share_rows, columns
             ),
-            all_inputs,
-            other_inputs,
-            all_cotangent,
-            of_other_tokens(all_cotangent, shares),
+            block,
+            sibling(lax.dynamic_index_in_dim(after(block, shares), 1 - core, 1, False)),
         )
         return grad_inputs, grad_gate.T, grad_up.T, grad_down
 

time: 150 us -> 148 us (0.987)
  waiting for transfers between devices: 2.08 us -> 17.4 us
  starting transfers between devices: 29.3 us -> 20.9 us
  blocking collectives: 106 us -> 98.2 us
  Pallas kernels: 9.01 us -> 7.2 us
    all_gather x2 -> x0, blocking collectives: 24.5 us -> none  [the longest x1 12.6 us: on_device(): all_cotangent = lax.all_gather(after(kept[:, :, width:], gate_up), 'x')]
    all_to_all x1, blocking collectives: 18.4 us -> 33.6 us  [on_device(): sums = lax.all_to_all(sums, 'y', 0, 0)]
    all_to_all x1, waiting for transfers between devices: 0.01 us -> 13.3 us  [on_device(): lax.all_to_all(jnp.broadcast_to(kept[None], (nx, *kept.shape)), 'x', 0, 0)]
    ppermute x5 -> x4, starting transfers between devices: 17.9 us -> 12.8 us  [sibling(): return lax.ppermute(value, 'c', SWAP)]
    all_to_all x1, starting transfers between devices: 6.82 us -> 4.14 us  [on_device(): lax.all_to_all(jnp.broadcast_to(kept[None], (nx, *kept.shape)), 'x', 0, 0)]
    pallas_call x7 -> x6, Pallas kernels: 9.01 us -> 7.2 us  [local(): pl.pallas_call(kernel, out_shape=out_shape, in_specs=[pl.BlockSpec(memory...]
    ppermute x5 -> x4, waiting for transfers between devices: 1.18 us -> 2.9 us  [sibling(): return lax.ppermute(value, 'c', SWAP)]
  transfers between devices with their start and end apart: 7 -> 6, of which waited for: 2 -> 4; matrix products, arithmetic and copies ran while one was open for 0% -> 0% of each run, Pallas kernels for 2% -> 2%
where the time goes in v5:
time: 148 us; the launch traced here: 147 us
  blocking collectives  98.2 us (66%)
  starting transfers between devices  20.9 us (14%)
  waiting for transfers between devices  17.4 us (12%)
  Pallas kernels  7.2 us (5%)
  local copies, waits for them, and re-layouts  2.26 us (2%)
    all_to_all x1, blocking collectives, on_device(): sums = lax.all_to_all(sums, 'y', 0, 0)  33.6 us
    all_gather x1, blocking collectives, on_device(): along_z = lax.all_gather(both, ('h', 'l', 'c'), axis=0, tiled=True)  26.6 us
    all_to_all x1, blocking collectives, on_device(): pieces = lax.all_to_all(pieces, 'y', 0, 0)  21.1 us
    all_gather x1, blocking collectives, on_device(): lax.all_gather(after(hidden, shares), ('y', 'c'), axis=0, tiled=True)  16.8 us
    all_to_all x1, waiting for transfers between devices, on_device(): lax.all_to_all(jnp.broadcast_to(kept[None], (nx, *kept.shape)), 'x', 0, 0)  13.3 us
    ppermute x4, starting transfers between devices, sibling(): return lax.ppermute(value, 'c', SWAP)  12.8 us
    pallas_call x6, Pallas kernels, local(): pl.pallas_call(kernel, out_shape=out_shape, in_specs=[pl.BlockSpec(memory...  7.2 us
    all_to_all x1, starting transfers between devices, on_device(): lax.all_to_all(jnp.broadcast_to(kept[None], (nx, *kept.shape)), 'x', 0, 0)  4.14 us
  transfers between devices with their start and end apart: 6, of which 4 were waited for; matrix products, arithmetic and copies ran while one was open for 0% of the time, Pallas kernels for 2%

profile of v5, /device:TPU:1, one launch (start us, length us, event | category | flops | bytes accessed | tf_op | source)
XLA Modules:
  0.0 147.4 jit_solution(16370316821305251579)
XLA Ops:
  0.6 0.8 pad_maximum_fusion.1
  1.4 26.6 %all_gather.6 = bf16[384,1024]{1,0:T(8,128)(2,1)S(1)} all-gather(bf16[24,1024]{1,0:T(8,128)(2,1)S(1)} %pad_maximum_fusion.1), channel_id=1, replica_groups=mesh['y'=8,'c'=2,'h'=2,'l'=4,'x'=4] {'h','l','c'}, dimensions={0}, use_global_device_ids=true | all-gather | bytes 835584 | tf_op jit(solution)/shard_map/all_gather | solution.py:157
  28.1 1.4 broadcast_in_dim.8
  29.5 4.1 %all-to-all-start = ((bf16[4,2,96,1024]{3,2,1,0:T(8,128)(2,1)}), bf16[4,2,96,1024]{3,2,1,0:T(8,128)(2,1)S(1)}, u32[]{:S(2)}, u32[]{:S(2)}) async-start(bf16[4,2,96,1024]{3,2,1,0:T(8,128)(2,1)} %broadcast_in_dim.8), calls=%async_computation | async-start | bytes 3145728 | tf_op jit(solution)/shard_map/all_to_all | solution.py:165
  33.6 0.1 pad_maximum_fusion.own_ref.weight_ref
  33.7 2.5 %collective-permute-start = (bf16[896,512]{1,0:T(8,128)(2,1)S(1)}, bf16[896,512]{1,0:T(8,128)(2,1)S(1)}, u32[]{:S(2)}, u32[]{:S(2)}) collective-permute-start(bf16[896,512]{1,0:T(8,128)(2,1)S(1)} %pad_maximum_fusion.own_ref.weight_ref), channel_id=1, source_target_pairs={{0,32},{32,0},{1,33},{33,1},{2,34},{34,2},{3,35},{35,3},{4,36},{36... | collective-permute-start | bytes 2752520 | tf_op jit(solution)/shard_map/ppermute | solution.py:20
  36.2 2.0 %collective-permute-start.1 = (bf16[448,512]{1,0:T(8,128)(2,1)S(1)}, bf16[448,512]{1,0:T(8,128)(2,1)S(1)}, u32[]{:S(2)}, u32[]{:S(2)}) collective-permute-start(bf16[448,512]{1,0:T(8,128)(2,1)S(1)} %copy-done.4), channel_id=1, source_target_pairs={{0,32},{32,0},{1,33},{33,1},{2,34},{34,2},{3,35},{35,3},{4,36},{36... | collective-permute-start | bytes 1376264 | tf_op jit(solution)/shard_map/ppermute | solution.py:20
  38.2 1.7 %collective-permute-done.1.sib_down_hbm = bf16[448,512]{1,0:T(8,128)(2,1)S(1)} collective-permute-done((bf16[448,512]{1,0:T(8,128)(2,1)S(1)}, bf16[448,512]{1,0:T(8,128)(2,1)S(1)}, u32[]{:S(2)}, u32[]{:S(2)}) %collective-permute-start.1) | collective-permute-done | bytes 458784 | tf_op jit(solution)/shard_map/ppermute | solution.py:20
  39.9 0.8 copy-done.5
  40.7 13.3 %all-to-all-done.block_ref.own_block_ref = bf16[4,2,96,1024]{3,2,1,0:T(8,128)(2,1)S(1)} async-done(((bf16[4,2,96,1024]{3,2,1,0:T(8,128)(2,1)}), bf16[4,2,96,1024]{3,2,1,0:T(8,128)(2,1)S(1)}, u32[]{:S(2)}, u32[]{:S(2)}) %all-to-all-start) | async-done | bytes 1572896 | tf_op jit(solution)/shard_map/all_to_all | solution.py:165
  54.0 1.8 %shard_map.84 = bf16[8,48,1344]{2,1,0:T(8,128)(2,1)S(1)} custom-call(s32[1]{0:T(128)} %bitcast.core_ref, bf16[4,2,96,1024]{3,2,1,0:T(8,128)(2,1)S(1)} %all-to-all-done.block_ref.own_block_ref, bf16[896,512]{1,0:T(8,128)(2,1)S(1)} %pad_maximum_fusion.own_ref.weight_ref, bf16[896,512]{1,0:T(8,128)(2,1)S(1)} %collective-permute-done.sib_ref, ...), custom_call_target="tpu_custom_call" | custom-call | flops 1056964608 | bytes 5357568 | tf_op jit(solution)/shard_map/pallas_call | solution.py:32
  55.8 33.6 %all_to_all.20.parts_ref = bf16[8,48,1344]{2,1,0:T(8,128)(2,1)S(1)} all-to-all(bf16[8,48,1344]{2,1,0:T(8,128)(2,1)S(1)} %shard_map.84), channel_id=1, replica_groups=mesh['y'=8,'c'=2,'h'=2,'l'=4,'x'=4] {'y'}, dimensions={0} | all-to-all | bytes 2064384 | tf_op jit(solution)/shard_map/all_to_all | solution.py:177
  89.4 0.3 shard_map.85
  89.7 21.1 %all_to_all.21.pieces_ref.own_ref = bf16[8,48,896]{2,1,0:T(8,128)(2,1)S(1)} all-to-all(bf16[8,48,896]{2,1,0:T(8,128)(2,1)S(1)} %get-tuple-element.17), channel_id=1, replica_groups=mesh['y'=8,'c'=2,'h'=2,'l'=4,'x'=4] {'y'}, dimensions={0} | all-to-all | bytes 1376256 | tf_op jit(solution)/shard_map/all_to_all | solution.py:189
  110.7 5.9 %collective-permute-start.2 = (bf16[8,48,896]{2,1,0:T(8,128)(2,1)S(1)}, bf16[8,48,896]{2,1,0:T(8,128)(2,1)S(1)}, u32[]{:S(2)}, u32[]{:S(2)}) collective-permute-start(bf16[8,48,896]{2,1,0:T(8,128)(2,1)S(1)} %all_to_all.21.pieces_ref.own_ref), channel_id=1, source_target_pairs={{0,32},{32,0},{1,33},{33,1},{2,34},{34,2},{3,35},{35,3},{4,36},{36... | collective-permute-start | bytes 2064392 | tf_op jit(solution)/shard_map/ppermute | solution.py:20
  116.7 0.6 shard_map.86.mine_ref
  117.3 1.2 collective-permute-done.2.pieces_ref.other_ref
  118.4 1.5 %shard_map.87 = bf16[768,512]{1,0:T(8,128)(2,1)} custom-call(s32[1]{0:T(128)} %bitcast.core_ref, bf16[384,512]{1,0:T(8,128)(2,1)S(1)} %shard_map.86.mine_ref, bf16[8,48,896]{2,1,0:T(8,128)(2,1)S(1)} %collective-permute-done.2.pieces_ref.other_ref, bf16[896,512]{1,0:T(8,128)(2,1)S(1)} %pad_maximum_fusion.own_ref.weight_ref), custom_call_target="tpu_custom_call" | custom-call | flops 352321536 | bytes 2785280 | tf_op jit(solution)/shard_map/pallas_call | solution.py:32
  119.9 3.9 %all-to-all-start.3 = ((bf16[32,24,512]{2,1,0:T(8,128)(2,1)}), bf16[32,24,512]{2,1,0:T(8,128)(2,1)S(1)}, u32[]{:S(2)}, u32[]{:S(2)}) async-start(bf16[32,24,512]{2,1,0:T(8,128)(2,1)} %bitcast.16), calls=%async_computation.3 | async-start | bytes 1572864 | tf_op jit(solution)/shard_map/all_to_all | solution.py:213
  123.9 2.4 %collective-permute-start.3 = (bf16[4,96,1024]{2,1,0:T(8,128)(2,1)S(1)}, bf16[4,96,1024]{2,1,0:T(8,128)(2,1)S(1)}, u32[]{:S(2)}, u32[]{:S(2)}) collective-permute-start(bf16[4,96,1024]{2,1,0:T(8,128)(2,1)S(1)} %dynamic-slice_bitcast_fusion), channel_id=1, source_target_pairs={{0,32},{32,0},{1,33},{33,1},{2,34},{34,2},{3,35},{35,3},{4,36},{36... | collective-permute-start | bytes 2359304 | tf_op jit(solution)/shard_map/ppermute | solution.py:20
  126.3 16.8 %all_gather.7 = bf16[768,448]{1,0:T(8,128)(2,1)S(1)} all-gather(bf16[48,448]{1,0:T(8,128)(2,1)S(1)} %get-tuple-element.19), channel_id=1, replica_groups=mesh['y'=8,'c'=2,'h'=2,'l'=4,'x'=4] {'y','c'}, dimensions={0}, use_global_device_ids=true | all-gather | bytes 731136 | tf_op jit(solution)/shard_map/all_gather | solution.py:234
  143.2 2.4 %shard_map.89 = (bf16[448,512]{1,0:T(8,128)(2,1)}, bf16[448,512]{1,0:T(8,128)(2,1)}, bf16[448,512]{1,0:T(8,128)(2,1)}) custom-call(s32[1]{0:T(128)} %bitcast.core_ref, bf16[8,48,896]{2,1,0:T(8,128)(2,1)S(1)} %all_to_all.21.pieces_ref.own_ref, bf16[8,48,896]{2,1,0:T(8,128)(2,1)S(1)} %copy-done.1, bf16[8,2,48,448]{3,2,1,0:T(8,128)(2,1)S(1)} %bitcast.15, ...), custom_call_target="tpu_custom_call" | custom-call | flops 1056964608 | bytes 5013504 | tf_op jit(solution)/shard_map/pallas_call | solution.py:32
  145.6 1.1 all-to-all-done.3.parts_ref
  146.7 0.7 shard_map.88
  (16 shorter events, 0.1 us)
Async XLA Ops:
  29.5 4.2 %copy-start.2 = (bf16[512,448]{0,1:T(8,128)(2,1)S(1)}, bf16[512,448]{0,1:T(8,128)(2,1)}, u32[]{:S(2)}) copy-start(bf16[512,448]{0,1:T(8,128)(2,1)} %param.7) | copy-start | bytes 1376260
  29.5 4.2 %copy-start.3 = (bf16[512,448]{0,1:T(8,128)(2,1)S(1)}, bf16[512,448]{0,1:T(8,128)(2,1)}, u32[]{:S(2)}) copy-start(bf16[512,448]{0,1:T(8,128)(2,1)} %param.6) | copy-start | bytes 1376260
  29.5 24.5 %all-to-all-start = ((bf16[4,2,96,1024]{3,2,1,0:T(8,128)(2,1)}), bf16[4,2,96,1024]{3,2,1,0:T(8,128)(2,1)S(1)}, u32[]{:S(2)}, u32[]{:S(2)}) async-start(bf16[4,2,96,1024]{3,2,1,0:T(8,128)(2,1)} %broadcast_in_dim.8), calls=%async_computation | async-start | bytes 3145728 | tf_op jit(solution)/shard_map/all_to_all | solution.py:165
  33.6 2.6 %copy-start.4 = (bf16[448,512]{1,0:T(8,128)(2,1)S(1)}, bf16[448,512]{1,0:T(8,128)(2,1)}, u32[]{:S(2)}) copy-start(bf16[448,512]{1,0:T(8,128)(2,1)} %own_down_hbm) | copy-start | bytes 1376260
  33.7 7.0 %collective-permute-start = (bf16[896,512]{1,0:T(8,128)(2,1)S(1)}, bf16[896,512]{1,0:T(8,128)(2,1)S(1)}, u32[]{:S(2)}, u32[]{:S(2)}) collective-permute-start(bf16[896,512]{1,0:T(8,128)(2,1)S(1)} %pad_maximum_fusion.own_ref.weight_ref), channel_id=1, source_target_pairs={{0,32},{32,0},{1,33},{33,1},{2,34},{34,2},{3,35},{35,3},{4,36},{36... | collective-permute-start | bytes 2752520 | tf_op jit(solution)/shard_map/ppermute | solution.py:20
  36.2 3.7 %collective-permute-start.1 = (bf16[448,512]{1,0:T(8,128)(2,1)S(1)}, bf16[448,512]{1,0:T(8,128)(2,1)S(1)}, u32[]{:S(2)}, u32[]{:S(2)}) collective-permute-start(bf16[448,512]{1,0:T(8,128)(2,1)S(1)} %copy-done.4), channel_id=1, source_target_pairs={{0,32},{32,0},{1,33},{33,1},{2,34},{34,2},{3,35},{35,3},{4,36},{36... | collective-permute-start | bytes 1376264 | tf_op jit(solution)/shard_map/ppermute | solution.py:20
  39.9 0.8 copy-start.5
  110.7 7.7 %collective-permute-start.2 = (bf16[8,48,896]{2,1,0:T(8,128)(2,1)S(1)}, bf16[8,48,896]{2,1,0:T(8,128)(2,1)S(1)}, u32[]{:S(2)}, u32[]{:S(2)}) collective-permute-start(bf16[8,48,896]{2,1,0:T(8,128)(2,1)S(1)} %all_to_all.21.pieces_ref.own_ref), channel_id=1, source_target_pairs={{0,32},{32,0},{1,33},{33,1},{2,34},{34,2},{3,35},{35,3},{4,36},{36... | collective-permute-start | bytes 2064392 | tf_op jit(solution)/shard_map/ppermute | solution.py:20
  118.4 1.5 %copy-start = (bf16[8,48,896]{2,1,0:T(8,128)(2,1)}, bf16[8,48,896]{2,1,0:T(8,128)(2,1)S(1)}, u32[]{:S(2)}) copy-start(bf16[8,48,896]{2,1,0:T(8,128)(2,1)S(1)} %collective-permute-done.2.pieces_ref.other_ref) | copy-start | bytes 2064388
  119.9 26.8 %all-to-all-start.3 = ((bf16[32,24,512]{2,1,0:T(8,128)(2,1)}), bf16[32,24,512]{2,1,0:T(8,128)(2,1)S(1)}, u32[]{:S(2)}, u32[]{:S(2)}) async-start(bf16[32,24,512]{2,1,0:T(8,128)(2,1)} %bitcast.16), calls=%async_computation.3 | async-start | bytes 1572864 | tf_op jit(solution)/shard_map/all_to_all | solution.py:213
  123.8 19.3 %copy-start.1 = (bf16[8,48,896]{2,1,0:T(8,128)(2,1)S(1)}, bf16[8,48,896]{2,1,0:T(8,128)(2,1)}, u32[]{:S(2)}) copy-start(bf16[8,48,896]{2,1,0:T(8,128)(2,1)} %copy-done) | copy-start | bytes 2064388
  123.9 19.3 %collective-permute-start.3 = (bf16[4,96,1024]{2,1,0:T(8,128)(2,1)S(1)}, bf16[4,96,1024]{2,1,0:T(8,128)(2,1)S(1)}, u32[]{:S(2)}, u32[]{:S(2)}) collective-permute-start(bf16[4,96,1024]{2,1,0:T(8,128)(2,1)S(1)} %dynamic-slice_bitcast_fusion), channel_id=1, source_target_pairs={{0,32},{32,0},{1,33},{33,1},{2,34},{34,2},{3,35},{35,3},{4,36},{36... | collective-permute-start | bytes 2359304 | tf_op jit(solution)/shard_map/ppermute | solution.py:20

commit v6 on v5

--- a/solution.py
+++ b/solution.py
@@ -66,22 +66,29 @@
     own = block_ref[:, core].reshape(half, 2 * width)
     sib = block_ref[:, 1 - core].reshape(half, 2 * width)
     ny, rows, _ = out_ref.shape
-    sums = dot(own[:, :width], own_ref[...], 1, 1) + dot(sib[:, :width], sib_ref[...], 1, 1)
-    out_ref[:, :, :packed] = sums.astype(BF16).reshape(ny, rows, packed)
+
+    def store(sums, start):
+        count = sums.shape[1]
+        pairs = sums.reshape(ny, 2 * rows, count)
+        out_ref[:, :, start : start + count] = pairs[:, :rows].astype(BF16)
+        out_ref[:, :, start + count : start + 2 * count] = pairs[:, rows:].astype(BF16)
+
+    store(dot(own[:, :width], own_ref[...], 1, 1) + dot(sib[:, :width], sib_ref[...], 1, 1), 0)
     own_copy.wait()
     sib_copy.wait()
-    back = dot(own[:, width:], own_down_ref[...], 1, 1) + dot(
-        sib[:, width:], sib_down_ref[...], 1, 1
-    )
-    out_ref[:, :, packed:] = back.astype(BF16).reshape(ny, rows, packed // 2)
+    back = dot(own[:, width:], own_down_ref[...], 1, 1)
+    store(back + dot(sib[:, width:], sib_down_ref[...], 1, 1), 2 * packed)
 
 
 def activations_kernel(core_ref, parts_ref, out_ref, hidden_ref):
     columns = hidden_ref.shape[1]
     sums = jnp.sum(parts_ref[...].astype(F32), axis=0)
-    gate_sum = sums[:, :columns]
-    up_sum = sums[:, columns : 2 * columns]
-    grad_hidden = sums[:, 2 * columns :]
+    gate_up = jnp.concatenate([sums[:, : 2 * columns], sums[:, 2 * columns : 4 * columns]], axis=0)
+    gate_sum = gate_up[:, :columns]
+    up_sum = gate_up[:, columns:]
+    grad_hidden = jnp.concatenate(
+        [sums[:, 4 * columns : 5 * columns], sums[:, 5 * columns :]], axis=0
+    )
     sigmoid_gate = jax.nn.sigmoid(gate_sum)
     activated = gate_sum * sigmoid_gate
     grad_gate_act = grad_hidden * up_sum * sigmoid_gate * (1.0 + gate_sum * (1.0 - sigmoid_gate))
@@ -165,7 +172,7 @@
         block = lax.all_to_all(jnp.broadcast_to(kept[None], (nx, *kept.shape)), "x", 0, 0)
         sums = local(
             sums_kernel,
-            jax.ShapeDtypeStruct((ny, share_rows, 3 * columns), BF16),
+            jax.ShapeDtypeStruct((ny, share_rows // 2, 6 * columns), BF16),
             12 * half * width * columns,
             8 * half * width + 12 * columns * width + 6 * half * columns,
             core,

time: 148 us -> 147 us (level)
  no operation moved by 1% of the time
where the time goes in v6:
time: 147 us; the launch traced here: 146 us
  blocking collectives  97 us (66%)
  starting transfers between devices  20.9 us (14%)
  waiting for transfers between devices  17.3 us (12%)
  Pallas kernels  7.27 us (5%)
  local copies, waits for them, and re-layouts  2.26 us (2%)
    all_to_all x1, blocking collectives, on_device(): sums = lax.all_to_all(sums, 'y', 0, 0)  32.8 us
    all_gather x1, blocking collectives, on_device(): along_z = lax.all_gather(both, ('h', 'l', 'c'), axis=0, tiled=True)  26.6 us
    all_to_all x1, blocking collectives, on_device(): pieces = lax.all_to_all(pieces, 'y', 0, 0)  20.8 us
    all_gather x1, blocking collectives, on_device(): lax.all_gather(after(hidden, shares), ('y', 'c'), axis=0, tiled=True)  16.8 us
    all_to_all x1, waiting for transfers between devices, on_device(): lax.all_to_all(jnp.broadcast_to(kept[None], (nx, *kept.shape)), 'x', 0, 0)  13.3 us
    ppermute x4, starting transfers between devices, sibling(): return lax.ppermute(value, 'c', SWAP)  12.8 us
    pallas_call x6, Pallas kernels, local(): pl.pallas_call(kernel, out_shape=out_shape, in_specs=[pl.BlockSpec(memory...  7.27 us
    all_to_all x1, starting transfers between devices, on_device(): lax.all_to_all(jnp.broadcast_to(kept[None], (nx, *kept.shape)), 'x', 0, 0)  4.14 us
  transfers between devices with their start and end apart: 6, of which 4 were waited for; matrix products, arithmetic and copies ran while one was open for 0% of the time, Pallas kernels for 2%

profile of v6, /device:TPU:1, one launch (start us, length us, event | category | flops | bytes accessed | tf_op | source)
XLA Modules:
  0.0 146.4 jit_solution(10644822209628102373)
XLA Ops:
  0.6 0.8 pad_maximum_fusion.1
  1.4 26.6 %all_gather.6 = bf16[384,1024]{1,0:T(8,128)(2,1)S(1)} all-gather(bf16[24,1024]{1,0:T(8,128)(2,1)S(1)} %pad_maximum_fusion.1), channel_id=1, replica_groups=mesh['y'=8,'c'=2,'h'=2,'l'=4,'x'=4] {'h','l','c'}, dimensions={0}, use_global_device_ids=true | all-gather | bytes 835584 | tf_op jit(solution)/shard_map/all_gather | solution.py:164
  28.1 1.4 broadcast_in_dim.8
  29.5 4.1 %all-to-all-start = ((bf16[4,2,96,1024]{3,2,1,0:T(8,128)(2,1)}), bf16[4,2,96,1024]{3,2,1,0:T(8,128)(2,1)S(1)}, u32[]{:S(2)}, u32[]{:S(2)}) async-start(bf16[4,2,96,1024]{3,2,1,0:T(8,128)(2,1)} %broadcast_in_dim.8), calls=%async_computation | async-start | bytes 3145728 | tf_op jit(solution)/shard_map/all_to_all | solution.py:172
  33.6 0.1 pad_maximum_fusion.own_ref.weight_ref
  33.7 2.5 %collective-permute-start = (bf16[896,512]{1,0:T(8,128)(2,1)S(1)}, bf16[896,512]{1,0:T(8,128)(2,1)S(1)}, u32[]{:S(2)}, u32[]{:S(2)}) collective-permute-start(bf16[896,512]{1,0:T(8,128)(2,1)S(1)} %pad_maximum_fusion.own_ref.weight_ref), channel_id=1, source_target_pairs={{0,32},{32,0},{1,33},{33,1},{2,34},{34,2},{3,35},{35,3},{4,36},{36... | collective-permute-start | bytes 2752520 | tf_op jit(solution)/shard_map/ppermute | solution.py:20
  36.2 2.0 %collective-permute-start.1 = (bf16[448,512]{1,0:T(8,128)(2,1)S(1)}, bf16[448,512]{1,0:T(8,128)(2,1)S(1)}, u32[]{:S(2)}, u32[]{:S(2)}) collective-permute-start(bf16[448,512]{1,0:T(8,128)(2,1)S(1)} %copy-done.4), channel_id=1, source_target_pairs={{0,32},{32,0},{1,33},{33,1},{2,34},{34,2},{3,35},{35,3},{4,36},{36... | collective-permute-start | bytes 1376264 | tf_op jit(solution)/shard_map/ppermute | solution.py:20
  38.2 1.7 %collective-permute-done.1.sib_down_hbm = bf16[448,512]{1,0:T(8,128)(2,1)S(1)} collective-permute-done((bf16[448,512]{1,0:T(8,128)(2,1)S(1)}, bf16[448,512]{1,0:T(8,128)(2,1)S(1)}, u32[]{:S(2)}, u32[]{:S(2)}) %collective-permute-start.1) | collective-permute-done | bytes 458784 | tf_op jit(solution)/shard_map/ppermute | solution.py:20
  39.9 0.8 copy-done.5
  40.7 13.3 %all-to-all-done.block_ref.own_block_ref = bf16[4,2,96,1024]{3,2,1,0:T(8,128)(2,1)S(1)} async-done(((bf16[4,2,96,1024]{3,2,1,0:T(8,128)(2,1)}), bf16[4,2,96,1024]{3,2,1,0:T(8,128)(2,1)S(1)}, u32[]{:S(2)}, u32[]{:S(2)}) %all-to-all-start) | async-done | bytes 1572896 | tf_op jit(solution)/shard_map/all_to_all | solution.py:172
  54.0 1.8 %shard_map.84 = bf16[8,24,2688]{2,1,0:T(8,128)(2,1)S(1)} custom-call(s32[1]{0:T(128)} %bitcast.core_ref, bf16[4,2,96,1024]{3,2,1,0:T(8,128)(2,1)S(1)} %all-to-all-done.block_ref.own_block_ref, bf16[896,512]{1,0:T(8,128)(2,1)S(1)} %pad_maximum_fusion.own_ref.weight_ref, bf16[896,512]{1,0:T(8,128)(2,1)S(1)} %collective-permute-done.sib_ref, ...), custom_call_target="tpu_custom_call" | custom-call | flops 1056964608 | bytes 5357568 | tf_op jit(solution)/shard_map/pallas_call | solution.py:32
  55.9 32.8 %all_to_all.20.parts_ref = bf16[8,24,2688]{2,1,0:T(8,128)(2,1)S(1)} all-to-all(bf16[8,24,2688]{2,1,0:T(8,128)(2,1)S(1)} %shard_map.84), channel_id=1, replica_groups=mesh['y'=8,'c'=2,'h'=2,'l'=4,'x'=4] {'y'}, dimensions={0} | all-to-all | bytes 2064384 | tf_op jit(solution)/shard_map/all_to_all | solution.py:184
  88.6 0.3 shard_map.85
  88.9 20.8 %all_to_all.21.pieces_ref.own_ref = bf16[8,48,896]{2,1,0:T(8,128)(2,1)S(1)} all-to-all(bf16[8,48,896]{2,1,0:T(8,128)(2,1)S(1)} %get-tuple-element.17), channel_id=1, replica_groups=mesh['y'=8,'c'=2,'h'=2,'l'=4,'x'=4] {'y'}, dimensions={0} | all-to-all | bytes 1376256 | tf_op jit(solution)/shard_map/all_to_all | solution.py:196
  109.7 6.0 %collective-permute-start.2 = (bf16[8,48,896]{2,1,0:T(8,128)(2,1)S(1)}, bf16[8,48,896]{2,1,0:T(8,128)(2,1)S(1)}, u32[]{:S(2)}, u32[]{:S(2)}) collective-permute-start(bf16[8,48,896]{2,1,0:T(8,128)(2,1)S(1)} %all_to_all.21.pieces_ref.own_ref), channel_id=1, source_target_pairs={{0,32},{32,0},{1,33},{33,1},{2,34},{34,2},{3,35},{35,3},{4,36},{36... | collective-permute-start | bytes 2064392 | tf_op jit(solution)/shard_map/ppermute | solution.py:20
  115.7 0.6 shard_map.86.mine_ref
  116.2 1.2 collective-permute-done.2.pieces_ref.other_ref
  117.4 1.5 %shard_map.87 = bf16[768,512]{1,0:T(8,128)(2,1)} custom-call(s32[1]{0:T(128)} %bitcast.core_ref, bf16[384,512]{1,0:T(8,128)(2,1)S(1)} %shard_map.86.mine_ref, bf16[8,48,896]{2,1,0:T(8,128)(2,1)S(1)} %collective-permute-done.2.pieces_ref.other_ref, bf16[896,512]{1,0:T(8,128)(2,1)S(1)} %pad_maximum_fusion.own_ref.weight_ref), custom_call_target="tpu_custom_call" | custom-call | flops 352321536 | bytes 2785280 | tf_op jit(solution)/shard_map/pallas_call | solution.py:32
  118.9 3.9 %all-to-all-start.3 = ((bf16[32,24,512]{2,1,0:T(8,128)(2,1)}), bf16[32,24,512]{2,1,0:T(8,128)(2,1)S(1)}, u32[]{:S(2)}, u32[]{:S(2)}) async-start(bf16[32,24,512]{2,1,0:T(8,128)(2,1)} %bitcast.16), calls=%async_computation.3 | async-start | bytes 1572864 | tf_op jit(solution)/shard_map/all_to_all | solution.py:220
  122.9 2.4 %collective-permute-start.3 = (bf16[4,96,1024]{2,1,0:T(8,128)(2,1)S(1)}, bf16[4,96,1024]{2,1,0:T(8,128)(2,1)S(1)}, u32[]{:S(2)}, u32[]{:S(2)}) collective-permute-start(bf16[4,96,1024]{2,1,0:T(8,128)(2,1)S(1)} %dynamic-slice_bitcast_fusion), channel_id=1, source_target_pairs={{0,32},{32,0},{1,33},{33,1},{2,34},{34,2},{3,35},{35,3},{4,36},{36... | collective-permute-start | bytes 2359304 | tf_op jit(solution)/shard_map/ppermute | solution.py:20
  125.3 16.8 %all_gather.7 = bf16[768,448]{1,0:T(8,128)(2,1)S(1)} all-gather(bf16[48,448]{1,0:T(8,128)(2,1)S(1)} %get-tuple-element.19), channel_id=1, replica_groups=mesh['y'=8,'c'=2,'h'=2,'l'=4,'x'=4] {'y','c'}, dimensions={0}, use_global_device_ids=true | all-gather | bytes 731136 | tf_op jit(solution)/shard_map/all_gather | solution.py:241
  142.2 2.4 %shard_map.89 = (bf16[448,512]{1,0:T(8,128)(2,1)}, bf16[448,512]{1,0:T(8,128)(2,1)}, bf16[448,512]{1,0:T(8,128)(2,1)}) custom-call(s32[1]{0:T(128)} %bitcast.core_ref, bf16[8,48,896]{2,1,0:T(8,128)(2,1)S(1)} %all_to_all.21.pieces_ref.own_ref, bf16[8,48,896]{2,1,0:T(8,128)(2,1)S(1)} %copy-done.1, bf16[8,2,48,448]{3,2,1,0:T(8,128)(2,1)S(1)} %bitcast.15, ...), custom_call_target="tpu_custom_call" | custom-call | flops 1056964608 | bytes 5013504 | tf_op jit(solution)/shard_map/pallas_call | solution.py:32
  144.6 1.1 all-to-all-done.3.parts_ref
  145.7 0.7 shard_map.88
  (16 shorter events, 0.1 us)
Async XLA Ops:
  29.5 4.2 %copy-start.2 = (bf16[512,448]{0,1:T(8,128)(2,1)S(1)}, bf16[512,448]{0,1:T(8,128)(2,1)}, u32[]{:S(2)}) copy-start(bf16[512,448]{0,1:T(8,128)(2,1)} %param.7) | copy-start | bytes 1376260
  29.5 4.2 %copy-start.3 = (bf16[512,448]{0,1:T(8,128)(2,1)S(1)}, bf16[512,448]{0,1:T(8,128)(2,1)}, u32[]{:S(2)}) copy-start(bf16[512,448]{0,1:T(8,128)(2,1)} %param.6) | copy-start | bytes 1376260
  29.5 24.5 %all-to-all-start = ((bf16[4,2,96,1024]{3,2,1,0:T(8,128)(2,1)}), bf16[4,2,96,1024]{3,2,1,0:T(8,128)(2,1)S(1)}, u32[]{:S(2)}, u32[]{:S(2)}) async-start(bf16[4,2,96,1024]{3,2,1,0:T(8,128)(2,1)} %broadcast_in_dim.8), calls=%async_computation | async-start | bytes 3145728 | tf_op jit(solution)/shard_map/all_to_all | solution.py:172
  33.6 2.6 %copy-start.4 = (bf16[448,512]{1,0:T(8,128)(2,1)S(1)}, bf16[448,512]{1,0:T(8,128)(2,1)}, u32[]{:S(2)}) copy-start(bf16[448,512]{1,0:T(8,128)(2,1)} %own_down_hbm) | copy-start | bytes 1376260
  33.7 7.0 %collective-permute-start = (bf16[896,512]{1,0:T(8,128)(2,1)S(1)}, bf16[896,512]{1,0:T(8,128)(2,1)S(1)}, u32[]{:S(2)}, u32[]{:S(2)}) collective-permute-start(bf16[896,512]{1,0:T(8,128)(2,1)S(1)} %pad_maximum_fusion.own_ref.weight_ref), channel_id=1, source_target_pairs={{0,32},{32,0},{1,33},{33,1},{2,34},{34,2},{3,35},{35,3},{4,36},{36... | collective-permute-start | bytes 2752520 | tf_op jit(solution)/shard_map/ppermute | solution.py:20
  36.2 3.7 %collective-permute-start.1 = (bf16[448,512]{1,0:T(8,128)(2,1)S(1)}, bf16[448,512]{1,0:T(8,128)(2,1)S(1)}, u32[]{:S(2)}, u32[]{:S(2)}) collective-permute-start(bf16[448,512]{1,0:T(8,128)(2,1)S(1)} %copy-done.4), channel_id=1, source_target_pairs={{0,32},{32,0},{1,33},{33,1},{2,34},{34,2},{3,35},{35,3},{4,36},{36... | collective-permute-start | bytes 1376264 | tf_op jit(solution)/shard_map/ppermute | solution.py:20
  39.9 0.8 copy-start.5
  109.7 7.7 %collective-permute-start.2 = (bf16[8,48,896]{2,1,0:T(8,128)(2,1)S(1)}, bf16[8,48,896]{2,1,0:T(8,128)(2,1)S(1)}, u32[]{:S(2)}, u32[]{:S(2)}) collective-permute-start(bf16[8,48,896]{2,1,0:T(8,128)(2,1)S(1)} %all_to_all.21.pieces_ref.own_ref), channel_id=1, source_target_pairs={{0,32},{32,0},{1,33},{33,1},{2,34},{34,2},{3,35},{35,3},{4,36},{36... | collective-permute-start | bytes 2064392 | tf_op jit(solution)/shard_map/ppermute | solution.py:20
  117.4 1.5 %copy-start = (bf16[8,48,896]{2,1,0:T(8,128)(2,1)}, bf16[8,48,896]{2,1,0:T(8,128)(2,1)S(1)}, u32[]{:S(2)}) copy-start(bf16[8,48,896]{2,1,0:T(8,128)(2,1)S(1)} %collective-permute-done.2.pieces_ref.other_ref) | copy-start | bytes 2064388
  118.9 26.8 %all-to-all-start.3 = ((bf16[32,24,512]{2,1,0:T(8,128)(2,1)}), bf16[32,24,512]{2,1,0:T(8,128)(2,1)S(1)}, u32[]{:S(2)}, u32[]{:S(2)}) async-start(bf16[32,24,512]{2,1,0:T(8,128)(2,1)} %bitcast.16), calls=%async_computation.3 | async-start | bytes 1572864 | tf_op jit(solution)/shard_map/all_to_all | solution.py:220
  122.8 19.3 %copy-start.1 = (bf16[8,48,896]{2,1,0:T(8,128)(2,1)S(1)}, bf16[8,48,896]{2,1,0:T(8,128)(2,1)}, u32[]{:S(2)}) copy-start(bf16[8,48,896]{2,1,0:T(8,128)(2,1)} %copy-done) | copy-start | bytes 2064388
  122.9 19.3 %collective-permute-start.3 = (bf16[4,96,1024]{2,1,0:T(8,128)(2,1)S(1)}, bf16[4,96,1024]{2,1,0:T(8,128)(2,1)S(1)}, u32[]{:S(2)}, u32[]{:S(2)}) collective-permute-start(bf16[4,96,1024]{2,1,0:T(8,128)(2,1)S(1)} %dynamic-slice_bitcast_fusion), channel_id=1, source_target_pairs={{0,32},{32,0},{1,33},{33,1},{2,34},{34,2},{3,35},{35,3},{4,36},{36... | collective-permute-start | bytes 2359304 | tf_op jit(solution)/shard_map/ppermute | solution.py:20

commit v7 on v6

--- a/solution.py
+++ b/solution.py
@@ -80,6 +80,11 @@
     store(back + dot(sib[:, width:], sib_down_ref[...], 1, 1), 2 * packed)
 
 
+def sigmoid(value):
+    small = jnp.exp(-jnp.abs(value))
+    return jnp.where(value >= 0.0, 1.0, small) / (1.0 + small)
+
+
 def activations_kernel(core_ref, parts_ref, out_ref, hidden_ref):
     columns = hidden_ref.shape[1]
     sums = jnp.sum(parts_ref[...].astype(F32), axis=0)
@@ -89,7 +94,7 @@
     grad_hidden = jnp.concatenate(
         [sums[:, 4 * columns : 5 * columns], sums[:, 5 * columns :]], axis=0
     )
-    sigmoid_gate = jax.nn.sigmoid(gate_sum)
+    sigmoid_gate = sigmoid(gate_sum)
     activated = gate_sum * sigmoid_gate
     grad_gate_act = grad_hidden * up_sum * sigmoid_gate * (1.0 + gate_sum * (1.0 - sigmoid_gate))
     out_ref[0, :, :columns] = grad_gate_act.astype(BF16)

time: 147 us -> 147 us (level)
  no operation moved by 1% of the time
where the time goes in v7:
time: 147 us; the launch traced here: 146 us
  blocking collectives  97 us (66%)
  starting transfers between devices  20.9 us (14%)
  waiting for transfers between devices  17.4 us (12%)
  Pallas kernels  7.28 us (5%)
  local copies, waits for them, and re-layouts  2.26 us (2%)
    all_to_all x1, blocking collectives, on_device(): sums = lax.all_to_all(sums, 'y', 0, 0)  32.8 us
    all_gather x1, blocking collectives, on_device(): along_z = lax.all_gather(both, ('h', 'l', 'c'), axis=0, tiled=True)  26.6 us
    all_to_all x1, blocking collectives, on_device(): pieces = lax.all_to_all(pieces, 'y', 0, 0)  20.8 us
    all_gather x1, blocking collectives, on_device(): lax.all_gather(after(hidden, shares), ('y', 'c'), axis=0, tiled=True)  16.8 us
    all_to_all x1, waiting for transfers between devices, on_device(): lax.all_to_all(jnp.broadcast_to(kept[None], (nx, *kept.shape)), 'x', 0, 0)  13.3 us
    ppermute x4, starting transfers between devices, sibling(): return lax.ppermute(value, 'c', SWAP)  12.8 us
    pallas_call x6, Pallas kernels, local(): pl.pallas_call(kernel, out_shape=out_shape, in_specs=[pl.BlockSpec(memory...  7.28 us
    all_to_all x1, starting transfers between devices, on_device(): lax.all_to_all(jnp.broadcast_to(kept[None], (nx, *kept.shape)), 'x', 0, 0)  4.14 us
  transfers between devices with their start and end apart: 6, of which 4 were waited for; matrix products, arithmetic and copies ran while one was open for 0% of the time, Pallas kernels for 2%

profile of v7, /device:TPU:1, one launch (start us, length us, event | category | flops | bytes accessed | tf_op | source)
XLA Modules:
  0.0 146.4 jit_solution(9836985584724355734)
XLA Ops:
  0.6 0.8 pad_maximum_fusion.1
  1.4 26.6 %all_gather.6 = bf16[384,1024]{1,0:T(8,128)(2,1)S(1)} all-gather(bf16[24,1024]{1,0:T(8,128)(2,1)S(1)} %pad_maximum_fusion.1), channel_id=1, replica_groups=mesh['y'=8,'c'=2,'h'=2,'l'=4,'x'=4] {'h','l','c'}, dimensions={0}, use_global_device_ids=true | all-gather | bytes 835584 | tf_op jit(solution)/shard_map/all_gather | solution.py:169
  28.1 1.4 broadcast_in_dim.8
  29.5 4.1 %all-to-all-start = ((bf16[4,2,96,1024]{3,2,1,0:T(8,128)(2,1)}), bf16[4,2,96,1024]{3,2,1,0:T(8,128)(2,1)S(1)}, u32[]{:S(2)}, u32[]{:S(2)}) async-start(bf16[4,2,96,1024]{3,2,1,0:T(8,128)(2,1)} %broadcast_in_dim.8), calls=%async_computation | async-start | bytes 3145728 | tf_op jit(solution)/shard_map/all_to_all | solution.py:177
  33.6 0.1 pad_maximum_fusion.own_ref.weight_ref
  33.7 2.5 %collective-permute-start = (bf16[896,512]{1,0:T(8,128)(2,1)S(1)}, bf16[896,512]{1,0:T(8,128)(2,1)S(1)}, u32[]{:S(2)}, u32[]{:S(2)}) collective-permute-start(bf16[896,512]{1,0:T(8,128)(2,1)S(1)} %pad_maximum_fusion.own_ref.weight_ref), channel_id=1, source_target_pairs={{0,32},{32,0},{1,33},{33,1},{2,34},{34,2},{3,35},{35,3},{4,36},{36... | collective-permute-start | bytes 2752520 | tf_op jit(solution)/shard_map/ppermute | solution.py:20
  36.2 2.0 %collective-permute-start.1 = (bf16[448,512]{1,0:T(8,128)(2,1)S(1)}, bf16[448,512]{1,0:T(8,128)(2,1)S(1)}, u32[]{:S(2)}, u32[]{:S(2)}) collective-permute-start(bf16[448,512]{1,0:T(8,128)(2,1)S(1)} %copy-done.4), channel_id=1, source_target_pairs={{0,32},{32,0},{1,33},{33,1},{2,34},{34,2},{3,35},{35,3},{4,36},{36... | collective-permute-start | bytes 1376264 | tf_op jit(solution)/shard_map/ppermute | solution.py:20
  38.2 1.7 %collective-permute-done.1.sib_down_hbm = bf16[448,512]{1,0:T(8,128)(2,1)S(1)} collective-permute-done((bf16[448,512]{1,0:T(8,128)(2,1)S(1)}, bf16[448,512]{1,0:T(8,128)(2,1)S(1)}, u32[]{:S(2)}, u32[]{:S(2)}) %collective-permute-start.1) | collective-permute-done | bytes 458784 | tf_op jit(solution)/shard_map/ppermute | solution.py:20
  39.9 0.8 copy-done.5
  40.7 13.3 %all-to-all-done.block_ref.own_block_ref = bf16[4,2,96,1024]{3,2,1,0:T(8,128)(2,1)S(1)} async-done(((bf16[4,2,96,1024]{3,2,1,0:T(8,128)(2,1)}), bf16[4,2,96,1024]{3,2,1,0:T(8,128)(2,1)S(1)}, u32[]{:S(2)}, u32[]{:S(2)}) %all-to-all-start) | async-done | bytes 1572896 | tf_op jit(solution)/shard_map/all_to_all | solution.py:177
  54.0 1.8 %shard_map.84 = bf16[8,24,2688]{2,1,0:T(8,128)(2,1)S(1)} custom-call(s32[1]{0:T(128)} %bitcast.core_ref, bf16[4,2,96,1024]{3,2,1,0:T(8,128)(2,1)S(1)} %all-to-all-done.block_ref.own_block_ref, bf16[896,512]{1,0:T(8,128)(2,1)S(1)} %pad_maximum_fusion.own_ref.weight_ref, bf16[896,512]{1,0:T(8,128)(2,1)S(1)} %collective-permute-done.sib_ref, ...), custom_call_target="tpu_custom_call" | custom-call | flops 1056964608 | bytes 5357568 | tf_op jit(solution)/shard_map/pallas_call | solution.py:32
  55.9 32.8 %all_to_all.20.parts_ref = bf16[8,24,2688]{2,1,0:T(8,128)(2,1)S(1)} all-to-all(bf16[8,24,2688]{2,1,0:T(8,128)(2,1)S(1)} %shard_map.84), channel_id=1, replica_groups=mesh['y'=8,'c'=2,'h'=2,'l'=4,'x'=4] {'y'}, dimensions={0} | all-to-all | bytes 2064384 | tf_op jit(solution)/shard_map/all_to_all | solution.py:189
  88.6 0.3 shard_map.85
  88.9 20.8 %all_to_all.21.pieces_ref.own_ref = bf16[8,48,896]{2,1,0:T(8,128)(2,1)S(1)} all-to-all(bf16[8,48,896]{2,1,0:T(8,128)(2,1)S(1)} %get-tuple-element.17), channel_id=1, replica_groups=mesh['y'=8,'c'=2,'h'=2,'l'=4,'x'=4] {'y'}, dimensions={0} | all-to-all | bytes 1376256 | tf_op jit(solution)/shard_map/all_to_all | solution.py:201
  109.7 6.0 %collective-permute-start.2 = (bf16[8,48,896]{2,1,0:T(8,128)(2,1)S(1)}, bf16[8,48,896]{2,1,0:T(8,128)(2,1)S(1)}, u32[]{:S(2)}, u32[]{:S(2)}) collective-permute-start(bf16[8,48,896]{2,1,0:T(8,128)(2,1)S(1)} %all_to_all.21.pieces_ref.own_ref), channel_id=1, source_target_pairs={{0,32},{32,0},{1,33},{33,1},{2,34},{34,2},{3,35},{35,3},{4,36},{36... | collective-permute-start | bytes 2064392 | tf_op jit(solution)/shard_map/ppermute | solution.py:20
  115.7 0.6 shard_map.86.mine_ref
  116.2 1.2 collective-permute-done.2.pieces_ref.other_ref
  117.4 1.5 %shard_map.87 = bf16[768,512]{1,0:T(8,128)(2,1)} custom-call(s32[1]{0:T(128)} %bitcast.core_ref, bf16[384,512]{1,0:T(8,128)(2,1)S(1)} %shard_map.86.mine_ref, bf16[8,48,896]{2,1,0:T(8,128)(2,1)S(1)} %collective-permute-done.2.pieces_ref.other_ref, bf16[896,512]{1,0:T(8,128)(2,1)S(1)} %pad_maximum_fusion.own_ref.weight_ref), custom_call_target="tpu_custom_call" | custom-call | flops 352321536 | bytes 2785280 | tf_op jit(solution)/shard_map/pallas_call | solution.py:32
  118.9 3.9 %all-to-all-start.3 = ((bf16[32,24,512]{2,1,0:T(8,128)(2,1)}), bf16[32,24,512]{2,1,0:T(8,128)(2,1)S(1)}, u32[]{:S(2)}, u32[]{:S(2)}) async-start(bf16[32,24,512]{2,1,0:T(8,128)(2,1)} %bitcast.16), calls=%async_computation.3 | async-start | bytes 1572864 | tf_op jit(solution)/shard_map/all_to_all | solution.py:225
  122.9 2.4 %collective-permute-start.3 = (bf16[4,96,1024]{2,1,0:T(8,128)(2,1)S(1)}, bf16[4,96,1024]{2,1,0:T(8,128)(2,1)S(1)}, u32[]{:S(2)}, u32[]{:S(2)}) collective-permute-start(bf16[4,96,1024]{2,1,0:T(8,128)(2,1)S(1)} %dynamic-slice_bitcast_fusion), channel_id=1, source_target_pairs={{0,32},{32,0},{1,33},{33,1},{2,34},{34,2},{3,35},{35,3},{4,36},{36... | collective-permute-start | bytes 2359304 | tf_op jit(solution)/shard_map/ppermute | solution.py:20
  125.3 16.8 %all_gather.7 = bf16[768,448]{1,0:T(8,128)(2,1)S(1)} all-gather(bf16[48,448]{1,0:T(8,128)(2,1)S(1)} %get-tuple-element.19), channel_id=1, replica_groups=mesh['y'=8,'c'=2,'h'=2,'l'=4,'x'=4] {'y','c'}, dimensions={0}, use_global_device_ids=true | all-gather | bytes 731136 | tf_op jit(solution)/shard_map/all_gather | solution.py:246
  142.2 2.4 %shard_map.89 = (bf16[448,512]{1,0:T(8,128)(2,1)}, bf16[448,512]{1,0:T(8,128)(2,1)}, bf16[448,512]{1,0:T(8,128)(2,1)}) custom-call(s32[1]{0:T(128)} %bitcast.core_ref, bf16[8,48,896]{2,1,0:T(8,128)(2,1)S(1)} %all_to_all.21.pieces_ref.own_ref, bf16[8,48,896]{2,1,0:T(8,128)(2,1)S(1)} %copy-done.1, bf16[8,2,48,448]{3,2,1,0:T(8,128)(2,1)S(1)} %bitcast.15, ...), custom_call_target="tpu_custom_call" | custom-call | flops 1056964608 | bytes 5013504 | tf_op jit(solution)/shard_map/pallas_call | solution.py:32
  144.6 1.1 all-to-all-done.3.parts_ref
  145.7 0.7 shard_map.88
  (16 shorter events, 0.1 us)
Async XLA Ops:
  29.5 4.2 %copy-start.2 = (bf16[512,448]{0,1:T(8,128)(2,1)S(1)}, bf16[512,448]{0,1:T(8,128)(2,1)}, u32[]{:S(2)}) copy-start(bf16[512,448]{0,1:T(8,128)(2,1)} %param.7) | copy-start | bytes 1376260
  29.5 4.2 %copy-start.3 = (bf16[512,448]{0,1:T(8,128)(2,1)S(1)}, bf16[512,448]{0,1:T(8,128)(2,1)}, u32[]{:S(2)}) copy-start(bf16[512,448]{0,1:T(8,128)(2,1)} %param.6) | copy-start | bytes 1376260
  29.5 24.5 %all-to-all-start = ((bf16[4,2,96,1024]{3,2,1,0:T(8,128)(2,1)}), bf16[4,2,96,1024]{3,2,1,0:T(8,128)(2,1)S(1)}, u32[]{:S(2)}, u32[]{:S(2)}) async-start(bf16[4,2,96,1024]{3,2,1,0:T(8,128)(2,1)} %broadcast_in_dim.8), calls=%async_computation | async-start | bytes 3145728 | tf_op jit(solution)/shard_map/all_to_all | solution.py:177
  33.6 2.6 %copy-start.4 = (bf16[448,512]{1,0:T(8,128)(2,1)S(1)}, bf16[448,512]{1,0:T(8,128)(2,1)}, u32[]{:S(2)}) copy-start(bf16[448,512]{1,0:T(8,128)(2,1)} %own_down_hbm) | copy-start | bytes 1376260
  33.7 7.0 %collective-permute-start = (bf16[896,512]{1,0:T(8,128)(2,1)S(1)}, bf16[896,512]{1,0:T(8,128)(2,1)S(1)}, u32[]{:S(2)}, u32[]{:S(2)}) collective-permute-start(bf16[896,512]{1,0:T(8,128)(2,1)S(1)} %pad_maximum_fusion.own_ref.weight_ref), channel_id=1, source_target_pairs={{0,32},{32,0},{1,33},{33,1},{2,34},{34,2},{3,35},{35,3},{4,36},{36... | collective-permute-start | bytes 2752520 | tf_op jit(solution)/shard_map/ppermute | solution.py:20
  36.2 3.7 %collective-permute-start.1 = (bf16[448,512]{1,0:T(8,128)(2,1)S(1)}, bf16[448,512]{1,0:T(8,128)(2,1)S(1)}, u32[]{:S(2)}, u32[]{:S(2)}) collective-permute-start(bf16[448,512]{1,0:T(8,128)(2,1)S(1)} %copy-done.4), channel_id=1, source_target_pairs={{0,32},{32,0},{1,33},{33,1},{2,34},{34,2},{3,35},{35,3},{4,36},{36... | collective-permute-start | bytes 1376264 | tf_op jit(solution)/shard_map/ppermute | solution.py:20
  39.9 0.8 copy-start.5
  109.7 7.7 %collective-permute-start.2 = (bf16[8,48,896]{2,1,0:T(8,128)(2,1)S(1)}, bf16[8,48,896]{2,1,0:T(8,128)(2,1)S(1)}, u32[]{:S(2)}, u32[]{:S(2)}) collective-permute-start(bf16[8,48,896]{2,1,0:T(8,128)(2,1)S(1)} %all_to_all.21.pieces_ref.own_ref), channel_id=1, source_target_pairs={{0,32},{32,0},{1,33},{33,1},{2,34},{34,2},{3,35},{35,3},{4,36},{36... | collective-permute-start | bytes 2064392 | tf_op jit(solution)/shard_map/ppermute | solution.py:20
  117.4 1.5 %copy-start = (bf16[8,48,896]{2,1,0:T(8,128)(2,1)}, bf16[8,48,896]{2,1,0:T(8,128)(2,1)S(1)}, u32[]{:S(2)}) copy-start(bf16[8,48,896]{2,1,0:T(8,128)(2,1)S(1)} %collective-permute-done.2.pieces_ref.other_ref) | copy-start | bytes 2064388
  118.9 26.8 %all-to-all-start.3 = ((bf16[32,24,512]{2,1,0:T(8,128)(2,1)}), bf16[32,24,512]{2,1,0:T(8,128)(2,1)S(1)}, u32[]{:S(2)}, u32[]{:S(2)}) async-start(bf16[32,24,512]{2,1,0:T(8,128)(2,1)} %bitcast.16), calls=%async_computation.3 | async-start | bytes 1572864 | tf_op jit(solution)/shard_map/all_to_all | solution.py:225
  122.8 19.3 %copy-start.1 = (bf16[8,48,896]{2,1,0:T(8,128)(2,1)S(1)}, bf16[8,48,896]{2,1,0:T(8,128)(2,1)}, u32[]{:S(2)}) copy-start(bf16[8,48,896]{2,1,0:T(8,128)(2,1)} %copy-done) | copy-start | bytes 2064388
  122.9 19.3 %collective-permute-start.3 = (bf16[4,96,1024]{2,1,0:T(8,128)(2,1)S(1)}, bf16[4,96,1024]{2,1,0:T(8,128)(2,1)S(1)}, u32[]{:S(2)}, u32[]{:S(2)}) collective-permute-start(bf16[4,96,1024]{2,1,0:T(8,128)(2,1)S(1)} %dynamic-slice_bitcast_fusion), channel_id=1, source_target_pairs={{0,32},{32,0},{1,33},{33,1},{2,34},{34,2},{3,35},{35,3},{4,36},{36... | collective-permute-start | bytes 2359304 | tf_op jit(solution)/shard_map/ppermute | solution.py:20

commit v8 on v7

--- a/solution.py
+++ b/solution.py
@@ -1,3 +1,5 @@
+import functools
+
 import jax
 import jax.numpy as jnp
 from jax import lax
@@ -35,7 +37,7 @@
         in_specs=[pl.BlockSpec(memory_space=space) for space in spaces],
         out_specs=jax.tree.map(lambda _: pl.BlockSpec(memory_space=pltpu.VMEM), out_shape),
         scratch_shapes=scratch,
-        compiler_params=pltpu.CompilerParams(vmem_limit_bytes=16 * 1024 * 1024),
+        compiler_params=pltpu.CompilerParams(vmem_limit_bytes=12 * 1024 * 1024),
         cost_estimate=pl.CostEstimate(flops=flops, bytes_accessed=moved, transcendentals=0),
     )(
         core.reshape(1).astype(jnp.int32),
@@ -104,19 +106,25 @@
     hidden_ref[...] = (activated * up_sum).astype(BF16)
 
 
-def share_kernel(core_ref, pieces_ref, weight_ref, out_ref):
-    packed = pieces_ref.shape[2]
-    pieces = pieces_ref[...].reshape(out_ref.shape[0], packed)
-    out_ref[...] = dot(pieces, weight_ref[...], 1, 0).astype(BF16)
-
-
-def shares_kernel(core_ref, mine_ref, pieces_ref, weight_ref, out_ref):
-    half = mine_ref.shape[0]
-    packed = pieces_ref.shape[2]
-    pieces = pieces_ref[...].reshape(half, packed)
-    theirs = dot(pieces, weight_ref[...], 1, 0).astype(BF16)
-    out_ref[pl.ds(pl.multiple_of(core_ref[0] * half, half), half), :] = mine_ref[...]
-    out_ref[pl.ds(pl.multiple_of((1 - core_ref[0]) * half, half), half), :] = theirs
+def share_kernel(flip, core_ref, pieces_ref, weight_ref, *refs):
+    out_hbm, share_ref, semaphores = refs[-3:]
+    half = share_ref.shape[0]
+    part = half // 2
+    side = 1 - core_ref[0] if flip else core_ref[0]
+    pieces = pieces_ref[...].reshape(half, weight_ref.shape[0])
+    copies = []
+    for k in range(2):
+        at = pl.ds(k * part, part)
+        share_ref[at, :] = dot(pieces[k * part : (k + 1) * part], weight_ref[...], 1, 0).astype(BF16)
+        start = pl.multiple_of(side * half + k * part, part)
+        copies.append(
+            pltpu.make_async_copy(
+                share_ref.at[at], out_hbm.at[pl.ds(start, part)], semaphores.at[k]
+            )
+        )
+        copies[-1].start()
+    for copy in copies:
+        copy.wait()
 
 
 def weights_kernel(
@@ -201,27 +209,26 @@
         pieces = lax.all_to_all(pieces, "y", 0, 0)
 
         other_pieces = sibling(pieces)
-        flops = 4 * half * width * columns
-        moved = 4 * half * columns + 2 * half * width + 4 * columns * width
-        mine = local(
-            share_kernel,
-            jax.ShapeDtypeStruct((half, width), BF16),
-            flops,
-            moved,
-            core,
-            pieces,
-            own_gate_up,
-        )
-        shares = local(
-            shares_kernel,
-            pltpu.HBM((2 * half, width), BF16),
-            flops,
-            moved + 4 * half * width,
-            core,
-            mine,
-            other_pieces,
-            own_gate_up,
-        )
+
+        def share(flip, tokens, *written):
+            return pl.pallas_call(
+                functools.partial(share_kernel, flip),
+                out_shape=pltpu.HBM((2 * half, width), BF16),
+                in_specs=[pl.BlockSpec(memory_space=pltpu.SMEM)]
+                + [pl.BlockSpec(memory_space=pltpu.VMEM)] * 2
+                + [pl.BlockSpec(memory_space=pltpu.HBM)] * len(written),
+                out_specs=pl.BlockSpec(memory_space=pltpu.HBM),
+                input_output_aliases={3: 0} if written else {},
+                scratch_shapes=[pltpu.VMEM((half, width), BF16), pltpu.SemaphoreType.DMA((2,))],
+                compiler_params=pltpu.CompilerParams(vmem_limit_bytes=12 * 1024 * 1024),
+                cost_estimate=pl.CostEstimate(
+                    flops=4 * half * width * columns,
+                    bytes_accessed=4 * half * columns + 2 * half * width + 4 * columns * width,
+                    transcendentals=0,
+                ),
+            )(core.reshape(1).astype(jnp.int32), tokens, own_gate_up, *written)
+
+        shares = share(True, other_pieces, share(False, pieces))
         parts = lax.all_to_all(
             shares.reshape(nz * nx, rows, width), ("h", "x", "l"), 0, 0
         )

time: 147 us -> 147 us (level)
    pallas_call x0 -> x2, Pallas kernels: none -> 2.56 us  [share(): pl.pallas_call(functools.partial(share_kernel, flip), out_shape=pltpu.HBM...]
    pallas_call x6 -> x4, Pallas kernels: 7.28 us -> 5.23 us  [local(): pl.pallas_call(kernel, out_shape=out_shape, in_specs=[pl.BlockSpec(memory...]
  transfers between devices with their start and end apart: 6 -> 6, of which waited for: 4 -> 4; matrix products, arithmetic and copies ran while one was open for 0% -> 0% of each run, Pallas kernels for 2% -> 3%
where the time goes in v8:
time: 147 us; the launch traced here: 146 us
  blocking collectives  97 us (66%)
  starting transfers between devices  20.9 us (14%)
  waiting for transfers between devices  16.6 us (11%)
  Pallas kernels  7.79 us (5%)
  local copies, waits for them, and re-layouts  2.26 us (2%)
    all_to_all x1, blocking collectives, on_device(): sums = lax.all_to_all(sums, 'y', 0, 0)  32.8 us
    all_gather x1, blocking collectives, on_device(): along_z = lax.all_gather(both, ('h', 'l', 'c'), axis=0, tiled=True)  26.6 us
    all_to_all x1, blocking collectives, on_device(): pieces = lax.all_to_all(pieces, 'y', 0, 0)  20.8 us
    all_gather x1, blocking collectives, on_device(): lax.all_gather(after(hidden, shares), ('y', 'c'), axis=0, tiled=True)  16.8 us
    all_to_all x1, waiting for transfers between devices, on_device(): lax.all_to_all(jnp.broadcast_to(kept[None], (nx, *kept.shape)), 'x', 0, 0)  13.3 us
    ppermute x4, starting transfers between devices, sibling(): return lax.ppermute(value, 'c', SWAP)  12.8 us
    pallas_call x4, Pallas kernels, local(): pl.pallas_call(kernel, out_shape=out_shape, in_specs=[pl.BlockSpec(memory...  5.23 us
    all_to_all x1, starting transfers between devices, on_device(): lax.all_to_all(jnp.broadcast_to(kept[None], (nx, *kept.shape)), 'x', 0, 0)  4.14 us
  transfers between devices with their start and end apart: 6, of which 4 were waited for; matrix products, arithmetic and copies ran while one was open for 0% of the time, Pallas kernels for 3%

profile of v8, /device:TPU:1, one launch (start us, length us, event | category | flops | bytes accessed | tf_op | source)
XLA Modules:
  0.0 146.2 jit_solution(14262262680813284387)
XLA Ops:
  0.6 0.8 pad_maximum_fusion.1
  1.4 26.6 %all_gather.6 = bf16[384,1024]{1,0:T(8,128)(2,1)S(1)} all-gather(bf16[24,1024]{1,0:T(8,128)(2,1)S(1)} %pad_maximum_fusion.1), channel_id=1, replica_groups=mesh['y'=8,'c'=2,'h'=2,'l'=4,'x'=4] {'h','l','c'}, dimensions={0}, use_global_device_ids=true | all-gather | bytes 835584 | tf_op jit(solution)/shard_map/all_gather | solution.py:177
  28.1 1.4 broadcast_in_dim.8
  29.5 4.1 %all-to-all-start = ((bf16[4,2,96,1024]{3,2,1,0:T(8,128)(2,1)}), bf16[4,2,96,1024]{3,2,1,0:T(8,128)(2,1)S(1)}, u32[]{:S(2)}, u32[]{:S(2)}) async-start(bf16[4,2,96,1024]{3,2,1,0:T(8,128)(2,1)} %broadcast_in_dim.8), calls=%async_computation | async-start | bytes 3145728 | tf_op jit(solution)/shard_map/all_to_all | solution.py:185
  33.6 0.1 pad_maximum_fusion.own_ref.weight_ref
  33.7 2.5 %collective-permute-start = (bf16[896,512]{1,0:T(8,128)(2,1)S(1)}, bf16[896,512]{1,0:T(8,128)(2,1)S(1)}, u32[]{:S(2)}, u32[]{:S(2)}) collective-permute-start(bf16[896,512]{1,0:T(8,128)(2,1)S(1)} %pad_maximum_fusion.own_ref.weight_ref), channel_id=1, source_target_pairs={{0,32},{32,0},{1,33},{33,1},{2,34},{34,2},{3,35},{35,3},{4,36},{36... | collective-permute-start | bytes 2752520 | tf_op jit(solution)/shard_map/ppermute | solution.py:22
  36.2 2.0 %collective-permute-start.1 = (bf16[448,512]{1,0:T(8,128)(2,1)S(1)}, bf16[448,512]{1,0:T(8,128)(2,1)S(1)}, u32[]{:S(2)}, u32[]{:S(2)}) collective-permute-start(bf16[448,512]{1,0:T(8,128)(2,1)S(1)} %copy-done.4), channel_id=1, source_target_pairs={{0,32},{32,0},{1,33},{33,1},{2,34},{34,2},{3,35},{35,3},{4,36},{36... | collective-permute-start | bytes 1376264 | tf_op jit(solution)/shard_map/ppermute | solution.py:22
  38.2 1.7 %collective-permute-done.1.sib_down_hbm = bf16[448,512]{1,0:T(8,128)(2,1)S(1)} collective-permute-done((bf16[448,512]{1,0:T(8,128)(2,1)S(1)}, bf16[448,512]{1,0:T(8,128)(2,1)S(1)}, u32[]{:S(2)}, u32[]{:S(2)}) %collective-permute-start.1) | collective-permute-done | bytes 458784 | tf_op jit(solution)/shard_map/ppermute | solution.py:22
  39.9 0.8 copy-done.5
  40.7 13.3 %all-to-all-done.block_ref.own_block_ref = bf16[4,2,96,1024]{3,2,1,0:T(8,128)(2,1)S(1)} async-done(((bf16[4,2,96,1024]{3,2,1,0:T(8,128)(2,1)}), bf16[4,2,96,1024]{3,2,1,0:T(8,128)(2,1)S(1)}, u32[]{:S(2)}, u32[]{:S(2)}) %all-to-all-start) | async-done | bytes 1572896 | tf_op jit(solution)/shard_map/all_to_all | solution.py:185
  54.0 1.8 %shard_map.84 = bf16[8,24,2688]{2,1,0:T(8,128)(2,1)S(1)} custom-call(s32[1]{0:T(128)} %bitcast.core_ref, bf16[4,2,96,1024]{3,2,1,0:T(8,128)(2,1)S(1)} %all-to-all-done.block_ref.own_block_ref, bf16[896,512]{1,0:T(8,128)(2,1)S(1)} %pad_maximum_fusion.own_ref.weight_ref, bf16[896,512]{1,0:T(8,128)(2,1)S(1)} %collective-permute-done.sib_ref, ...), custom_call_target="tpu_custom_call" | custom-call | flops 1056964608 | bytes 5357568 | tf_op jit(solution)/shard_map/pallas_call | solution.py:34
  55.9 32.8 %all_to_all.20.parts_ref = bf16[8,24,2688]{2,1,0:T(8,128)(2,1)S(1)} all-to-all(bf16[8,24,2688]{2,1,0:T(8,128)(2,1)S(1)} %shard_map.84), channel_id=1, replica_groups=mesh['y'=8,'c'=2,'h'=2,'l'=4,'x'=4] {'y'}, dimensions={0} | all-to-all | bytes 2064384 | tf_op jit(solution)/shard_map/all_to_all | solution.py:197
  88.6 0.3 shard_map.85
  88.9 20.8 %all_to_all.21.pieces_ref.own_ref = bf16[8,48,896]{2,1,0:T(8,128)(2,1)S(1)} all-to-all(bf16[8,48,896]{2,1,0:T(8,128)(2,1)S(1)} %get-tuple-element.17), channel_id=1, replica_groups=mesh['y'=8,'c'=2,'h'=2,'l'=4,'x'=4] {'y'}, dimensions={0} | all-to-all | bytes 1376256 | tf_op jit(solution)/shard_map/all_to_all | solution.py:209
  109.7 6.0 %collective-permute-start.2 = (bf16[8,48,896]{2,1,0:T(8,128)(2,1)S(1)}, bf16[8,48,896]{2,1,0:T(8,128)(2,1)S(1)}, u32[]{:S(2)}, u32[]{:S(2)}) collective-permute-start(bf16[8,48,896]{2,1,0:T(8,128)(2,1)S(1)} %all_to_all.21.pieces_ref.own_ref), channel_id=1, source_target_pairs={{0,32},{32,0},{1,33},{33,1},{2,34},{34,2},{3,35},{35,3},{4,36},{36... | collective-permute-start | bytes 2064392 | tf_op jit(solution)/shard_map/ppermute | solution.py:22
  115.7 1.3 shard_map.86.refs_0_
  117.0 0.5 collective-permute-done.2.pieces_ref.other_ref
  117.4 1.3 shard_map.87
  118.7 3.9 %all-to-all-start.3 = ((bf16[32,24,512]{2,1,0:T(8,128)(2,1)}), bf16[32,24,512]{2,1,0:T(8,128)(2,1)S(1)}, u32[]{:S(2)}, u32[]{:S(2)}) async-start(bf16[32,24,512]{2,1,0:T(8,128)(2,1)} %bitcast.16), calls=%async_computation.3 | async-start | bytes 1572864 | tf_op jit(solution)/shard_map/all_to_all | solution.py:232
  122.7 2.4 %collective-permute-start.3 = (bf16[4,96,1024]{2,1,0:T(8,128)(2,1)S(1)}, bf16[4,96,1024]{2,1,0:T(8,128)(2,1)S(1)}, u32[]{:S(2)}, u32[]{:S(2)}) collective-permute-start(bf16[4,96,1024]{2,1,0:T(8,128)(2,1)S(1)} %dynamic-slice_bitcast_fusion), channel_id=1, source_target_pairs={{0,32},{32,0},{1,33},{33,1},{2,34},{34,2},{3,35},{35,3},{4,36},{36... | collective-permute-start | bytes 2359304 | tf_op jit(solution)/shard_map/ppermute | solution.py:22
  125.2 16.8 %all_gather.7 = bf16[768,448]{1,0:T(8,128)(2,1)S(1)} all-gather(bf16[48,448]{1,0:T(8,128)(2,1)S(1)} %get-tuple-element.19), channel_id=1, replica_groups=mesh['y'=8,'c'=2,'h'=2,'l'=4,'x'=4] {'y','c'}, dimensions={0}, use_global_device_ids=true | all-gather | bytes 731136 | tf_op jit(solution)/shard_map/all_gather | solution.py:253
  142.0 2.4 %shard_map.89 = (bf16[448,512]{1,0:T(8,128)(2,1)}, bf16[448,512]{1,0:T(8,128)(2,1)}, bf16[448,512]{1,0:T(8,128)(2,1)}) custom-call(s32[1]{0:T(128)} %bitcast.core_ref, bf16[8,48,896]{2,1,0:T(8,128)(2,1)S(1)} %all_to_all.21.pieces_ref.own_ref, bf16[8,48,896]{2,1,0:T(8,128)(2,1)S(1)} %copy-done.1, bf16[8,2,48,448]{3,2,1,0:T(8,128)(2,1)S(1)} %bitcast.15, ...), custom_call_target="tpu_custom_call" | custom-call | flops 1056964608 | bytes 5013504 | tf_op jit(solution)/shard_map/pallas_call | solution.py:34
  144.4 1.1 all-to-all-done.3.parts_ref
  145.5 0.7 shard_map.88
  (16 shorter events, 0.1 us)
Async XLA Ops:
  29.5 4.2 %copy-start.2 = (bf16[512,448]{0,1:T(8,128)(2,1)S(1)}, bf16[512,448]{0,1:T(8,128)(2,1)}, u32[]{:S(2)}) copy-start(bf16[512,448]{0,1:T(8,128)(2,1)} %param.7) | copy-start | bytes 1376260
  29.5 4.2 %copy-start.3 = (bf16[512,448]{0,1:T(8,128)(2,1)S(1)}, bf16[512,448]{0,1:T(8,128)(2,1)}, u32[]{:S(2)}) copy-start(bf16[512,448]{0,1:T(8,128)(2,1)} %param.6) | copy-start | bytes 1376260
  29.5 24.5 %all-to-all-start = ((bf16[4,2,96,1024]{3,2,1,0:T(8,128)(2,1)}), bf16[4,2,96,1024]{3,2,1,0:T(8,128)(2,1)S(1)}, u32[]{:S(2)}, u32[]{:S(2)}) async-start(bf16[4,2,96,1024]{3,2,1,0:T(8,128)(2,1)} %broadcast_in_dim.8), calls=%async_computation | async-start | bytes 3145728 | tf_op jit(solution)/shard_map/all_to_all | solution.py:185
  33.6 2.6 %copy-start.4 = (bf16[448,512]{1,0:T(8,128)(2,1)S(1)}, bf16[448,512]{1,0:T(8,128)(2,1)}, u32[]{:S(2)}) copy-start(bf16[448,512]{1,0:T(8,128)(2,1)} %own_down_hbm) | copy-start | bytes 1376260
  33.7 7.0 %collective-permute-start = (bf16[896,512]{1,0:T(8,128)(2,1)S(1)}, bf16[896,512]{1,0:T(8,128)(2,1)S(1)}, u32[]{:S(2)}, u32[]{:S(2)}) collective-permute-start(bf16[896,512]{1,0:T(8,128)(2,1)S(1)} %pad_maximum_fusion.own_ref.weight_ref), channel_id=1, source_target_pairs={{0,32},{32,0},{1,33},{33,1},{2,34},{34,2},{3,35},{35,3},{4,36},{36... | collective-permute-start | bytes 2752520 | tf_op jit(solution)/shard_map/ppermute | solution.py:22
  36.2 3.7 %collective-permute-start.1 = (bf16[448,512]{1,0:T(8,128)(2,1)S(1)}, bf16[448,512]{1,0:T(8,128)(2,1)S(1)}, u32[]{:S(2)}, u32[]{:S(2)}) collective-permute-start(bf16[448,512]{1,0:T(8,128)(2,1)S(1)} %copy-done.4), channel_id=1, source_target_pairs={{0,32},{32,0},{1,33},{33,1},{2,34},{34,2},{3,35},{35,3},{4,36},{36... | collective-permute-start | bytes 1376264 | tf_op jit(solution)/shard_map/ppermute | solution.py:22
  39.9 0.8 copy-start.5
  109.7 7.7 %collective-permute-start.2 = (bf16[8,48,896]{2,1,0:T(8,128)(2,1)S(1)}, bf16[8,48,896]{2,1,0:T(8,128)(2,1)S(1)}, u32[]{:S(2)}, u32[]{:S(2)}) collective-permute-start(bf16[8,48,896]{2,1,0:T(8,128)(2,1)S(1)} %all_to_all.21.pieces_ref.own_ref), channel_id=1, source_target_pairs={{0,32},{32,0},{1,33},{33,1},{2,34},{34,2},{3,35},{35,3},{4,36},{36... | collective-permute-start | bytes 2064392 | tf_op jit(solution)/shard_map/ppermute | solution.py:22
  117.4 1.3 copy-start
  118.7 26.8 %all-to-all-start.3 = ((bf16[32,24,512]{2,1,0:T(8,128)(2,1)}), bf16[32,24,512]{2,1,0:T(8,128)(2,1)S(1)}, u32[]{:S(2)}, u32[]{:S(2)}) async-start(bf16[32,24,512]{2,1,0:T(8,128)(2,1)} %bitcast.16), calls=%async_computation.3 | async-start | bytes 1572864 | tf_op jit(solution)/shard_map/all_to_all | solution.py:232
  122.7 19.3 %copy-start.1 = (bf16[8,48,896]{2,1,0:T(8,128)(2,1)S(1)}, bf16[8,48,896]{2,1,0:T(8,128)(2,1)}, u32[]{:S(2)}) copy-start(bf16[8,48,896]{2,1,0:T(8,128)(2,1)} %copy-done) | copy-start | bytes 2064388
  122.7 19.3 %collective-permute-start.3 = (bf16[4,96,1024]{2,1,0:T(8,128)(2,1)S(1)}, bf16[4,96,1024]{2,1,0:T(8,128)(2,1)S(1)}, u32[]{:S(2)}, u32[]{:S(2)}) collective-permute-start(bf16[4,96,1024]{2,1,0:T(8,128)(2,1)S(1)} %dynamic-slice_bitcast_fusion), channel_id=1, source_target_pairs={{0,32},{32,0},{1,33},{33,1},{2,34},{34,2},{3,35},{35,3},{4,36},{36... | collective-permute-start | bytes 2359304 | tf_op jit(solution)/shard_map/ppermute | solution.py:22

commit v9 on v7

--- a/solution.py
+++ b/solution.py
@@ -62,9 +62,9 @@
     sib_copy.start()
     core = core_ref[0]
     packed, width = own_ref.shape
-    half = block_ref.shape[0] * block_ref.shape[2]
-    own = block_ref[:, core].reshape(half, 2 * width)
-    sib = block_ref[:, 1 - core].reshape(half, 2 * width)
+    half = block_ref.shape[0] * block_ref.shape[3]
+    own, own_co = (block_ref[:, core, k].reshape(half, width) for k in range(2))
+    sib, sib_co = (block_ref[:, 1 - core, k].reshape(half, width) for k in range(2))
     ny, rows, _ = out_ref.shape
 
     def store(sums, start):
@@ -73,11 +73,11 @@
         out_ref[:, :, start : start + count] = pairs[:, :rows].astype(BF16)
         out_ref[:, :, start + count : start + 2 * count] = pairs[:, rows:].astype(BF16)
 
-    store(dot(own[:, :width], own_ref[...], 1, 1) + dot(sib[:, :width], sib_ref[...], 1, 1), 0)
+    store(dot(own, own_ref[...], 1, 1) + dot(sib, sib_ref[...], 1, 1), 0)
     own_copy.wait()
     sib_copy.wait()
-    back = dot(own[:, width:], own_down_ref[...], 1, 1)
-    store(back + dot(sib[:, width:], sib_down_ref[...], 1, 1), 2 * packed)
+    back = dot(own_co, own_down_ref[...], 1, 1)
+    store(back + dot(sib_co, sib_down_ref[...], 1, 1), 2 * packed)
 
 
 def sigmoid(value):
@@ -137,10 +137,12 @@
     other = other_ref[...].reshape(half, 2 * columns)
     own_hidden = hidden_ref[:, core].reshape(half, columns)
     other_hidden = hidden_ref[:, 1 - core].reshape(half, columns)
-    own_block = own_block_ref[:, core].reshape(half, 2 * width)
-    own_inputs, own_cotangent = own_block[:, :width], own_block[:, width:]
-    other_block = other_block_ref[...].reshape(half, 2 * width)
-    other_inputs, other_cotangent = other_block[:, :width], other_block[:, width:]
+    own_inputs, own_cotangent = (
+        own_block_ref[:, core, k].reshape(half, width) for k in range(2)
+    )
+    other_inputs, other_cotangent = (
+        other_block_ref[:, k].reshape(half, width) for k in range(2)
+    )
     packed = dot(own, own_inputs, 0, 0) + dot(other, other_inputs, 0, 0)
     gate_ref[...] = packed[:columns].astype(BF16)
     up_ref[...] = packed[columns:].astype(BF16)
@@ -165,11 +167,11 @@
         half = part * nx
         share_rows = half // ny
         core = lax.axis_index("c")
-        both = jnp.concatenate([inputs, cotangent], axis=1)
+        both = jnp.concatenate([inputs, cotangent], axis=0)
         along_z = lax.all_gather(both, ("h", "l", "c"), axis=0, tiled=True)
-        along_z = along_z.reshape(nh, nl, nc, rows, 2 * width)
+        along_z = along_z.reshape(nh, nl, nc, 2, rows, width)
         kept = lax.dynamic_index_in_dim(along_z, core, 0, False)
-        kept = kept.swapaxes(0, 1).reshape(nc, part, 2 * width)
+        kept = kept.transpose(1, 2, 0, 3, 4).reshape(nc, 2, part, width)
 
         w_gate, w_up, w_down = (after(w, along_z) for w in (w_gate, w_up, w_down))
         own_gate_up = jnp.concatenate([w_gate.T, w_up.T], axis=0)

time: 147 us -> 147 us (level)
  no operation moved by 1% of the time
where the time goes in v9:
time: 147 us
  blocking collectives  97 us (66%)
  starting transfers between devices  20.9 us (14%)
  waiting for transfers between devices  17.4 us (12%)
  Pallas kernels  7.51 us (5%)
  local copies, waits for them, and re-layouts  2.22 us (2%)
    all_to_all x1, blocking collectives, on_device(): sums = lax.all_to_all(sums, 'y', 0, 0)  32.8 us
    all_gather x1, blocking collectives, on_device(): along_z = lax.all_gather(both, ('h', 'l', 'c'), axis=0, tiled=True)  26.6 us
    all_to_all x1, blocking collectives, on_device(): pieces = lax.all_to_all(pieces, 'y', 0, 0)  20.8 us
    all_gather x1, blocking collectives, on_device(): lax.all_gather(after(hidden, shares), ('y', 'c'), axis=0, tiled=True)  16.8 us
    all_to_all x1, waiting for transfers between devices, on_device(): lax.all_to_all(jnp.broadcast_to(kept[None], (nx, *kept.shape)), 'x', 0, 0)  13.3 us
    ppermute x4, starting transfers between devices, sibling(): return lax.ppermute(value, 'c', SWAP)  12.8 us
    pallas_call x6, Pallas kernels, local(): pl.pallas_call(kernel, out_shape=out_shape, in_specs=[pl.BlockSpec(memory...  7.51 us
    all_to_all x1, starting transfers between devices, on_device(): lax.all_to_all(jnp.broadcast_to(kept[None], (nx, *kept.shape)), 'x', 0, 0)  4.14 us
  transfers between devices with their start and end apart: 6, of which 4 were waited for; matrix products, arithmetic and copies ran while one was open for 0% of the time, Pallas kernels for 2%

profile of v9, /device:TPU:1, one launch (start us, length us, event | category | flops | bytes accessed | tf_op | source)
XLA Modules:
  0.0 146.6 jit_solution(1312764759053103186)
XLA Ops:
  0.6 0.8 pad_maximum_fusion.1
  1.4 26.6 %all_gather.6 = bf16[768,512]{1,0:T(8,128)(2,1)S(1)} all-gather(bf16[48,512]{1,0:T(8,128)(2,1)S(1)} %pad_maximum_fusion.1), channel_id=1, replica_groups=mesh['y'=8,'c'=2,'h'=2,'l'=4,'x'=4] {'h','l','c'}, dimensions={0}, use_global_device_ids=true | all-gather | bytes 835584 | tf_op jit(solution)/shard_map/all_gather | solution.py:171
  28.1 1.3 broadcast_in_dim.8
  29.4 4.1 %all-to-all-start = ((bf16[4,2,2,96,512]{4,3,2,1,0:T(8,128)(2,1)}), bf16[4,2,2,96,512]{4,3,2,1,0:T(8,128)(2,1)S(1)}, u32[]{:S(2)}, u32[]{:S(2)}) async-start(bf16[4,2,2,96,512]{4,3,2,1,0:T(8,128)(2,1)} %broadcast_in_dim.8), calls=%async_computation | async-start | bytes 3145728 | tf_op jit(solution)/shard_map/all_to_all | solution.py:179
  33.6 0.1 pad_maximum_fusion.own_ref.weight_ref
  33.7 2.5 %collective-permute-start = (bf16[896,512]{1,0:T(8,128)(2,1)S(1)}, bf16[896,512]{1,0:T(8,128)(2,1)S(1)}, u32[]{:S(2)}, u32[]{:S(2)}) collective-permute-start(bf16[896,512]{1,0:T(8,128)(2,1)S(1)} %pad_maximum_fusion.own_ref.weight_ref), channel_id=1, source_target_pairs={{0,32},{32,0},{1,33},{33,1},{2,34},{34,2},{3,35},{35,3},{4,36},{36... | collective-permute-start | bytes 2752520 | tf_op jit(solution)/shard_map/ppermute | solution.py:20
  36.1 2.0 %collective-permute-start.1 = (bf16[448,512]{1,0:T(8,128)(2,1)S(1)}, bf16[448,512]{1,0:T(8,128)(2,1)S(1)}, u32[]{:S(2)}, u32[]{:S(2)}) collective-permute-start(bf16[448,512]{1,0:T(8,128)(2,1)S(1)} %copy-done.4), channel_id=1, source_target_pairs={{0,32},{32,0},{1,33},{33,1},{2,34},{34,2},{3,35},{35,3},{4,36},{36... | collective-permute-start | bytes 1376264 | tf_op jit(solution)/shard_map/ppermute | solution.py:20
  38.1 1.7 %collective-permute-done.1.sib_down_hbm = bf16[448,512]{1,0:T(8,128)(2,1)S(1)} collective-permute-done((bf16[448,512]{1,0:T(8,128)(2,1)S(1)}, bf16[448,512]{1,0:T(8,128)(2,1)S(1)}, u32[]{:S(2)}, u32[]{:S(2)}) %collective-permute-start.1) | collective-permute-done | bytes 458784 | tf_op jit(solution)/shard_map/ppermute | solution.py:20
  39.9 0.8 copy-done.5
  40.6 13.3 %all-to-all-done.block_ref.own_block_ref = bf16[4,2,2,96,512]{4,3,2,1,0:T(8,128)(2,1)S(1)} async-done(((bf16[4,2,2,96,512]{4,3,2,1,0:T(8,128)(2,1)}), bf16[4,2,2,96,512]{4,3,2,1,0:T(8,128)(2,1)S(1)}, u32[]{:S(2)}, u32[]{:S(2)}) %all-to-all-start) | async-done | bytes 1572896 | tf_op jit(solution)/shard_map/all_to_all | solution.py:179
  54.0 2.1 %shard_map.84 = bf16[8,24,2688]{2,1,0:T(8,128)(2,1)S(1)} custom-call(s32[1]{0:T(128)} %bitcast.core_ref, bf16[4,2,2,96,512]{4,3,2,1,0:T(8,128)(2,1)S(1)} %all-to-all-done.block_ref.own_block_ref, bf16[896,512]{1,0:T(8,128)(2,1)S(1)} %pad_maximum_fusion.own_ref.weight_ref, bf16[896,512]{1,0:T(8,128)(2,1)S(1)} %collective-permute-done.sib_ref, ...), custom_call_target="tpu_custom_call" | custom-call | flops 1056964608 | bytes 5357568 | tf_op jit(solution)/shard_map/pallas_call | solution.py:32
  56.0 32.8 %all_to_all.20.parts_ref = bf16[8,24,2688]{2,1,0:T(8,128)(2,1)S(1)} all-to-all(bf16[8,24,2688]{2,1,0:T(8,128)(2,1)S(1)} %shard_map.84), channel_id=1, replica_groups=mesh['y'=8,'c'=2,'h'=2,'l'=4,'x'=4] {'y'}, dimensions={0} | all-to-all | bytes 2064384 | tf_op jit(solution)/shard_map/all_to_all | solution.py:191
  88.8 0.3 shard_map.85
  89.1 20.8 %all_to_all.21.pieces_ref.own_ref = bf16[8,48,896]{2,1,0:T(8,128)(2,1)S(1)} all-to-all(bf16[8,48,896]{2,1,0:T(8,128)(2,1)S(1)} %get-tuple-element.17), channel_id=1, replica_groups=mesh['y'=8,'c'=2,'h'=2,'l'=4,'x'=4] {'y'}, dimensions={0} | all-to-all | bytes 1376256 | tf_op jit(solution)/shard_map/all_to_all | solution.py:203
  109.9 6.0 %collective-permute-start.2 = (bf16[8,48,896]{2,1,0:T(8,128)(2,1)S(1)}, bf16[8,48,896]{2,1,0:T(8,128)(2,1)S(1)}, u32[]{:S(2)}, u32[]{:S(2)}) collective-permute-start(bf16[8,48,896]{2,1,0:T(8,128)(2,1)S(1)} %all_to_all.21.pieces_ref.own_ref), channel_id=1, source_target_pairs={{0,32},{32,0},{1,33},{33,1},{2,34},{34,2},{3,35},{35,3},{4,36},{36... | collective-permute-start | bytes 2064392 | tf_op jit(solution)/shard_map/ppermute | solution.py:20
  115.9 0.6 shard_map.86.mine_ref
  116.4 1.2 collective-permute-done.2.pieces_ref.other_ref
  117.6 1.5 %shard_map.87 = bf16[768,512]{1,0:T(8,128)(2,1)} custom-call(s32[1]{0:T(128)} %bitcast.core_ref, bf16[384,512]{1,0:T(8,128)(2,1)S(1)} %shard_map.86.mine_ref, bf16[8,48,896]{2,1,0:T(8,128)(2,1)S(1)} %collective-permute-done.2.pieces_ref.other_ref, bf16[896,512]{1,0:T(8,128)(2,1)S(1)} %pad_maximum_fusion.own_ref.weight_ref), custom_call_target="tpu_custom_call" | custom-call | flops 352321536 | bytes 2785280 | tf_op jit(solution)/shard_map/pallas_call | solution.py:32
  119.1 3.9 %all-to-all-start.3 = ((bf16[32,24,512]{2,1,0:T(8,128)(2,1)}), bf16[32,24,512]{2,1,0:T(8,128)(2,1)S(1)}, u32[]{:S(2)}, u32[]{:S(2)}) async-start(bf16[32,24,512]{2,1,0:T(8,128)(2,1)} %bitcast.16), calls=%async_computation.3 | async-start | bytes 1572864 | tf_op jit(solution)/shard_map/all_to_all | solution.py:227
  123.1 2.4 %collective-permute-start.3 = (bf16[4,2,96,512]{3,2,1,0:T(8,128)(2,1)S(1)}, bf16[4,2,96,512]{3,2,1,0:T(8,128)(2,1)S(1)}, u32[]{:S(2)}, u32[]{:S(2)}) collective-permute-start(bf16[4,2,96,512]{3,2,1,0:T(8,128)(2,1)S(1)} %dynamic-slice_bitcast_fusion), channel_id=1, source_target_pairs={{0,32},{32,0},{1,33},{33,1},{2,34},{34,2},{3,35},{35,3},{4,36},{36... | collective-permute-start | bytes 2359304 | tf_op jit(solution)/shard_map/ppermute | solution.py:20
  125.5 16.8 %all_gather.7 = bf16[768,448]{1,0:T(8,128)(2,1)S(1)} all-gather(bf16[48,448]{1,0:T(8,128)(2,1)S(1)} %get-tuple-element.19), channel_id=1, replica_groups=mesh['y'=8,'c'=2,'h'=2,'l'=4,'x'=4] {'y','c'}, dimensions={0}, use_global_device_ids=true | all-gather | bytes 731136 | tf_op jit(solution)/shard_map/all_gather | solution.py:248
  142.4 2.4 %shard_map.89 = (bf16[448,512]{1,0:T(8,128)(2,1)}, bf16[448,512]{1,0:T(8,128)(2,1)}, bf16[448,512]{1,0:T(8,128)(2,1)}) custom-call(s32[1]{0:T(128)} %bitcast.core_ref, bf16[8,48,896]{2,1,0:T(8,128)(2,1)S(1)} %all_to_all.21.pieces_ref.own_ref, bf16[8,48,896]{2,1,0:T(8,128)(2,1)S(1)} %copy-done.1, bf16[8,2,48,448]{3,2,1,0:T(8,128)(2,1)S(1)} %bitcast.15, ...), custom_call_target="tpu_custom_call" | custom-call | flops 1056964608 | bytes 5013504 | tf_op jit(solution)/shard_map/pallas_call | solution.py:32
  144.8 1.1 all-to-all-done.3.parts_ref
  145.9 0.7 shard_map.88
  (16 shorter events, 0.1 us)
Async XLA Ops:
  29.4 4.2 %copy-start.2 = (bf16[512,448]{0,1:T(8,128)(2,1)S(1)}, bf16[512,448]{0,1:T(8,128)(2,1)}, u32[]{:S(2)}) copy-start(bf16[512,448]{0,1:T(8,128)(2,1)} %param.7) | copy-start | bytes 1376260
  29.4 4.2 %copy-start.3 = (bf16[512,448]{0,1:T(8,128)(2,1)S(1)}, bf16[512,448]{0,1:T(8,128)(2,1)}, u32[]{:S(2)}) copy-start(bf16[512,448]{0,1:T(8,128)(2,1)} %param.6) | copy-start | bytes 1376260
  29.4 24.5 %all-to-all-start = ((bf16[4,2,2,96,512]{4,3,2,1,0:T(8,128)(2,1)}), bf16[4,2,2,96,512]{4,3,2,1,0:T(8,128)(2,1)S(1)}, u32[]{:S(2)}, u32[]{:S(2)}) async-start(bf16[4,2,2,96,512]{4,3,2,1,0:T(8,128)(2,1)} %broadcast_in_dim.8), calls=%async_computation | async-start | bytes 3145728 | tf_op jit(solution)/shard_map/all_to_all | solution.py:179
  33.6 2.6 %copy-start.4 = (bf16[448,512]{1,0:T(8,128)(2,1)S(1)}, bf16[448,512]{1,0:T(8,128)(2,1)}, u32[]{:S(2)}) copy-start(bf16[448,512]{1,0:T(8,128)(2,1)} %own_down_hbm) | copy-start | bytes 1376260
  33.7 7.0 %collective-permute-start = (bf16[896,512]{1,0:T(8,128)(2,1)S(1)}, bf16[896,512]{1,0:T(8,128)(2,1)S(1)}, u32[]{:S(2)}, u32[]{:S(2)}) collective-permute-start(bf16[896,512]{1,0:T(8,128)(2,1)S(1)} %pad_maximum_fusion.own_ref.weight_ref), channel_id=1, source_target_pairs={{0,32},{32,0},{1,33},{33,1},{2,34},{34,2},{3,35},{35,3},{4,36},{36... | collective-permute-start | bytes 2752520 | tf_op jit(solution)/shard_map/ppermute | solution.py:20
  36.1 3.7 %collective-permute-start.1 = (bf16[448,512]{1,0:T(8,128)(2,1)S(1)}, bf16[448,512]{1,0:T(8,128)(2,1)S(1)}, u32[]{:S(2)}, u32[]{:S(2)}) collective-permute-start(bf16[448,512]{1,0:T(8,128)(2,1)S(1)} %copy-done.4), channel_id=1, source_target_pairs={{0,32},{32,0},{1,33},{33,1},{2,34},{34,2},{3,35},{35,3},{4,36},{36... | collective-permute-start | bytes 1376264 | tf_op jit(solution)/shard_map/ppermute | solution.py:20
  39.9 0.8 copy-start.5
  109.9 7.7 %collective-permute-start.2 = (bf16[8,48,896]{2,1,0:T(8,128)(2,1)S(1)}, bf16[8,48,896]{2,1,0:T(8,128)(2,1)S(1)}, u32[]{:S(2)}, u32[]{:S(2)}) collective-permute-start(bf16[8,48,896]{2,1,0:T(8,128)(2,1)S(1)} %all_to_all.21.pieces_ref.own_ref), channel_id=1, source_target_pairs={{0,32},{32,0},{1,33},{33,1},{2,34},{34,2},{3,35},{35,3},{4,36},{36... | collective-permute-start | bytes 2064392 | tf_op jit(solution)/shard_map/ppermute | solution.py:20
  117.6 1.5 %copy-start = (bf16[8,48,896]{2,1,0:T(8,128)(2,1)}, bf16[8,48,896]{2,1,0:T(8,128)(2,1)S(1)}, u32[]{:S(2)}) copy-start(bf16[8,48,896]{2,1,0:T(8,128)(2,1)S(1)} %collective-permute-done.2.pieces_ref.other_ref) | copy-start | bytes 2064388
  119.1 26.8 %all-to-all-start.3 = ((bf16[32,24,512]{2,1,0:T(8,128)(2,1)}), bf16[32,24,512]{2,1,0:T(8,128)(2,1)S(1)}, u32[]{:S(2)}, u32[]{:S(2)}) async-start(bf16[32,24,512]{2,1,0:T(8,128)(2,1)} %bitcast.16), calls=%async_computation.3 | async-start | bytes 1572864 | tf_op jit(solution)/shard_map/all_to_all | solution.py:227
  123.0 19.3 %copy-start.1 = (bf16[8,48,896]{2,1,0:T(8,128)(2,1)S(1)}, bf16[8,48,896]{2,1,0:T(8,128)(2,1)}, u32[]{:S(2)}) copy-start(bf16[8,48,896]{2,1,0:T(8,128)(2,1)} %copy-done) | copy-start | bytes 2064388
  123.1 19.3 %collective-permute-start.3 = (bf16[4,2,96,512]{3,2,1,0:T(8,128)(2,1)S(1)}, bf16[4,2,96,512]{3,2,1,0:T(8,128)(2,1)S(1)}, u32[]{:S(2)}, u32[]{:S(2)}) collective-permute-start(bf16[4,2,96,512]{3,2,1,0:T(8,128)(2,1)S(1)} %dynamic-slice_bitcast_fusion), channel_id=1, source_target_pairs={{0,32},{32,0},{1,33},{33,1},{2,34},{34,2},{3,35},{35,3},{4,36},{36... | collective-permute-start | bytes 2359304 | tf_op jit(solution)/shard_map/ppermute | solution.py:20
